TPU v7x, 256 devices: a whole 4x4x8 slice. The times are simulated.
256 devices in a mesh: span: 8 (over z), chord: 32 (over x, y, core).
Axes of the slice: x: 4, y: 4, z: 8, core: 2. Of those that a mesh axis runs over, the one named last changes fastest.
Arguments:
- skin_now: float32 [3, 6, 1024, 4096], P(None, None, 'span', 'chord'), may hold values from -6 to 6
- skin_prev: float32 [3, 6, 1024, 4096], P(None, None, 'span', 'chord'), may hold values from -6 to 6
- skin_mat: int32 [6, 1024, 4096], P(None, 'span', 'chord'), may hold values from 0 to 7
- stringer_now: float32 [64, 3, 6, 96, 1024], P('chord', None, None, None, 'span'), as said below
- stringer_prev: float32 [64, 3, 6, 96, 1024], P('chord', None, None, None, 'span'), as said below
- stringer_mat: int32 [64, 6, 96, 1024], P('chord', None, None, 'span'), may hold values from 0 to 7
- owner_slot: int32 [48], replicated, may hold values from 0 to 63, as said below
- rivet_span: int32 [196608], P(('span', 'chord')), may hold values from 0 to 1023, as said below
- rivet_chord: int32 [196608], P(('span', 'chord')), may hold values from 0 to 4095, as said below
- rivet_stringer: int32 [196608], P(('span', 'chord')), may hold values from 0 to 47, as said below
- rivet_cell: int32 [196608], P(('span', 'chord')), may hold values from 0 to 95
- rivet_stiff: float32 [196608], P(('span', 'chord')), may hold values from 0.5 to 3
- mat_stiff: float32 [8], replicated, may hold values from 0.5 to 2
- mat_coef: float32 [8], replicated, may hold values from 0.04 to 0.16
Outputs:
- skin_out: float32 [3, 6, 1024, 4096], P(None, None, 'span', 'chord')
- stringer_out: float32 [64, 3, 6, 96, 1024], P('chord', None, None, None, 'span')
Inputs may be any that keep to these rules, and one draw needn't show every extreme that they name: Distinct slots; stringer s is held in slot owner_slot[s], on chord device owner_slot[s] // 2. `stringer_now`: slots that no stringer holds are zero. `stringer_prev`: slots that no stringer holds are zero. `rivet_span`: the 768 rows of one device (devices in span-major order) lie in that device's span slab. `rivet_chord`: each stringer's rivets lie in its foot, a band of 64 skin chord cells inside one chord device, at foot start + rivet_cell * 64 // 96; feet do not intersect and every chord device holds one or two feet, so the rows of one device put exactly 32 on the skin of each chord device with two feet and half of that on the others. `rivet_stringer`: the 768 rows of one device name every stringer exactly 768 // 48 times.
All inputs are finite; a program needn't handle non-finite values.
Results may differ from a plain program's by a relative error of at most 0.00002.
Values sent between devices are 32-bit elements; how exact they have to be, the bound alone decides.
No kernel may reach another device: no remote copies, remote signals or barrier semaphores. Data moves between devices by JAX's collectives and lax.ppermute only.
A program may use at most 128 MiB of HBM per device.

v0:
```python
import jax
import jax.numpy as jnp
from jax import lax
from jax.sharding import PartitionSpec as P

STEPS = 2


def padded(cells, sides, width):
    for axis, dim in sides:
        count = lax.axis_size(axis)
        ends = count - 1
        head = lax.slice_in_dim(cells, 0, width, axis=dim)
        tail = lax.slice_in_dim(cells, cells.shape[dim] - width, cells.shape[dim], axis=dim)
        cells = jnp.concatenate(
            [
                lax.ppermute(tail, axis, [(i, (i + 1) % count) for i in range(ends)]),
                cells,
                lax.ppermute(head, axis, [((i + 1) % count, i) for i in range(ends)]),
            ],
            axis=dim,
        )
    return cells


def bond_stiff(stiff_left, stiff_right):
    return 2.0 * stiff_left * stiff_right / (stiff_left + stiff_right)


def pad_axis(values_in, axis_dim):
    widths = [(0, 0)] * values_in.ndim
    widths[axis_dim] = (1, 1)
    return jnp.pad(values_in, widths)


def side_bonds(stiff_ext, axis_dim, comp_axis):
    inner_count = stiff_ext.shape[axis_dim] - 2
    centre = lax.slice_in_dim(stiff_ext, 1, 1 + inner_count, axis=axis_dim)
    bond_pair = []
    for offset in (0, 2):
        beside = lax.slice_in_dim(stiff_ext, offset, offset + inner_count, axis=axis_dim)
        bond_pair.append(jnp.expand_dims(bond_stiff(centre, beside), comp_axis))
    return bond_pair


def side_pull(field_ext, axis_dim, bond_pair):
    inner_count = field_ext.shape[axis_dim] - 2
    centre = lax.slice_in_dim(field_ext, 1, 1 + inner_count, axis=axis_dim)
    result = bond_pair[0] * (lax.slice_in_dim(field_ext, 0, inner_count, axis=axis_dim) - centre)
    return result + bond_pair[1] * (
        lax.slice_in_dim(field_ext, 2, 2 + inner_count, axis=axis_dim) - centre
    )


def material_lookup(material, table_values):
    looked_up = jnp.zeros(material.shape, jnp.float32)
    for material_index in range(table_values.shape[0]):
        looked_up = looked_up + jnp.where(
            material == material_index, table_values[material_index], 0.0
        )
    return looked_up


def bucket_place(targets, peer_count, capacity):
    one_hot = (targets[:, None] == jnp.arange(peer_count, dtype=jnp.int32)[None, :]).astype(
        jnp.int32
    )
    before = jnp.sum(jnp.cumsum(one_hot, axis=0) * one_hot, axis=1) - 1
    return targets * capacity + before


def slot_source(place, peer_count, capacity):
    source = jnp.full((peer_count * capacity,), -1, jnp.int32)
    return source.at[place].set(jnp.arange(place.shape[0], dtype=jnp.int32))


def pack_rows(values_in, source, peer_count, capacity):
    taken = values_in[:, jnp.maximum(source, 0)]
    filled = jnp.where(source[None, :] >= 0, taken, jnp.zeros_like(taken))
    return filled.reshape(values_in.shape[0], peer_count, capacity)


def unpack_rows(received, place):
    return received.reshape(received.shape[0], -1)[:, place]


def shards(
    skin_now,
    skin_prev,
    skin_mat,
    stringer_now,
    stringer_prev,
    stringer_mat,
    owner_slot,
    rivet_span,
    rivet_chord,
    rivet_stringer,
    rivet_cell,
    rivet_stiff,
    mat_stiff,
    mat_coef,
):
    peer_count = lax.axis_size("chord")
    slab_index = lax.axis_index("span")
    span_cells = skin_now.shape[2]
    chord_cells = skin_now.shape[3]
    thickness = skin_now.shape[1]
    local_slots = stringer_now.shape[0]
    flange_cells = stringer_now.shape[3]
    row_count = rivet_span.shape[0]
    skin_capacity = 2 * row_count // owner_slot.shape[0]
    flange_capacity = 2 * row_count // owner_slot.shape[0]
    skin_stiff = material_lookup(skin_mat, mat_stiff)
    skin_coef = material_lookup(skin_mat, mat_coef)
    flange_stiff = material_lookup(stringer_mat, mat_stiff)
    flange_coef = material_lookup(stringer_mat, mat_coef)
    stiff_ext = padded(skin_stiff, (("span", 1), ("chord", 2)), 1)
    skin_bonds = [
        side_bonds(stiff_ext[:, :, 1:-1], 1, 0),
        side_bonds(stiff_ext[:, 1:-1, :], 2, 0),
        side_bonds(pad_axis(skin_stiff, 0), 0, 0),
    ]
    flange_ext = padded(flange_stiff, (("span", 3),), 1)
    flange_bonds = [
        side_bonds(flange_ext, 3, 1),
        side_bonds(pad_axis(flange_stiff, 1), 1, 1),
        side_bonds(pad_axis(flange_stiff, 2), 2, 1),
    ]
    span_local = rivet_span - slab_index * span_cells
    skin_target = rivet_chord // chord_cells
    skin_cell = span_local * chord_cells + rivet_chord % chord_cells
    stringer_ids = jnp.arange(owner_slot.shape[0], dtype=jnp.int32)
    slot_index = jnp.sum(
        jnp.where(rivet_stringer[:, None] == stringer_ids[None, :], owner_slot[None, :], 0), axis=1
    )
    flange_target = slot_index // local_slots
    flange_cell = (
        slot_index % local_slots * flange_cells * span_cells + rivet_cell * span_cells + span_local
    )
    skin_place = bucket_place(skin_target, peer_count, skin_capacity)
    flange_place = bucket_place(flange_target, peer_count, flange_capacity)
    skin_source = slot_source(skin_place, peer_count, skin_capacity)
    flange_source = slot_source(flange_place, peer_count, flange_capacity)
    skin_asked, flange_asked = (
        lax.all_to_all(
            pack_rows(skin_cell[None], skin_source, peer_count, skin_capacity)[0],
            "chord",
            split_axis=0,
            concat_axis=0,
            tiled=True,
        ),
        lax.all_to_all(
            pack_rows(flange_cell[None], flange_source, peer_count, flange_capacity)[0],
            "chord",
            split_axis=0,
            concat_axis=0,
            tiled=True,
        ),
    )
    skin_asked = skin_asked.reshape(-1)
    flange_asked = flange_asked.reshape(-1)
    asked_slot = flange_asked // (flange_cells * span_cells)
    asked_rest = flange_asked % (flange_cells * span_cells)
    asked_cell = asked_rest // span_cells
    asked_span = asked_rest % span_cells
    stiff_held = lax.all_to_all(
        pack_rows(rivet_stiff[None], flange_source, peer_count, flange_capacity),
        "chord",
        split_axis=1,
        concat_axis=1,
        tiled=True,
    )
    for step_index in range(STEPS):
        skin_ext = padded(skin_now, (("span", 2), ("chord", 3)), 1)
        skin_pull = side_pull(skin_ext[:, :, :, 1:-1], 2, skin_bonds[0])
        skin_pull = skin_pull + side_pull(skin_ext[:, :, 1:-1, :], 3, skin_bonds[1])
        skin_pull = skin_pull + side_pull(pad_axis(skin_now, 1), 1, skin_bonds[2])
        field_ext = padded(stringer_now, (("span", 4),), 1)
        flange_pull = side_pull(field_ext, 4, flange_bonds[0])
        flange_pull = flange_pull + side_pull(pad_axis(stringer_now, 2), 2, flange_bonds[1])
        flange_pull = flange_pull + side_pull(pad_axis(stringer_now, 3), 3, flange_bonds[2])
        skin_face = skin_now[:, -1].reshape(3, -1)
        skin_asked_values = skin_face[:, skin_asked].reshape(3, peer_count, -1)
        skin_got = unpack_rows(
            lax.all_to_all(skin_asked_values, "chord", split_axis=1, concat_axis=1, tiled=True),
            skin_place,
        )
        posted = lax.all_to_all(
            pack_rows(skin_got, flange_source, peer_count, flange_capacity),
            "chord",
            split_axis=1,
            concat_axis=1,
            tiled=True,
        )
        spring_held = stiff_held * (
            posted
            - stringer_now[:, :, 0][asked_slot, :, asked_cell, asked_span].T.reshape(
                3, peer_count, -1
            )
        )
        load_field = jnp.zeros((local_slots, 3, flange_cells, span_cells), jnp.float32)
        flange_load = load_field.at[asked_slot, :, asked_cell, asked_span].add(
            spring_held.reshape(3, -1).T
        )
        spring = unpack_rows(
            lax.all_to_all(spring_held, "chord", split_axis=1, concat_axis=1, tiled=True),
            flange_place,
        )
        skin_sent = lax.all_to_all(
            pack_rows(-spring, skin_source, peer_count, skin_capacity),
            "chord",
            split_axis=1,
            concat_axis=1,
            tiled=True,
        )
        skin_load = (
            jnp.zeros((3, span_cells * chord_cells), jnp.float32)
            .at[:, skin_asked]
            .add(skin_sent.reshape(3, -1))
        )
        skin_layer = jnp.pad(
            skin_load.reshape(3, 1, span_cells, chord_cells),
            ((0, 0), (thickness - 1, 0), (0, 0), (0, 0)),
        )
        flange_layer = jnp.pad(
            flange_load[:, :, None], ((0, 0), (0, 0), (0, thickness - 1), (0, 0), (0, 0))
        )
        skin_next = 2.0 * skin_now - skin_prev + skin_coef[None] * (skin_pull + skin_layer)
        flange_next = (
            2.0 * stringer_now - stringer_prev + flange_coef[:, None] * (flange_pull + flange_layer)
        )
        skin_prev, skin_now = (skin_now, skin_next)
        stringer_prev, stringer_now = (stringer_now, flange_next)
    return (skin_now, stringer_now)


def solution(mesh):
    placed = (
        P(None, None, "span", "chord"),
        P(None, None, "span", "chord"),
        P(None, "span", "chord"),
        P("chord", None, None, None, "span"),
        P("chord", None, None, None, "span"),
        P("chord", None, None, "span"),
        P(),
        P(("span", "chord")),
        P(("span", "chord")),
        P(("span", "chord")),
        P(("span", "chord")),
        P(("span", "chord")),
        P(),
        P(),
    )
    return jax.shard_map(
        shards,
        mesh=mesh,
        in_specs=placed,
        out_specs=(P(None, None, "span", "chord"), P("chord", None, None, None, "span")),
        check_vma=False,
    )
```

profile of v0, /device:TPU:135, one launch (start us, length us, event | category | flops | bytes accessed | tf_op | source)
XLA Modules:
  0.0 589.4 jit_solution(8529958675094909636)
XLA Ops:
  5.4 7.7 %select_add_fusion.1 = (f32[2,6,96,128]{2,1,3,0:T(8,128)}, pred[2,6,96,128]{2,1,3,0:T(8,128)(4,1)S(1)}, pred[2,6,96,128]{2,1,3,0:T(8,128)(4,1)S(1)}, pred[2,6,96...) fusion(f32[]{:T(128)} %bitcast.7, f32[]{:T(128)} %bitcast.6, ...), kind=kLoop, calls=%fused_computation.140 | loop fusion | flops 3391488 | bytes 2359328 | tf_op jit(solution)/shard_map/add | solution.py:58
  13.0 6.1 %select_add_fusion = f32[2,6,96,128]{2,1,3,0:T(8,128)S(1)} fusion(pred[2,6,96,128]{2,1,3,0:T(8,128)(4,1)S(1)} %get-tuple-element.30, pred[2,6,96,128]{2,1,3,0:T(8,128)(4,1)S(1)} %get-tuple-element.29, pred[2,6,96,128]{2,1,3,0:T(8,128)(4,1)S(1)} %get-tuple-element.28, pred[2,6,96,128]{2,1,3,0:T(8,128)(4,1)S(1)} %get-tuple-element.27, ...), kind=kLoop, calls=%fused_computation.139 | loop fusion | flops 2211840 | bytes 1769504 | tf_op jit(solution)/shard_map/add | solution.py:58
  43.9 8.5 %all-to-all-start.4 = ((s32[32,1,32]{2,1,0:T(1,128)}), s32[32,1,32]{2,1,0:T(1,128)S(1)}, u32[]{:S(2)}, u32[]{:S(2)}) async-start(s32[32,1,32]{2,1,0:T(1,128)} %all_to_all.44), calls=%async_computation.4 | async-start | bytes 32768 | tf_op jit(solution)/shard_map/all_to_all | solution.py:152
  58.8 7.3 %select_add_fusion.3 = (f32[6,128,128]{2,1,0:T(8,128)}, pred[6,128,128]{2,1,0:T(8,128)(4,1)S(1)}, pred[6,128,128]{2,1,0:T(8,128)(4,1)S(1)}, pred[6,128,128]{2,1,...) fusion(f32[]{:T(128)} %bitcast.7, f32[]{:T(128)} %bitcast.6, ...), kind=kLoop, calls=%fused_computation.173 | loop fusion | flops 2260992 | bytes 1572896 | tf_op jit(solution)/shard_map/add | solution.py:58
  90.9 6.7 %copy.764 = f32[2,3,1,96,128]{1,4,3,0,2:T(8,128)} copy(f32[2,3,1,96,128]{4,3,2,1,0:T(8,128)S(1)} %slice-done) | data formatting | bytes 589824
  122.5 8.5 %all-to-all-start = ((s32[32,1,32]{2,1,0:T(1,128)}), s32[32,1,32]{2,1,0:T(1,128)S(1)}, u32[]{:S(2)}, u32[]{:S(2)}) async-start(s32[32,1,32]{2,1,0:T(1,128)} %all_to_all.39), calls=%async_computation | async-start | bytes 32768 | tf_op jit(solution)/shard_map/all_to_all | solution.py:145
  137.5 16.4 %gather_fusion.6 = f32[1024,3]{1,0:T(8,128)} fusion(f32[2,3,96,128]{1,3,2,0:T(8,128)} %bitcast.127, s32[1024]{0:T(1024)S(1)} %bitcast.121), kind=kCustom, calls=%fused_computation.6 | custom fusion | bytes 36864 | tf_op jit(solution)/shard_map/gather | solution.py:197
  155.2 7.4 %gather_fusion.2 = f32[1024,3]{1,0:T(8,128)} fusion(f32[3,16384]{0,1:T(8,128)} %bitcast.128, s32[1024]{0:T(1024)S(1)} %broadcast_clamp_fusion), kind=kCustom, calls=%fused_computation.2 | custom fusion | bytes 28672 | tf_op jit(solution)/shard_map/gather | solution.py:183
  164.6 36.6 %all-to-all-start.2 = ((f32[3,32,32]{2,0,1:T(4,128)}), f32[3,32,32]{2,0,1:T(4,128)S(1)}, u32[]{:S(2)}, u32[]{:S(2)}) async-start(f32[3,32,32]{2,0,1:T(4,128)} %copy.698), calls=%async_computation.2 | async-start | bytes 131072 | tf_op jit(solution)/shard_map/all_to_all | solution.py:185
  242.3 8.0 %all-to-all-start.1 = ((f32[1,32,32]{2,0,1:T(1,128)}), f32[1,32,32]{2,0,1:T(1,128)S(1)}, u32[]{:S(2)}, u32[]{:S(2)}) async-start(f32[1,32,32]{2,0,1:T(1,128)} %reshape.418), calls=%async_computation.1 | async-start | bytes 32768 | tf_op jit(solution)/shard_map/all_to_all | solution.py:166
  261.6 7.4 %all-to-all-start.3 = ((f32[3,32,32]{2,0,1:T(4,128)}), f32[3,32,32]{2,0,1:T(4,128)S(1)}, u32[]{:S(2)}, u32[]{:S(2)}) async-start(f32[3,32,32]{2,0,1:T(4,128)} %broadcast_select_fusion.3), calls=%async_computation.3 | async-start | bytes 131072 | tf_op jit(solution)/shard_map/all_to_all | solution.py:188
  282.3 7.7 %all-to-all-start.5 = ((f32[3,32,32]{2,0,1:T(4,128)}), f32[3,32,32]{2,0,1:T(4,128)S(1)}, u32[]{:S(2)}, u32[]{:S(2)}) async-start(f32[3,32,32]{2,0,1:T(4,128)} %subtract_multiply_fusion.1), calls=%async_computation.5 | async-start | bytes 131072 | tf_op jit(solution)/shard_map/all_to_all | solution.py:206
  290.3 11.4 %scatter_custom_fusion.4 = f32[24576,3]{1,0:T(8,128)} fusion(s32[1024]{0:T(1024)S(1)} %broadcast_select_fusion.7, f32[1024,3]{1,0:T(8,128)S(1)} %copy.739, f32[]{:T(128)} %constant.125.clone.1), kind=kCustom, calls=%fused_computation.23 | custom fusion | flops 3072 | bytes 294916
  301.7 7.7 %copy.741 = f32[2,96,128,3]{2,1,3,0:T(8,128)S(1)} copy(f32[2,96,128,3]{3,2,1,0:T(8,128)} %bitcast.124) | data formatting | bytes 589824
  320.6 7.4 %all-to-all-start.6 = ((f32[3,32,32]{2,0,1:T(4,128)}), f32[3,32,32]{2,0,1:T(4,128)S(1)}, u32[]{:S(2)}, u32[]{:S(2)}) async-start(f32[3,32,32]{2,0,1:T(4,128)} %broadcast_select_fusion.2), calls=%async_computation.6 | async-start | bytes 131072 | tf_op jit(solution)/shard_map/all_to_all | solution.py:209
  344.5 10.2 %scatter_custom_fusion.2 = f32[3,16384]{0,1:T(8,128)} fusion(s32[1024]{0:T(1024)S(1)} %bitcast.156, f32[1024,3]{1,0:T(8,128)S(1)} %copy.706, f32[]{:T(128)} %constant.125.clone.1), kind=kCustom, calls=%fused_computation.27 | custom fusion | flops 3072 | bytes 196612 | tf_op jit(solution)/shard_map/scatter-add | solution.py:219
  354.7 6.6 %copy.707 = f32[3,1,128,128]{2,1,3,0:T(1,128)S(1)} copy(f32[3,1,128,128]{0,3,2,1:T(8,128)} %bitcast.126) | data formatting | bytes 393216 | tf_op jit(solution)/shard_map/reshape | solution.py:222
  361.3 10.3 %fusion.70 = f32[3,6,128,128]{2,1,3,0:T(8,128)S(1)} fusion(f32[3,6,128,128]{2,1,3,0:T(8,128)} %copy.670, f32[3,6,130,1]{2,1,3,0:T(8,128)} %collective-permute-done.7, f32[3,6,1,128]{2,1,3,0:T(8,128)} %copy.681, f32[3,6,1,128]{2,1,3,0:T(8,128)} %copy.675, f32[3,6,130,1]{2,1,3,0:T(8,128)} %collective-permute-done.5, f32[3,1,128,128]{2,1,3,0:T(1,128)S(1)} %copy.707, ...), kind=kLoop, calls=%fused_computation.112 | loop fusion | flops 8847360 | bytes 6525216 | tf_op jit(solution)/shard_map/add | solution.py:228
  371.8 7.5 %copy.715 = f32[3,1,128,128]{0,3,2,1:T(8,128)} copy(f32[3,1,128,128]{2,1,3,0:T(1,128)S(1)} %slice.413) | data formatting | bytes 393216 | tf_op jit(solution)/shard_map/slice | solution.py:182
  379.3 7.7 %gather_fusion.9 = f32[1024,3]{1,0:T(8,128)} fusion(f32[3,16384]{0,1:T(8,128)} %bitcast.129, s32[1024]{0:T(1024)} %copy-done.21), kind=kCustom, calls=%fused_computation.9 | custom fusion | bytes 28672 | tf_op jit(solution)/shard_map/gather | solution.py:183
  389.0 7.9 %all-to-all-start.7 = ((f32[3,32,32]{2,0,1:T(4,128)}), f32[3,32,32]{2,0,1:T(4,128)S(1)}, u32[]{:S(2)}, u32[]{:S(2)}) async-start(f32[3,32,32]{2,0,1:T(4,128)} %copy.716), calls=%async_computation.7 | async-start | bytes 131072 | tf_op jit(solution)/shard_map/all_to_all | solution.py:185
  420.9 7.9 %all-to-all-start.8 = ((f32[3,32,32]{2,0,1:T(4,128)}), f32[3,32,32]{2,0,1:T(4,128)S(1)}, u32[]{:S(2)}, u32[]{:S(2)}) async-start(f32[3,32,32]{2,0,1:T(4,128)} %broadcast_select_fusion.1), calls=%async_computation.8 | async-start | bytes 131072 | tf_op jit(solution)/shard_map/all_to_all | solution.py:188
  430.6 7.7 %copy.742 = f32[2,3,96,128]{1,3,2,0:T(8,128)} copy(f32[2,3,96,128]{3,2,1,0:T(8,128)} %slice_bitcast_fusion) | data formatting | bytes 589824 | tf_op jit(solution)/shard_map/squeeze | solution.py:197
  438.3 16.5 %gather_fusion.12 = f32[1024,3]{1,0:T(8,128)} fusion(f32[2,3,96,128]{1,3,2,0:T(8,128)} %copy.742, s32[1024]{0:T(1024)S(1)} %bitcast.122), kind=kCustom, calls=%fused_computation.12 | custom fusion | bytes 36864 | tf_op jit(solution)/shard_map/gather | solution.py:197
  465.1 37.0 %all-to-all-start.9 = ((f32[3,32,32]{2,0,1:T(4,128)}), f32[3,32,32]{2,0,1:T(4,128)S(1)}, u32[]{:S(2)}, u32[]{:S(2)}) async-start(f32[3,32,32]{2,0,1:T(4,128)} %subtract_multiply_fusion), calls=%async_computation.9 | async-start | bytes 131072 | tf_op jit(solution)/shard_map/all_to_all | solution.py:206
  510.4 11.8 %scatter_custom_fusion.5 = f32[24576,3]{1,0:T(8,128)} fusion(s32[1024]{0:T(1024)} %copy-done.26, f32[1024,3]{1,0:T(8,128)} %copy.754, f32[]{:T(128)} %constant.125.clone.1), kind=kCustom, calls=%fused_computation.21 | custom fusion | flops 3072 | bytes 295424
  522.2 8.3 %copy.756 = f32[2,96,128,3]{2,1,3,0:T(8,128)} copy(f32[2,96,128,3]{3,2,1,0:T(8,128)} %bitcast.123) | data formatting | bytes 589824
  543.5 9.0 %all-to-all-start.10 = ((f32[3,32,32]{2,0,1:T(4,128)}), f32[3,32,32]{2,0,1:T(4,128)S(1)}, u32[]{:S(2)}, u32[]{:S(2)}) async-start(f32[3,32,32]{2,0,1:T(4,128)} %broadcast_select_fusion), calls=%async_computation.10 | async-start | bytes 131072 | tf_op jit(solution)/shard_map/all_to_all | solution.py:209
  552.5 9.8 %fusion.23 = f32[2,3,6,96,128]{4,3,2,1,0:T(8,128)} fusion(f32[2,3,6,96,128]{4,3,2,1,0:T(8,128)} %fusion.14, f32[2,3,6,96,1]{4,3,2,1,0:T(8,128)} %copy.752, f32[2,3,6,96,1]{4,3,2,1,0:T(8,128)} %copy.750, f32[2,3,1,96,128]{4,3,2,1,0:T(8,128)} %bitcast.132, f32[2,3,6,96,128]{4,3,2,1,0:T(8,128)S(1)} %copy-done.2, f32[2,6,96,128]{3,2,1,0:T(8,128)} %copy.737, ...), kind=kLoop, calls=%fused_computation.52 | loop fusion | flops 10616832 | bytes 9759744 | tf_op jit(solution)/shard_map/add | solution.py:230
  562.7 10.2 %scatter_custom_fusion.3 = f32[3,16384]{0,1:T(8,128)} fusion(s32[1024]{0:T(1024)} %bitcast.157, f32[1024,3]{1,0:T(8,128)S(1)} %copy.747, f32[]{:T(128)} %constant.125.clone.1), kind=kCustom, calls=%fused_computation.25 | custom fusion | flops 3072 | bytes 197120 | tf_op jit(solution)/shard_map/scatter-add | solution.py:219
  572.9 6.7 %copy.748 = f32[3,1,128,128]{2,1,3,0:T(1,128)S(1)} copy(f32[3,1,128,128]{0,3,2,1:T(8,128)} %bitcast.125) | data formatting | bytes 393216 | tf_op jit(solution)/shard_map/reshape | solution.py:222
  579.6 6.7 %fusion.55 = f32[3,6,128,128]{2,1,3,0:T(8,128)} fusion(f32[3,6,128,128]{2,1,3,0:T(8,128)S(1)} %fusion.70, f32[3,6,130,1]{2,1,3,0:T(8,128)} %collective-permute-done.11, f32[3,6,1,128]{2,1,3,0:T(8,128)} %copy.712, f32[3,6,1,128]{2,1,3,0:T(8,128)} %copy.710, f32[3,6,130,1]{2,1,3,0:T(8,128)} %collective-permute-done.10, f32[3,1,128,128]{2,1,3,0:T(1,128)S(1)} %copy.748, ...), kind=kLoop, calls=%fused_computation.89 | loop fusion | flops 8847360 | bytes 6525216 | tf_op jit(solution)/shard_map/add | solution.py:228
  (258 shorter events, 251.1 us)
Async XLA Ops:
  19.7 181.4 %collective-permute-start.12 = (f32[2,6,96,1]{2,1,3,0:T(8,128)}, f32[2,6,96,1]{2,1,3,0:T(8,128)}, u32[]{:S(2)}, u32[]{:S(2)}) collective-permute-start(f32[2,6,96,1]{2,1,3,0:T(8,128)} %get-tuple-element.66), channel_id=1, source_target_pairs={{0,32},{32,64},{64,96},{96,128},{128,160},{160,192},{192,224},{1,3... | collective-permute-start | bytes 13832 | tf_op jit(solution)/shard_map/ppermute | solution.py:17
  22.4 182.2 %collective-permute-start.14 = (f32[2,6,96,1]{2,1,3,0:T(8,128)}, f32[2,6,96,1]{2,1,3,0:T(8,128)}, u32[]{:S(2)}, u32[]{:S(2)}) collective-permute-start(f32[2,6,96,1]{2,1,3,0:T(8,128)} %get-tuple-element.67), channel_id=1, source_target_pairs={{32,0},{64,32},{96,64},{128,96},{160,128},{192,160},{224,192},{33,... | collective-permute-start | bytes 13832 | tf_op jit(solution)/shard_map/ppermute | solution.py:19
  43.9 78.5 %all-to-all-start.4 = ((s32[32,1,32]{2,1,0:T(1,128)}), s32[32,1,32]{2,1,0:T(1,128)S(1)}, u32[]{:S(2)}, u32[]{:S(2)}) async-start(s32[32,1,32]{2,1,0:T(1,128)} %all_to_all.44), calls=%async_computation.4 | async-start | bytes 32768 | tf_op jit(solution)/shard_map/all_to_all | solution.py:152
  56.9 218.9 %collective-permute-start.13 = (f32[2,3,6,96,1]{3,0,4,2,1:T(2,128)S(1)}, f32[2,3,6,96,1]{3,0,4,2,1:T(2,128)}, u32[]{:S(2)}, u32[]{:S(2)}) collective-permute-start(f32[2,3,6,96,1]{3,0,4,2,1:T(2,128)S(1)} %copy.765), channel_id=1, source_target_pairs={{0,32},{32,64},{64,96},{96,128},{128,160},{160,192},{192,224},{1,3... | collective-permute-start | bytes 41480 | tf_op jit(solution)/shard_map/ppermute | solution.py:17
  72.3 42.7 %collective-permute-start = (f32[6,1,128]{2,1,0:T(1,128)S(1)}, f32[6,1,128]{2,1,0:T(1,128)S(1)}, u32[]{:S(2)}, u32[]{:S(2)}) collective-permute-start(f32[6,1,128]{2,1,0:T(1,128)S(1)} %get-tuple-element.76), channel_id=1, source_target_pairs={{0,32},{32,64},{64,96},{96,128},{128,160},{160,192},{192,224},{1,3... | collective-permute-start | bytes 9224 | tf_op jit(solution)/shard_map/ppermute | solution.py:17
  74.4 44.0 %collective-permute-start.2 = (f32[6,1,128]{2,1,0:T(1,128)S(1)}, f32[6,1,128]{2,1,0:T(1,128)S(1)}, u32[]{:S(2)}, u32[]{:S(2)}) collective-permute-start(f32[6,1,128]{2,1,0:T(1,128)S(1)} %get-tuple-element.77), channel_id=1, source_target_pairs={{32,0},{64,32},{96,64},{128,96},{160,128},{192,160},{224,192},{33,... | collective-permute-start | bytes 9224 | tf_op jit(solution)/shard_map/ppermute | solution.py:19
  87.9 227.4 %copy-start.17 = (s32[1024]{0:T(1024)}, s32[1024]{0:T(1024)S(1)}, u32[]{:S(2)}) copy-start(s32[1024]{0:T(1024)S(1)} %pad_clamp_fusion) | copy-start | bytes 12292
  88.0 173.0 %copy-start.15 = (pred[32,32]{1,0:T(8,128)(4,1)}, pred[32,32]{1,0:T(8,128)(4,1)S(1)}, u32[]{:S(2)}) copy-start(pred[32,32]{1,0:T(8,128)(4,1)S(1)} %broadcast_in_dim.281) | copy-start | bytes 3076
  115.0 163.3 %collective-permute-start.15 = (f32[2,3,6,96,1]{3,0,4,2,1:T(2,128)}, f32[2,3,6,96,1]{3,0,4,2,1:T(2,128)}, u32[]{:S(2)}, u32[]{:S(2)}) collective-permute-start(f32[2,3,6,96,1]{3,0,4,2,1:T(2,128)} %copy.766), channel_id=1, source_target_pairs={{32,0},{64,32},{96,64},{128,96},{160,128},{192,160},{224,192},{33,... | collective-permute-start | bytes 41480 | tf_op jit(solution)/shard_map/ppermute | solution.py:19
  118.5 119.7 %collective-permute-start.1 = (f32[3,6,1,128]{3,1,2,0:T(8,128)}, f32[3,6,1,128]{3,1,2,0:T(8,128)S(1)}, u32[]{:S(2)}, u32[]{:S(2)}) collective-permute-start(f32[3,6,1,128]{3,1,2,0:T(8,128)} %copy.762), channel_id=1, source_target_pairs={{0,32},{32,64},{64,96},{96,128},{128,160},{160,192},{192,224},{1,3... | collective-permute-start | bytes 27656 | tf_op jit(solution)/shard_map/ppermute | solution.py:17
  122.5 13.7 %all-to-all-start = ((s32[32,1,32]{2,1,0:T(1,128)}), s32[32,1,32]{2,1,0:T(1,128)S(1)}, u32[]{:S(2)}, u32[]{:S(2)}) async-start(s32[32,1,32]{2,1,0:T(1,128)} %all_to_all.39), calls=%async_computation | async-start | bytes 32768 | tf_op jit(solution)/shard_map/all_to_all | solution.py:145
  137.5 207.0 %copy-start.22 = (s32[1024,1]{0,1:T(1,128)}, s32[1024,1]{0,1:T(1,128)S(1)}, u32[]{:S(2)}) copy-start(s32[1024,1]{0,1:T(1,128)S(1)} %compare_select_fusion.3) | copy-start | bytes 12292
  164.6 77.7 %all-to-all-start.2 = ((f32[3,32,32]{2,0,1:T(4,128)}), f32[3,32,32]{2,0,1:T(4,128)S(1)}, u32[]{:S(2)}, u32[]{:S(2)}) async-start(f32[3,32,32]{2,0,1:T(4,128)} %copy.698), calls=%async_computation.2 | async-start | bytes 131072 | tf_op jit(solution)/shard_map/all_to_all | solution.py:185
  201.2 21.0 %collective-permute-start.4 = (f32[6,130,1]{2,1,0:T(8,128)}, f32[6,130,1]{2,1,0:T(8,128)}, u32[]{:S(2)}, u32[]{:S(2)}) collective-permute-start(f32[6,130,1]{2,1,0:T(8,128)} %get-tuple-element.68), channel_id=1, source_target_pairs={{0,1},{1,2},{2,3},{3,4},{4,5},{5,6},{6,7},{7,8},{8,9},{9,10},{10,1... | collective-permute-start | bytes 9368 | tf_op jit(solution)/shard_map/ppermute | solution.py:17
  204.5 22.5 %collective-permute-start.6 = (f32[6,130,1]{2,1,0:T(8,128)}, f32[6,130,1]{2,1,0:T(8,128)}, u32[]{:S(2)}, u32[]{:S(2)}) collective-permute-start(f32[6,130,1]{2,1,0:T(8,128)} %get-tuple-element.69), channel_id=1, source_target_pairs={{1,0},{2,1},{3,2},{4,3},{5,4},{6,5},{7,6},{8,7},{9,8},{10,9},{11,1... | collective-permute-start | bytes 9368 | tf_op jit(solution)/shard_map/ppermute | solution.py:19
  222.2 17.6 %collective-permute-start.3 = (f32[3,6,1,128]{3,1,2,0:T(8,128)}, f32[3,6,1,128]{3,1,2,0:T(8,128)}, u32[]{:S(2)}, u32[]{:S(2)}) collective-permute-start(f32[3,6,1,128]{3,1,2,0:T(8,128)} %copy.763), channel_id=1, source_target_pairs={{32,0},{64,32},{96,64},{128,96},{160,128},{192,160},{224,192},{33,... | collective-permute-start | bytes 27656 | tf_op jit(solution)/shard_map/ppermute | solution.py:19
  242.3 19.3 %all-to-all-start.1 = ((f32[1,32,32]{2,0,1:T(1,128)}), f32[1,32,32]{2,0,1:T(1,128)S(1)}, u32[]{:S(2)}, u32[]{:S(2)}) async-start(f32[1,32,32]{2,0,1:T(1,128)} %reshape.418), calls=%async_computation.1 | async-start | bytes 32768 | tf_op jit(solution)/shard_map/all_to_all | solution.py:166
  261.6 19.1 %all-to-all-start.3 = ((f32[3,32,32]{2,0,1:T(4,128)}), f32[3,32,32]{2,0,1:T(4,128)S(1)}, u32[]{:S(2)}, u32[]{:S(2)}) async-start(f32[3,32,32]{2,0,1:T(4,128)} %broadcast_select_fusion.3), calls=%async_computation.3 | async-start | bytes 131072 | tf_op jit(solution)/shard_map/all_to_all | solution.py:188
  270.5 90.8 %collective-permute-start.5 = (f32[3,6,130,1]{2,1,3,0:T(8,128)}, f32[3,6,130,1]{2,1,3,0:T(8,128)}, u32[]{:S(2)}, u32[]{:S(2)}) collective-permute-start(f32[3,6,130,1]{2,1,3,0:T(8,128)} %get-tuple-element.50), channel_id=1, source_target_pairs={{0,1},{1,2},{2,3},{3,4},{4,5},{5,6},{6,7},{7,8},{8,9},{9,10},{10,1... | collective-permute-start | bytes 28088 | tf_op jit(solution)/shard_map/ppermute | solution.py:17
  273.9 87.5 %collective-permute-start.7 = (f32[3,6,130,1]{2,1,3,0:T(8,128)}, f32[3,6,130,1]{2,1,3,0:T(8,128)}, u32[]{:S(2)}, u32[]{:S(2)}) collective-permute-start(f32[3,6,130,1]{2,1,3,0:T(8,128)} %get-tuple-element.51), channel_id=1, source_target_pairs={{1,0},{2,1},{3,2},{4,3},{5,4},{6,5},{7,6},{8,7},{9,8},{10,9},{11,1... | collective-permute-start | bytes 28088 | tf_op jit(solution)/shard_map/ppermute | solution.py:19
  282.3 32.7 %all-to-all-start.5 = ((f32[3,32,32]{2,0,1:T(4,128)}), f32[3,32,32]{2,0,1:T(4,128)S(1)}, u32[]{:S(2)}, u32[]{:S(2)}) async-start(f32[3,32,32]{2,0,1:T(4,128)} %subtract_multiply_fusion.1), calls=%async_computation.5 | async-start | bytes 131072 | tf_op jit(solution)/shard_map/all_to_all | solution.py:206
  320.6 23.5 %all-to-all-start.6 = ((f32[3,32,32]{2,0,1:T(4,128)}), f32[3,32,32]{2,0,1:T(4,128)S(1)}, u32[]{:S(2)}, u32[]{:S(2)}) async-start(f32[3,32,32]{2,0,1:T(4,128)} %broadcast_select_fusion.2), calls=%async_computation.6 | async-start | bytes 131072 | tf_op jit(solution)/shard_map/all_to_all | solution.py:209
  335.0 121.0 %collective-permute-start.16 = (f32[2,3,6,96,1]{3,0,4,2,1:T(2,128)}, f32[2,3,6,96,1]{3,0,4,2,1:T(2,128)}, u32[]{:S(2)}, u32[]{:S(2)}) collective-permute-start(f32[2,3,6,96,1]{3,0,4,2,1:T(2,128)} %copy.749), channel_id=1, source_target_pairs={{0,32},{32,64},{64,96},{96,128},{128,160},{160,192},{192,224},{1,3... | collective-permute-start | bytes 41480 | tf_op jit(solution)/shard_map/ppermute | solution.py:17
  339.6 119.0 %collective-permute-start.17 = (f32[2,3,6,96,1]{3,0,4,2,1:T(2,128)}, f32[2,3,6,96,1]{3,0,4,2,1:T(2,128)}, u32[]{:S(2)}, u32[]{:S(2)}) collective-permute-start(f32[2,3,6,96,1]{3,0,4,2,1:T(2,128)} %copy.751), channel_id=1, source_target_pairs={{32,0},{64,32},{96,64},{128,96},{160,128},{192,160},{224,192},{33,... | collective-permute-start | bytes 41480 | tf_op jit(solution)/shard_map/ppermute | solution.py:19
  389.0 20.6 %all-to-all-start.7 = ((f32[3,32,32]{2,0,1:T(4,128)}), f32[3,32,32]{2,0,1:T(4,128)S(1)}, u32[]{:S(2)}, u32[]{:S(2)}) async-start(f32[3,32,32]{2,0,1:T(4,128)} %copy.716), calls=%async_computation.7 | async-start | bytes 131072 | tf_op jit(solution)/shard_map/all_to_all | solution.py:185
  401.0 60.1 %collective-permute-start.8 = (f32[3,6,1,128]{3,1,2,0:T(8,128)S(1)}, f32[3,6,1,128]{3,1,2,0:T(8,128)S(1)}, u32[]{:S(2)}, u32[]{:S(2)}) collective-permute-start(f32[3,6,1,128]{3,1,2,0:T(8,128)S(1)} %copy.709), channel_id=1, source_target_pairs={{0,32},{32,64},{64,96},{96,128},{128,160},{160,192},{192,224},{1,3... | collective-permute-start | bytes 27656 | tf_op jit(solution)/shard_map/ppermute | solution.py:17
  404.9 57.8 %collective-permute-start.9 = (f32[3,6,1,128]{3,1,2,0:T(8,128)S(1)}, f32[3,6,1,128]{3,1,2,0:T(8,128)S(1)}, u32[]{:S(2)}, u32[]{:S(2)}) collective-permute-start(f32[3,6,1,128]{3,1,2,0:T(8,128)S(1)} %copy.711), channel_id=1, source_target_pairs={{32,0},{64,32},{96,64},{128,96},{160,128},{192,160},{224,192},{33,... | collective-permute-start | bytes 27656 | tf_op jit(solution)/shard_map/ppermute | solution.py:19
  420.9 43.5 %all-to-all-start.8 = ((f32[3,32,32]{2,0,1:T(4,128)}), f32[3,32,32]{2,0,1:T(4,128)S(1)}, u32[]{:S(2)}, u32[]{:S(2)}) async-start(f32[3,32,32]{2,0,1:T(4,128)} %broadcast_select_fusion.1), calls=%async_computation.8 | async-start | bytes 131072 | tf_op jit(solution)/shard_map/all_to_all | solution.py:188
  465.1 65.3 %all-to-all-start.9 = ((f32[3,32,32]{2,0,1:T(4,128)}), f32[3,32,32]{2,0,1:T(4,128)S(1)}, u32[]{:S(2)}, u32[]{:S(2)}) async-start(f32[3,32,32]{2,0,1:T(4,128)} %subtract_multiply_fusion), calls=%async_computation.9 | async-start | bytes 131072 | tf_op jit(solution)/shard_map/all_to_all | solution.py:206
  503.0 76.6 %collective-permute-start.10 = (f32[3,6,130,1]{2,1,3,0:T(8,128)S(1)}, f32[3,6,130,1]{2,1,3,0:T(8,128)}, u32[]{:S(2)}, u32[]{:S(2)}) collective-permute-start(f32[3,6,130,1]{2,1,3,0:T(8,128)S(1)} %get-tuple-element.48), channel_id=1, source_target_pairs={{0,1},{1,2},{2,3},{3,4},{4,5},{5,6},{6,7},{7,8},{8,9},{9,10},{10,1... | collective-permute-start | bytes 28088 | tf_op jit(solution)/shard_map/ppermute | solution.py:17
  506.4 73.3 %collective-permute-start.11 = (f32[3,6,130,1]{2,1,3,0:T(8,128)S(1)}, f32[3,6,130,1]{2,1,3,0:T(8,128)}, u32[]{:S(2)}, u32[]{:S(2)}) collective-permute-start(f32[3,6,130,1]{2,1,3,0:T(8,128)S(1)} %get-tuple-element.49), channel_id=1, source_target_pairs={{1,0},{2,1},{3,2},{4,3},{5,4},{6,5},{7,6},{8,7},{9,8},{10,9},{11,1... | collective-permute-start | bytes 28088 | tf_op jit(solution)/shard_map/ppermute | solution.py:19
  543.5 18.8 %all-to-all-start.10 = ((f32[3,32,32]{2,0,1:T(4,128)}), f32[3,32,32]{2,0,1:T(4,128)S(1)}, u32[]{:S(2)}, u32[]{:S(2)}) async-start(f32[3,32,32]{2,0,1:T(4,128)} %broadcast_select_fusion), calls=%async_computation.10 | async-start | bytes 131072 | tf_op jit(solution)/shard_map/all_to_all | solution.py:209
  (32 other events, 677.9 us)
where the time goes:
time: 601 us; the launch traced here: 589 us
  local copies, waits for them, and re-layouts  260 us (43%)
  starting transfers between devices  200 us (33%)
  other arithmetic  123 us (20%)
    all_to_all x2, starting transfers between devices, shards(): lax.all_to_all(spring_held, 'chord', split_axis=1, concat_axis=1, tiled=T...  44.7 us
    all_to_all x2, starting transfers between devices, shards(): lax.all_to_all(skin_asked_values, 'chord', split_axis=1, concat_axis=1, t...  44.5 us
    unnamed x77, local copies, waits for them, and re-layouts  39.5 us
    gather x11, local copies, waits for them, and re-layouts, pack_rows(): taken = values_in[:, jnp.maximum(source, 0)]  35.6 us
    gather x2, local copies, waits for them, and re-layouts, shards(): stringer_now[:, :, 0][asked_slot, :, asked_cell, asked_span]  32.9 us
    ppermute x9, starting transfers between devices, padded(): lax.ppermute(head, axis, [((i + 1) % count, i) for i in range(ends)])  31.6 us
    add x4, other arithmetic, material_lookup(): looked_up + jnp.where(material == material_index, table_values[material_i...  26.4 us
    unnamed x5, other arithmetic  23.3 us
  transfers between devices with their start and end apart: 29, of which 1 were waited for; matrix products, arithmetic and copies ran while one was open for 60% of the time, Pallas kernels for 0%

commit v1 on v0

v1 whole, which is shorter than its diff:
```python
import jax
import jax.numpy as jnp
from jax import lax
from jax.experimental import pallas as pl
from jax.experimental.pallas import tpu as pltpu
from jax.sharding import PartitionSpec as P

F32 = jnp.float32
BF16 = jnp.bfloat16
NT = (((1,), (1,)), ((), ()))
TN = (((0,), (0,)), ((), ()))
FIELDS = 7


def iota(shape, dim):
    return lax.broadcasted_iota(jnp.int32, shape, dim)


def two_parts(values):
    high = values.astype(BF16)
    return high, (values - high.astype(F32)).astype(BF16)


def pick(mask, values):
    return jnp.where(mask, values, 0.0).astype(BF16)


def params():
    return pltpu.CompilerParams(vmem_limit_bytes=48 * 1024 * 1024)


def call(body, outs, ins, name, smem=(), flops=0, nbytes=0):
    specs = [
        pl.BlockSpec(memory_space=pltpu.SMEM) if i in smem else pl.BlockSpec(memory_space=pltpu.VMEM)
        for i in range(len(ins))
    ]
    return pl.pallas_call(
        body,
        out_shape=[jax.ShapeDtypeStruct(s, F32) for s in outs],
        in_specs=specs,
        out_specs=[pl.BlockSpec(memory_space=pltpu.VMEM) for _ in outs],
        compiler_params=params(),
        cost_estimate=pl.CostEstimate(flops=flops, bytes_accessed=nbytes, transcendentals=0),
        name=name,
    )(*ins)


def tables(stiff_ref, coef_ref):
    half = [0.5 / jnp.full((1, 128), stiff_ref[m], F32) for m in range(8)]
    return half, [coef_ref[m] for m in range(8)]


def half_of(mat, tabs):
    out = jnp.broadcast_to(tabs[0][0], mat.shape)
    for m in range(1, 8):
        out = jnp.where(mat == m, tabs[0][m], out)
    return out


def half_coef(mat, tabs):
    half = jnp.broadcast_to(tabs[0][0], mat.shape)
    coef = jnp.full(mat.shape, tabs[1][0], F32)
    for m in range(1, 8):
        same = mat == m
        half = jnp.where(same, tabs[0][m], half)
        coef = jnp.where(same, tabs[1][m], coef)
    return half, coef


def edge_bond(half, beside):
    return jnp.where(beside > 0.0, 1.0 / (half + beside), 0.0)


def layer_bonds(half, rows, cols):
    count = half.shape[0]
    row, lane = iota(half.shape, 0), iota(half.shape, 1)
    below = pltpu.roll(half, count - 1, 0)
    down = 1.0 / (half + below)
    if rows is None:
        down = jnp.where(row == count - 1, 0.0, down)
        first = None
    else:
        first = edge_bond(half[0:1], rows[0])
        last = edge_bond(half[count - 1 : count], rows[1])
        down = jnp.where(row == count - 1, last, down)
    across = 1.0 / (half + pltpu.roll(half, 127, 1))
    left = edge_bond(half[:, 0:1], cols[0])
    right = edge_bond(half[:, 127:128], cols[1])
    across = jnp.where(lane == 127, right, across)
    return down, first, across, left


def layer_pull(cells, bonds, rows, cols):
    down, first, across, left = bonds
    count = cells.shape[0]
    row, lane = iota(cells.shape, 0), iota(cells.shape, 1)
    below = pltpu.roll(cells, count - 1, 0)
    if rows is not None:
        below = jnp.where(row == count - 1, rows[1], below)
    flux = down * (below - cells)
    above = pltpu.roll(flux, 1, 0)
    if rows is not None:
        above = jnp.where(row == 0, first * (cells[0:1] - rows[0]), above)
    beside = jnp.where(lane == 127, cols[1], pltpu.roll(cells, 127, 1))
    side = across * (beside - cells)
    before = jnp.where(lane == 0, left * (cells[:, 0:1] - cols[0]), pltpu.roll(side, 1, 1))
    return (flux - above) + (side - before)


def update_layer(layer, comps, now, prev, half, coef, thick, rows, cols, half_rows, half_cols, extra, put):
    bonds = layer_bonds(half, half_rows, half_cols)
    for comp in range(comps):
        cells = now(comp, layer)
        pull = layer_pull(cells, bonds, rows(comp), cols(comp))
        if layer < 5:
            pull = pull + thick(layer) * (now(comp, layer + 1) - cells)
        if layer > 0:
            pull = pull + thick(layer - 1) * (now(comp, layer - 1) - cells)
        if extra is not None:
            pull = pull + extra(comp)
        put(comp, 2.0 * cells - prev(comp, layer) + coef * pull)


def skin_rows(before, after, index):
    return before[index : index + 1, :], after[index : index + 1, :]


def lanes_of(before, after, index):
    return before[:, index : index + 1], after[:, index : index + 1]


def prep_body(span_ref, chord_ref, stringer_ref, cell_ref, stiff_ref, owner_ref, out_ref, match_ref):
    def row_of(ref):
        return ref[...]

    span, chord, stringer = row_of(span_ref), row_of(chord_ref), row_of(stringer_ref)
    cell, stiff = row_of(cell_ref), row_of(stiff_ref)
    count = span.shape[1]
    chunks = count // 128
    same = iota((48, count), 0) == stringer
    owner = owner_ref[...]
    slot = jnp.sum(jnp.where(same, owner, 0).astype(F32), axis=0, keepdims=True).astype(jnp.int32)
    foot = (chord - (((2 * cell) * 171) >> 9)) >> 6
    foot_of = jnp.max(jnp.where(same, foot, 0).astype(F32), axis=1, keepdims=True).astype(jnp.int32)
    slots = iota((48, 64), 1)
    slot_hot = (slots == (owner & 1) * 32 + (owner >> 1)).astype(F32).astype(BF16)
    foot_hot = (slots == (foot_of & 1) * 32 + (foot_of >> 1)).astype(F32).astype(BF16)
    match_ref[0:64, 0:64] = lax.dot_general(foot_hot, slot_hot, TN, preferred_element_type=F32)
    match_ref[64:128, 0:64] = lax.dot_general(slot_hot, foot_hot, TN, preferred_element_type=F32)
    one = same.astype(F32)
    lower = (iota((128, 128), 0) < iota((128, 128), 1)).astype(F32).astype(BF16)
    both = jnp.concatenate([lower, jnp.ones((128, 128), BF16)], axis=1)
    offset = jnp.zeros((48, 128), F32)
    ranks = []
    for k in range(chunks):
        part = one[:, k * 128 : (k + 1) * 128]
        ahead = jnp.dot(part.astype(BF16), both, preferred_element_type=F32)
        ranks.append(jnp.sum(part * (ahead[:, :128] + offset), axis=0, keepdims=True))
        offset = offset + ahead[:, 128:]
    rank = jnp.concatenate(ranks, axis=1).astype(jnp.int32)
    place = iota((128, count), 0)
    place = place == jnp.where(
        place < 64, (slot & 1) * 32 + (slot >> 1), 64 + (foot & 1) * 32 + (foot >> 1)
    )
    place = place.astype(F32).astype(BF16)
    order = iota((16, count), 0) == rank
    high = stiff.astype(BF16).astype(F32)
    rest = stiff - high
    middle = rest.astype(BF16).astype(F32)
    fields = [cell.astype(F32), (span & 127).astype(F32), (chord & 127).astype(F32), high, middle, rest - middle]
    rows = jnp.concatenate([pick(order, f) for f in fields], axis=0)
    got = lax.dot_general(place, rows, NT, preferred_element_type=F32)
    for side in range(2):
        index, weight = [], []
        for p in range(2):
            part = got[side * 64 + p * 32 : side * 64 + p * 32 + 32]
            where_, across = part[:, 0:16], part[:, 16:32]
            if side == 1:
                where_, across = part[:, 16:32], part[:, 32:48]
            index.append(where_ * 128.0 + across)
            weight.append(part[:, 48:64] + part[:, 64:80] + part[:, 80:96])
        out_ref[:, side * 64 : side * 64 + 64] = jnp.concatenate(index + weight, axis=1)


def halo_body(stiff_ref, coef_ref, skin_ref, mat_ref, str_ref, smat_ref, last_ref, first_ref, right_ref, left_ref):
    tabs = tables(stiff_ref, coef_ref)
    lane = iota((128, 128), 1)
    slane = iota((96, 128), 1)
    right = jnp.zeros((128, 128), F32)
    left = jnp.zeros((128, 128), F32)
    for l in range(6):
        half = half_of(mat_ref[l], tabs)
        for f, tile in [(c * 6 + l, skin_ref[c, l]) for c in range(3)] + [(18 + l, half)]:
            last_ref[f : f + 1, :] = tile[127:128, :]
            first_ref[f : f + 1, :] = tile[0:1, :]
            right = jnp.where(lane == f, tile[:, 127:128], right)
            left = jnp.where(lane == f, tile[:, 0:1], left)
    right_ref[...] = right
    left_ref[...] = left
    last = jnp.zeros((96, 128), F32)
    first = jnp.zeros((96, 128), F32)
    for p in range(2):
        for t in range(6):
            half = half_of(smat_ref[p, t], tabs)
            tiles = [((p * 3 + c) * 6 + t, str_ref[p, c, t]) for c in range(3)] + [(36 + p * 6 + t, half)]
            for f, tile in tiles:
                last = jnp.where(slane == f, tile[:, 127:128], last)
                first = jnp.where(slane == f, tile[:, 0:1], first)
    last_ref[24:120, :] = last
    first_ref[24:120, :] = first


def exchange(last, first, right, left):
    up = [(i, i + 1) for i in range(lax.axis_size("span") - 1)]
    side = [(i, i + 1) for i in range(lax.axis_size("chord") - 1)]
    back = lambda pairs: [(b, a) for a, b in pairs]
    before = lax.ppermute(last, "span", up)
    after = lax.ppermute(first, "span", back(up))
    lefts = lax.ppermute(right, "chord", side)
    rights = lax.ppermute(left, "chord", back(side))
    return before, after, lefts, rights


def row_lists(index):
    return jnp.concatenate([index[q * 8 : q * 8 + 8, :] for q in range(4)], axis=1)


def one_row(values):
    return jnp.concatenate([values[a : a + 1, :] for a in range(8)], axis=1)


def hots(rows_ref):
    text = one_row(row_lists(rows_ref[:, 0:32])).astype(jnp.int32)
    tk = one_row(row_lists(rows_ref[:, 32:64]))
    sext = one_row(row_lists(rows_ref[:, 64:96])).astype(jnp.int32)
    sk = one_row(row_lists(rows_ref[:, 96:128]))
    slot = ((iota((1, 1024), 1) >> 4) & 1) * 128
    t_row = iota((96, 1024), 0) == (text >> 7)
    t_lane = (iota((256, 1024), 0) == (text & 127) + slot).astype(F32).astype(BF16)
    s_row = iota((128, 1024), 0) == (sext >> 7)
    s_lane = (iota((128, 1024), 0) == (sext & 127)).astype(F32).astype(BF16)
    return (t_row, t_lane, tk), (s_row, s_lane, sk)


def spread(row_mask, lane_hot, values):
    high, low = two_parts(values)
    left = jnp.concatenate([pick(row_mask, high.astype(F32)), pick(row_mask, low.astype(F32))], axis=1)
    right = jnp.concatenate([lane_hot, lane_hot], axis=1)
    return lax.dot_general(left, right, NT, preferred_element_type=F32)


def fetch(row_mask, lane_hot2, cells):
    high, low = two_parts(cells)
    wide = jnp.dot(jnp.concatenate([high, low], axis=1), lane_hot2, preferred_element_type=F32)
    return jnp.sum(jnp.where(row_mask, wide, 0.0), axis=0, keepdims=True)


def as_lanes(row):
    return jnp.concatenate([row[:, a * 128 : (a + 1) * 128] for a in range(8)], axis=0)


def gather_body(
    stiff_ref, coef_ref, rows_ref, skin_ref, skin_prev_ref, mat_ref, str_ref, str_prev_ref, smat_ref,
    before_ref, after_ref, lefts_ref, rights_ref,
    out_ref, ks_ref, ps_ref, cs_ref, kt_ref, pt_ref, ct_ref,
):
    tabs = tables(stiff_ref, coef_ref)
    (t_row, t_lane, tk), (s_row, s_lane, sk) = hots(rows_ref)
    k_skin = spread(s_row, s_lane, sk)
    k_str = spread(t_row, t_lane, tk)
    ks_ref[...] = k_skin
    kt_ref[...] = k_str
    under = half_of(mat_ref[0], tabs)
    half, coef = half_coef(mat_ref[1], tabs)
    bt = 1.0 / (half + under)
    skin_fields = [skin_ref[c, 1] for c in range(3)]
    cs_ref[...] = coef

    def put_skin(c, value):
        moved = value - coef * k_skin * skin_fields[c]
        ps_ref[c] = moved

    update_layer(
        5, 3, lambda c, l: skin_ref[c, l - 4], lambda c, l: skin_prev_ref[c, 0], half, coef, lambda l: bt,
        lambda c: skin_rows(before_ref, after_ref, c * 6 + 5), lambda c: lanes_of(lefts_ref, rights_ref, c * 6 + 5),
        skin_rows(before_ref, after_ref, 23), lanes_of(lefts_ref, rights_ref, 23), None, put_skin,
    )
    for p in range(2):
        over = half_of(smat_ref[p, 1], tabs)
        half_t, coef_t = half_coef(smat_ref[p, 0], tabs)
        bt_t = 1.0 / (half_t + over)
        ct_ref[:, p * 128 : p * 128 + 128] = coef_t
        kt = k_str[:, p * 128 : p * 128 + 128]

        def put_str(c, value, p=p, coef_t=coef_t, kt=kt):
            pt_ref[c, :, p * 128 : p * 128 + 128] = value - coef_t * kt * str_ref[p, c, 0]

        def cols(f):
            return before_ref[24:120, f : f + 1], after_ref[24:120, f : f + 1]

        update_layer(
            0, 3, lambda c, l: str_ref[p, c, l], lambda c, l: str_prev_ref[p, c, 0], half_t, coef_t, lambda l: bt_t,
            lambda c: None, lambda c: cols((p * 3 + c) * 6), None, cols(36 + p * 6), None, put_str,
        )
    t_fields = [jnp.concatenate([str_ref[0, c, 0], str_ref[1, c, 0]], axis=1) for c in range(3)]
    t_fields += [pt_ref[c] for c in range(3)] + [ct_ref[...] * k_str]
    s_fields = skin_fields + [ps_ref[c] for c in range(3)] + [coef]
    t_two = jnp.concatenate([t_lane, t_lane], axis=0)
    s_two = jnp.concatenate([s_lane, s_lane], axis=0)
    got = [as_lanes(fetch(t_row, t_two, f)) for f in t_fields]
    got += [as_lanes(fetch(s_row, s_two, f)) for f in s_fields]
    pad = jnp.zeros((8, 64), F32)
    for q in range(4):
        out_ref[q * 8 : q * 8 + 8, :] = jnp.concatenate([g[:, q * 32 : q * 32 + 32] for g in got] + [pad], axis=1)


def bounce_body(match_ref, got_ref, out_ref):
    got = got_ref[...]
    lane = iota(got.shape, 1)
    zero = (lane & 16) == 0

    def turned(base):
        def part(to, frm):
            m = match_ref[base + to * 32 : base + to * 32 + 32, frm * 32 : frm * 32 + 32]
            return jnp.dot(m, got, preferred_element_type=F32, precision=lax.Precision.HIGHEST)

        a = part(0, 0) + pltpu.roll(part(0, 1), 512 - 16, 1)
        b = part(1, 1) + pltpu.roll(part(1, 0), 16, 1)
        return jnp.where(zero, a, b)

    out_ref[...] = jnp.where(lane < FIELDS * 32, turned(0), turned(64))


def load_body(
    rows_ref, posted_ref, ks_ref, ps_ref, cs_ref, kt_ref, pt_ref, ct_ref, skin_ref, str_ref,
    last_in, first_in, right_in, left_in,
    skin1_ref, sload_ref, str1_ref, tload_ref, last_ref, first_ref, right_ref, left_ref,
):
    (t_row, t_lane, tk), (s_row, s_lane, sk) = hots(rows_ref)

    def sums(side, row_mask, lane_hot, weight, f):
        at = (side * FIELDS + f) * 32
        return spread(row_mask, lane_hot, weight * one_row(row_lists(posted_ref[:, at : at + 32])))

    last_ref[...] = last_in[...]
    first_ref[...] = first_in[...]
    lane = iota((128, 128), 1)
    right, left = right_in[...], left_in[...]
    ks, cs = ks_ref[...], cs_ref[...]
    qs = sums(0, s_row, s_lane, sk, 6)
    for c in range(3):
        now = skin_ref[c, 0]
        new = ps_ref[c] + cs * sums(0, s_row, s_lane, sk, c)
        skin1_ref[c] = new
        sload_ref[c] = sums(0, s_row, s_lane, sk, 3 + c) + qs * now - ks * new
        f = c * 6 + 5
        last_ref[f : f + 1, :] = new[127:128, :]
        first_ref[f : f + 1, :] = new[0:1, :]
        right = jnp.where(lane == f, new[:, 127:128], right)
        left = jnp.where(lane == f, new[:, 0:1], left)
    right_ref[...] = right
    left_ref[...] = left
    kt, ct = kt_ref[...], ct_ref[...]
    qt = sums(1, t_row, t_lane, tk, 6)
    third = iota((96, 256), 0) % 3
    slane = iota((96, 128), 1)
    last, first = last_in[24:120, :], first_in[24:120, :]
    for c in range(3):
        now = jnp.concatenate([str_ref[0, c, 0], str_ref[1, c, 0]], axis=1)
        own = kt * now
        pair = jnp.where(third == 0, pltpu.roll(own, 95, 0), jnp.where(third == 1, pltpu.roll(own, 1, 0), 0.0))
        new = pt_ref[c] + ct * sums(1, t_row, t_lane, tk, c)
        load = sums(1, t_row, t_lane, tk, 3 + c) + qt * (own + pair) - kt * new
        for p in range(2):
            str1_ref[p, c] = new[:, p * 128 : p * 128 + 128]
            tload_ref[p, c] = load[:, p * 128 : p * 128 + 128]
            f = (p * 3 + c) * 6
            last = jnp.where(slane == f, new[:, p * 128 + 127 : p * 128 + 128], last)
            first = jnp.where(slane == f, new[:, p * 128 : p * 128 + 1], first)
    last_ref[24:120, :] = last
    first_ref[24:120, :] = first


def whole_step(tabs, mat_ref, smat_ref, skin, skin_prev, stringer, str_prev, halos, skin_layers, str_layers, skin_load, str_load, put_skin, put_str):
    before_ref, after_ref, lefts_ref, rights_ref, hb_ref, ha_ref, hl_ref, hr_ref = halos
    halves = [half_coef(mat_ref[l], tabs) for l in range(6)]
    bt = [1.0 / (halves[l][0] + halves[l + 1][0]) for l in range(5)]
    for l in skin_layers:
        update_layer(
            l, 3, skin, skin_prev, halves[l][0], halves[l][1], lambda m: bt[m],
            lambda c: skin_rows(before_ref, after_ref, c * 6 + l),
            lambda c: lanes_of(lefts_ref, rights_ref, c * 6 + l),
            skin_rows(hb_ref, ha_ref, 18 + l), lanes_of(hl_ref, hr_ref, 18 + l),
            skin_load if l == 5 else None, lambda c, v: put_skin(c, l, v),
        )
    for p in range(2):
        th = [half_coef(smat_ref[p, t], tabs) for t in range(6)]
        tb = [1.0 / (th[t][0] + th[t + 1][0]) for t in range(5)]

        def cols(b, a, f):
            return b[24:120, f : f + 1], a[24:120, f : f + 1]

        for t in str_layers:
            update_layer(
                t, 3, lambda c, m: stringer(p, c, m), lambda c, m: str_prev(p, c, m), th[t][0], th[t][1], lambda m: tb[m],
                lambda c: None, lambda c: cols(before_ref, after_ref, (p * 3 + c) * 6 + t),
                None, cols(hb_ref, ha_ref, 36 + p * 6 + t),
                (lambda c: str_load(p, c)) if (t == 0 and str_load is not None) else None,
                lambda c, v: put_str(p, c, t, v),
            )


def first_body(
    stiff_ref, coef_ref, skin_ref, skin_prev_ref, mat_ref, str_ref, str_prev_ref, smat_ref,
    before_ref, after_ref, lefts_ref, rights_ref,
    skin1_ref, str1_ref, last_ref, first_ref, right_ref, left_ref,
):
    tabs = tables(stiff_ref, coef_ref)
    lane = iota((128, 128), 1)
    slane = iota((96, 128), 1)
    zero = jnp.zeros((128, 128), F32)
    right_ref[...] = zero
    left_ref[...] = zero
    last_ref[...] = jnp.zeros((120, 128), F32)
    first_ref[...] = jnp.zeros((120, 128), F32)

    def put_skin(c, l, value):
        skin1_ref[c, l] = value
        f = c * 6 + l
        last_ref[f : f + 1, :] = value[127:128, :]
        first_ref[f : f + 1, :] = value[0:1, :]
        right_ref[...] = jnp.where(lane == f, value[:, 127:128], right_ref[...])
        left_ref[...] = jnp.where(lane == f, value[:, 0:1], left_ref[...])

    def put_str(p, c, t, value):
        str1_ref[p, c, t - 1] = value
        f = (p * 3 + c) * 6 + t
        last_ref[24:120, :] = jnp.where(slane == f, value[:, 127:128], last_ref[24:120, :])
        first_ref[24:120, :] = jnp.where(slane == f, value[:, 0:1], first_ref[24:120, :])

    halos = (before_ref, after_ref, lefts_ref, rights_ref) * 2
    whole_step(
        tabs, mat_ref, smat_ref, lambda c, l: skin_ref[c, l], lambda c, l: skin_prev_ref[c, l],
        lambda p, c, t: str_ref[p, c, t], lambda p, c, t: str_prev_ref[p, c, t], halos,
        range(5), range(1, 6), None, None, put_skin, put_str,
    )


def second_body(
    stiff_ref, coef_ref, skin_ref, skin_prev_ref, mat_ref, str_ref, str_prev_ref, smat_ref,
    hb_ref, ha_ref, hl_ref, hr_ref, before_ref, after_ref, lefts_ref, rights_ref,
    skin_face_ref, str_face_ref, sload_ref, tload_ref, skin2_ref, str2_ref,
):
    tabs = tables(stiff_ref, coef_ref)
    halos = (before_ref, after_ref, lefts_ref, rights_ref, hb_ref, ha_ref, hl_ref, hr_ref)

    def put_skin(c, l, value):
        skin2_ref[c, l] = value

    def put_str(p, c, t, value):
        str2_ref[p, c, t] = value

    whole_step(
        tabs, mat_ref, smat_ref,
        lambda c, l: skin_face_ref[c] if l == 5 else skin_ref[c, l], lambda c, l: skin_prev_ref[c, l],
        lambda p, c, t: str_face_ref[p, c] if t == 0 else str_ref[p, c, t - 1],
        lambda p, c, t: str_prev_ref[p, c, t], halos, range(6), range(6),
        lambda c: sload_ref[c], lambda p, c: tload_ref[p, c], put_skin, put_str,
    )


def swap(values):
    return lax.all_to_all(values, "chord", split_axis=0, concat_axis=0, tiled=True)


def blocks(shape, at):
    return pl.BlockSpec(shape, lambda i: at)


def gather_call(ins):
    whole = lambda a: pl.BlockSpec(a.shape, lambda i, n=a.ndim: (0,) * n)
    specs = [pl.BlockSpec(memory_space=pltpu.SMEM)] * 2 + [whole(ins[2])]
    specs += [
        blocks((3, 2, 128, 128), (0, 2, 0, 0)),
        blocks((3, 1, 128, 128), (0, 5, 0, 0)),
        blocks((2, 128, 128), (2, 0, 0)),
        blocks((2, 3, 2, 96, 128), (0, 0, 0, 0, 0)),
        blocks((2, 3, 1, 96, 128), (0, 0, 0, 0, 0)),
        blocks((2, 2, 96, 128), (0, 0, 0, 0)),
    ] + [whole(a) for a in ins[9:]]
    outs = [(32, 512), (128, 128), (3, 128, 128), (128, 128), (96, 256), (3, 96, 256), (96, 256)]
    return pl.pallas_call(
        gather_body, grid=(1,), in_specs=specs,
        out_shape=[jax.ShapeDtypeStruct(s, F32) for s in outs],
        out_specs=[pl.BlockSpec(s, lambda i, n=len(s): (0,) * n) for s in outs],
        compiler_params=params(), name="gather",
        cost_estimate=pl.CostEstimate(flops=1000000000, bytes_accessed=2000000, transcendentals=0),
    )(*ins)


def load_call(ins):
    whole = lambda a: pl.BlockSpec(a.shape, lambda i, n=a.ndim: (0,) * n)
    specs = [whole(a) for a in ins[:8]]
    specs += [blocks((3, 1, 128, 128), (0, 5, 0, 0)), blocks((2, 3, 1, 96, 128), (0, 0, 0, 0, 0))]
    specs += [whole(a) for a in ins[10:]]
    outs = [(3, 128, 128), (3, 128, 128), (2, 3, 96, 128), (2, 3, 96, 128), (120, 128), (120, 128), (128, 128), (128, 128)]
    return pl.pallas_call(
        load_body, grid=(1,), in_specs=specs,
        out_shape=[jax.ShapeDtypeStruct(s, F32) for s in outs],
        out_specs=[pl.BlockSpec(s, lambda i, n=len(s): (0,) * n) for s in outs],
        compiler_params=params(), name="load",
        cost_estimate=pl.CostEstimate(flops=1000000000, bytes_accessed=2000000, transcendentals=0),
    )(*ins)


def shards(
    skin_now, skin_prev, skin_mat, stringer_now, stringer_prev, stringer_mat, owner_slot,
    rivet_span, rivet_chord, rivet_stringer, rivet_cell, rivet_stiff, mat_stiff, mat_coef,
):
    rivets = [a.reshape(1, -1) for a in (rivet_span, rivet_chord, rivet_stringer, rivet_cell, rivet_stiff)]
    sent, match = call(prep_body, [(32, 128), (128, 128)], rivets + [owner_slot.reshape(-1, 1)], "prep")
    rows = swap(sent)
    packs = call(
        halo_body, [(120, 128), (120, 128), (128, 128), (128, 128)],
        [mat_stiff, mat_coef, skin_now, skin_mat, stringer_now, stringer_mat], "halo", smem=(0, 1),
        flops=4000000, nbytes=4000000,
    )
    halos = exchange(*packs)
    mats = [mat_stiff, mat_coef]
    own = [skin_now, skin_prev, skin_mat, stringer_now, stringer_prev, stringer_mat]
    found, *kept = gather_call([*mats, rows, *own, *halos])
    given = swap(found)
    skin1, str1, *packs1 = call(
        first_body, [(3, 5, 128, 128), (2, 3, 5, 96, 128), (120, 128), (120, 128), (128, 128), (128, 128)],
        [*mats, *own, *halos], "first", smem=(0, 1), flops=20000000, nbytes=10000000,
    )
    (turned,) = call(bounce_body, [(32, 512)], [match, given], "bounce")
    posted = swap(turned)
    skin_face, sload, str_face, tload, *packs2 = load_call([rows, posted, *kept, skin_now, stringer_now, *packs1])
    halos1 = exchange(*packs2)
    return call(
        second_body, [(3, 6, 128, 128), (2, 3, 6, 96, 128)],
        [*mats, skin1, skin_now, skin_mat, str1, stringer_now, stringer_mat, *halos, *halos1, skin_face, str_face, sload, tload],
        "second", smem=(0, 1), flops=20000000, nbytes=10000000,
    )


def solution(mesh):
    placed = (
        P(None, None, "span", "chord"),
        P(None, None, "span", "chord"),
        P(None, "span", "chord"),
        P("chord", None, None, None, "span"),
        P("chord", None, None, None, "span"),
        P("chord", None, None, "span"),
        P(),
        P(("span", "chord")),
        P(("span", "chord")),
        P(("span", "chord")),
        P(("span", "chord")),
        P(("span", "chord")),
        P(),
        P(),
    )
    body = jax.shard_map(
        shards,
        mesh=mesh,
        in_specs=placed,
        out_specs=(P(None, None, "span", "chord"), P("chord", None, None, None, "span")),
        check_vma=False,
    )
    return lambda *args: tuple(body(*args))
```

time: 601 us -> 147 us (0.24)
  the two profiles are of different devices: /device:TPU:135 before, /device:TPU:102 now
where the time goes in v1:
time: 147 us; the launch traced here: 145 us
  Pallas kernels  51 us (35%)
  starting transfers between devices  35.9 us (24%)
  local copies, waits for them, and re-layouts  30.1 us (20%)
  blocking collectives  21.6 us (15%)
  waiting for transfers between devices  5.41 us (4%)
    pallas_call x5, Pallas kernels, call(): pl.pallas_call(body, out_shape=[jax.ShapeDtypeStruct(s, F32) for s in out...  42.8 us
    unnamed x118, local copies, waits for them, and re-layouts  28 us
    all_to_all x2, blocking collectives, swap(): lax.all_to_all(values, 'chord', split_axis=0, concat_axis=0, tiled=True)  21.6 us
    ppermute x2, starting transfers between devices, exchange(): rights = lax.ppermute(left, 'chord', back(side))  11.4 us
    ppermute x2, starting transfers between devices, exchange(): before = lax.ppermute(last, 'span', up)  10.2 us
    all_to_all x1, starting transfers between devices, swap(): lax.all_to_all(values, 'chord', split_axis=0, concat_axis=0, tiled=True)  6.58 us
    ppermute x2, waiting for transfers between devices, exchange(): after = lax.ppermute(first, 'span', back(up))  5.39 us
    pallas_call x1, Pallas kernels, gather_call(): pl.pallas_call(gather_body, grid=(1,), in_specs=specs, out_shape=[jax.Sha...  4.27 us
  transfers between devices with their start and end apart: 9, of which 1 were waited for; matrix products, arithmetic and copies ran while one was open for 1% of the time, Pallas kernels for 14%

profile of v1, /device:TPU:102, one launch (start us, length us, event | category | flops | bytes accessed | tf_op | source)
XLA Modules:
  0.0 145.2 jit_solution(12188835948575057625)
XLA Ops:
  0.6 1.5 %copy-done = f32[2,3,6,96,128]{4,3,2,1,0:T(8,128)S(1)} copy-done((f32[2,3,6,96,128]{4,3,2,1,0:T(8,128)S(1)}, f32[2,3,6,96,128]{4,3,2,1,0:T(8,128)}, u32[]{:S(2)}) %copy-start) | copy-done | bytes 1769496
  2.1 1.3 copy-done.2
  3.4 1.1 copy-done.4
  4.4 1.0 copy-done.6
  6.8 3.8 %halo.1 = (f32[120,128]{1,0:T(8,128)}, f32[120,128]{1,0:T(8,128)}, f32[128,128]{1,0:T(8,128)}, f32[128,128]{1,0:T(8,128)}) custom-call(f32[8]{0:T(128)S(1)} %copy-done.45, f32[8]{0:T(128)S(1)} %copy-done.49, f32[3,6,128,128]{3,2,1,0:T(8,128)S(1)} %copy-done.2, s32[6,128,128]{2,1,0:T(8,128)S(1)} %copy-done.6, f32[2,3,6,96,128]{4,3,2,1,0:T(8,128)S(1)} %copy-done, ...), custom_call_target="tpu_custom_call" | custom-call | flops 4000000 | bytes 4000000 | tf_op jit(solution)/shard_map/halo/pallas_call | solution.py:37
  10.6 1.9 %collective-permute-start.2 = (f32[128,128]{1,0:T(8,128)}, f32[128,128]{1,0:T(8,128)S(1)}, u32[]{:S(2)}, u32[]{:S(2)}) collective-permute-start(f32[128,128]{1,0:T(8,128)} %get-tuple-element.31), channel_id=1, source_target_pairs={{0,1},{1,2},{2,3},{3,4},{4,5},{5,6},{6,7},{7,8},{8,9},{9,10},{10,1... | collective-permute-start | bytes 196616 | tf_op jit(solution)/shard_map/ppermute | solution.py:219
  12.6 5.8 %collective-permute-start.3 = (f32[128,128]{1,0:T(8,128)}, f32[128,128]{1,0:T(8,128)S(1)}, u32[]{:S(2)}, u32[]{:S(2)}) collective-permute-start(f32[128,128]{1,0:T(8,128)} %get-tuple-element.32), channel_id=1, source_target_pairs={{1,0},{2,1},{3,2},{4,3},{5,4},{6,5},{7,6},{8,7},{9,8},{10,9},{11,1... | collective-permute-start | bytes 196616 | tf_op jit(solution)/shard_map/ppermute | solution.py:220
  18.3 5.0 %collective-permute-start = (f32[120,128]{1,0:T(8,128)}, f32[120,128]{1,0:T(8,128)S(1)}, u32[]{:S(2)}, u32[]{:S(2)}) collective-permute-start(f32[120,128]{1,0:T(8,128)} %get-tuple-element.29), channel_id=1, source_target_pairs={{0,32},{32,64},{64,96},{96,128},{128,160},{160,192},{192,224},{1,3... | collective-permute-start | bytes 184328 | tf_op jit(solution)/shard_map/ppermute | solution.py:217
  23.4 1.9 %collective-permute-start.1 = (f32[120,128]{1,0:T(8,128)}, f32[120,128]{1,0:T(8,128)}, u32[]{:S(2)}, u32[]{:S(2)}) collective-permute-start(f32[120,128]{1,0:T(8,128)} %get-tuple-element.30), channel_id=1, source_target_pairs={{32,0},{64,32},{96,64},{128,96},{160,128},{192,160},{224,192},{33,... | collective-permute-start | bytes 184328 | tf_op jit(solution)/shard_map/ppermute | solution.py:218
  25.4 1.3 copy.17.owner_ref
  28.2 10.8 %all_to_all.33 = f32[32,1,128]{2,1,0:T(1,128)S(1)} all-to-all(f32[32,1,128]{2,1,0:T(1,128)S(1)} %bitcast.19), channel_id=1, replica_groups=mesh['span'=8,'chord'=32] {'chord'}, dimensions={0} | all-to-all | bytes 32768 | tf_op jit(solution)/shard_map/all_to_all | solution.py:473
  40.4 4.3 %gather.1 = (f32[32,512]{1,0:T(8,128)S(1)}, f32[128,128]{1,0:T(8,128)S(1)}, f32[3,128,128]{2,1,0:T(8,128)S(1)}, f32[128,128]{1,0:T(8,128)S(1)}, f32[96,256]{1,0:...) custom-call(f32[8]{0:T(128)S(1)} %copy-done.46, f32[8]{0:T(128)S(1)} %copy-done.50, ...), custom_call_target="tpu_custom_call" | custom-call | flops 1000000000 | bytes 2000000 | tf_op jit(solution)/shard_map/gather/pallas_call | solution.py:492
  45.5 10.8 %all_to_all.34 = f32[32,1,512]{2,1,0:T(1,128)S(1)} all-to-all(f32[32,1,512]{2,1,0:T(1,128)S(1)} %copy.19), channel_id=1, replica_groups=mesh['span'=8,'chord'=32] {'chord'}, dimensions={0} | all-to-all | bytes 131072 | tf_op jit(solution)/shard_map/all_to_all | solution.py:473
  57.7 6.6 %all-to-all-start.2 = ((f32[32,1,512]{2,1,0:T(1,128)}), f32[32,1,512]{2,1,0:T(1,128)}, u32[]{:S(2)}, u32[]{:S(2)}) async-start(f32[32,1,512]{2,1,0:T(1,128)} %copy.20), calls=%async_computation.2 | async-start | bytes 131072 | tf_op jit(solution)/shard_map/all_to_all | solution.py:473
  64.3 1.0 copy-done.8
  65.3 1.3 copy-done.11
  66.5 0.8 copy-done.16
  67.4 0.8 copy-done.19
  70.4 19.7 %first.1 = (f32[3,5,128,128]{3,2,1,0:T(8,128)S(1)}, f32[2,3,5,96,128]{4,3,2,1,0:T(8,128)}, f32[120,128]{1,0:T(8,128)S(1)}, f32[120,128]{1,0:T(8,128)S(1)}, f32[1...) custom-call(f32[8]{0:T(128)S(1)} %copy-done.47, f32[8]{0:T(128)S(1)} %copy-done.51, f32[3,6,128,128]{3,2,1,0:T(8,128)S(1)} %copy-done.3, ...), custom_call_target="tpu_custom_call" | custom-call | flops 20000000 | bytes 10000000 | tf_op jit(solution)/shard_map/first/pallas_call | solution.py:37
  90.1 0.9 copy-done.13
  93.5 0.8 copy.25
  94.4 1.0 copy-done.25
  95.3 0.9 copy-done.27
  96.3 0.9 copy-done.30
  97.2 0.9 copy-done.32
  103.1 3.9 %load.1 = (f32[3,128,128]{2,1,0:T(8,128)S(1)}, f32[3,128,128]{2,1,0:T(8,128)S(1)}, f32[2,3,96,128]{3,2,1,0:T(8,128)S(1)}, f32[2,3,96,128]{3,2,1,0:T(8,128)S(1)},...) custom-call(f32[32,128]{1,0:T(8,128)S(1)} %bitcast.17, ...), custom_call_target="tpu_custom_call" | custom-call | flops 1000000000 | bytes 2000000 | tf_op jit(solution)/shard_map/load/pallas_call | solution.py:507
  107.0 2.1 %collective-permute-start.6 = (f32[128,128]{1,0:T(8,128)S(1)}, f32[128,128]{1,0:T(8,128)S(1)}, u32[]{:S(2)}, u32[]{:S(2)}) collective-permute-start(f32[128,128]{1,0:T(8,128)S(1)} %get-tuple-element.50), channel_id=1, source_target_pairs={{0,1},{1,2},{2,3},{3,4},{4,5},{5,6},{6,7},{7,8},{8,9},{9,10},{10,1... | collective-permute-start | bytes 196616 | tf_op jit(solution)/shard_map/ppermute | solution.py:219
  109.1 5.6 %collective-permute-start.7 = (f32[128,128]{1,0:T(8,128)S(1)}, f32[128,128]{1,0:T(8,128)S(1)}, u32[]{:S(2)}, u32[]{:S(2)}) collective-permute-start(f32[128,128]{1,0:T(8,128)S(1)} %get-tuple-element.51), channel_id=1, source_target_pairs={{1,0},{2,1},{3,2},{4,3},{5,4},{6,5},{7,6},{8,7},{9,8},{10,9},{11,1... | collective-permute-start | bytes 196616 | tf_op jit(solution)/shard_map/ppermute | solution.py:220
  114.7 5.1 %collective-permute-start.4 = (f32[120,128]{1,0:T(8,128)S(1)}, f32[120,128]{1,0:T(8,128)S(1)}, u32[]{:S(2)}, u32[]{:S(2)}) collective-permute-start(f32[120,128]{1,0:T(8,128)S(1)} %get-tuple-element.48), channel_id=1, source_target_pairs={{0,32},{32,64},{64,96},{96,128},{128,160},{160,192},{192,224},{1,3... | collective-permute-start | bytes 184328 | tf_op jit(solution)/shard_map/ppermute | solution.py:217
  119.8 1.9 %collective-permute-start.5 = (f32[120,128]{1,0:T(8,128)S(1)}, f32[120,128]{1,0:T(8,128)S(1)}, u32[]{:S(2)}, u32[]{:S(2)}) collective-permute-start(f32[120,128]{1,0:T(8,128)S(1)} %get-tuple-element.49), channel_id=1, source_target_pairs={{32,0},{64,32},{96,64},{128,96},{160,128},{192,160},{224,192},{33,... | collective-permute-start | bytes 184328 | tf_op jit(solution)/shard_map/ppermute | solution.py:218
  121.8 5.4 %collective-permute-done.5.after_ref = f32[120,128]{1,0:T(8,128)S(1)} collective-permute-done((f32[120,128]{1,0:T(8,128)S(1)}, f32[120,128]{1,0:T(8,128)S(1)}, u32[]{:S(2)}, u32[]{:S(2)}) %collective-permute-start.5) | collective-permute-done | bytes 61472 | tf_op jit(solution)/shard_map/ppermute | solution.py:218
  127.3 18.0 %second.1 = (f32[3,6,128,128]{3,2,1,0:T(8,128)}, f32[2,3,6,96,128]{4,3,2,1,0:T(8,128)}) custom-call(f32[8]{0:T(128)S(1)} %copy-done.48, f32[8]{0:T(128)S(1)} %copy-done.52, f32[3,5,128,128]{3,2,1,0:T(8,128)S(1)} %copy-done.14, f32[3,6,128,128]{3,2,1,0:T(8,128)S(1)} %copy-done.3, s32[6,128,128]{2,1,0:T(8,128)S(1)} %copy-done.9, ...), custom_call_target="tpu_custom_call" | custom-call | flops 20000000 | bytes 10000000 | tf_op jit(solution)/shard_map/second/pallas_call | solution.py:37
  (121 shorter events, 16.0 us)
Async XLA Ops:
  6.8 18.5 %copy-start.53 = (s32[768]{0:T(1024)S(1)}, s32[768]{0:T(1024)}, u32[]{:S(2)}) copy-start(s32[768]{0:T(1024)} %param.21) | copy-start | bytes 9220
  6.8 18.6 %copy-start.54 = (s32[768]{0:T(1024)S(1)}, s32[768]{0:T(1024)}, u32[]{:S(2)}) copy-start(s32[768]{0:T(1024)} %param.22) | copy-start | bytes 9220
  6.8 18.6 %copy-start.55 = (s32[768]{0:T(1024)S(1)}, s32[768]{0:T(1024)}, u32[]{:S(2)}) copy-start(s32[768]{0:T(1024)} %param.23) | copy-start | bytes 9220
  6.8 18.6 %copy-start.56 = (s32[768]{0:T(1024)S(1)}, s32[768]{0:T(1024)}, u32[]{:S(2)}) copy-start(s32[768]{0:T(1024)} %param.24) | copy-start | bytes 9220
  6.8 18.6 %copy-start.57 = (f32[768]{0:T(1024)S(1)}, f32[768]{0:T(1024)}, u32[]{:S(2)}) copy-start(f32[768]{0:T(1024)} %param.25) | copy-start | bytes 9220
  6.8 32.2 %copy-start.3 = (f32[3,6,128,128]{3,2,1,0:T(8,128)S(1)}, f32[3,6,128,128]{3,2,1,0:T(8,128)}, u32[]{:S(2)}) copy-start(f32[3,6,128,128]{3,2,1,0:T(8,128)} %skin_prev_ref.5) | copy-start | bytes 3538948
  6.8 32.2 %copy-start.5 = (s32[2,6,96,128]{3,2,1,0:T(8,128)S(1)}, s32[2,6,96,128]{3,2,1,0:T(8,128)}, u32[]{:S(2)}) copy-start(s32[2,6,96,128]{3,2,1,0:T(8,128)} %smat_ref.7) | copy-start | bytes 1769476
  6.8 32.2 %copy-start.7 = (s32[6,128,128]{2,1,0:T(8,128)S(1)}, s32[6,128,128]{2,1,0:T(8,128)}, u32[]{:S(2)}) copy-start(s32[6,128,128]{2,1,0:T(8,128)} %mat_ref.7) | copy-start | bytes 1179652
  6.8 32.2 %copy-start.10 = (f32[3,6,128,128]{3,2,1,0:T(8,128)S(1)}, f32[3,6,128,128]{3,2,1,0:T(8,128)}, u32[]{:S(2)}) copy-start(f32[3,6,128,128]{3,2,1,0:T(8,128)} %skin_prev_ref.4) | copy-start | bytes 3538948
  10.6 28.3 %collective-permute-start.2 = (f32[128,128]{1,0:T(8,128)}, f32[128,128]{1,0:T(8,128)S(1)}, u32[]{:S(2)}, u32[]{:S(2)}) collective-permute-start(f32[128,128]{1,0:T(8,128)} %get-tuple-element.31), channel_id=1, source_target_pairs={{0,1},{1,2},{2,3},{3,4},{4,5},{5,6},{6,7},{7,8},{8,9},{9,10},{10,1... | collective-permute-start | bytes 196616 | tf_op jit(solution)/shard_map/ppermute | solution.py:219
  12.6 26.4 %collective-permute-start.3 = (f32[128,128]{1,0:T(8,128)}, f32[128,128]{1,0:T(8,128)S(1)}, u32[]{:S(2)}, u32[]{:S(2)}) collective-permute-start(f32[128,128]{1,0:T(8,128)} %get-tuple-element.32), channel_id=1, source_target_pairs={{1,0},{2,1},{3,2},{4,3},{5,4},{6,5},{7,6},{8,7},{9,8},{10,9},{11,1... | collective-permute-start | bytes 196616 | tf_op jit(solution)/shard_map/ppermute | solution.py:220
  18.3 20.7 %collective-permute-start = (f32[120,128]{1,0:T(8,128)}, f32[120,128]{1,0:T(8,128)S(1)}, u32[]{:S(2)}, u32[]{:S(2)}) collective-permute-start(f32[120,128]{1,0:T(8,128)} %get-tuple-element.29), channel_id=1, source_target_pairs={{0,32},{32,64},{64,96},{96,128},{128,160},{160,192},{192,224},{1,3... | collective-permute-start | bytes 184328 | tf_op jit(solution)/shard_map/ppermute | solution.py:217
  23.4 15.6 %collective-permute-start.1 = (f32[120,128]{1,0:T(8,128)}, f32[120,128]{1,0:T(8,128)}, u32[]{:S(2)}, u32[]{:S(2)}) collective-permute-start(f32[120,128]{1,0:T(8,128)} %get-tuple-element.30), channel_id=1, source_target_pairs={{32,0},{64,32},{96,64},{128,96},{160,128},{192,160},{224,192},{33,... | collective-permute-start | bytes 184328 | tf_op jit(solution)/shard_map/ppermute | solution.py:218
  45.4 11.6 %copy-start.26 = (f32[3,128,128]{2,1,0:T(8,128)}, f32[3,128,128]{2,1,0:T(8,128)S(1)}, u32[]{:S(2)}) copy-start(f32[3,128,128]{2,1,0:T(8,128)S(1)} %get-tuple-element.39.ps_ref) | copy-start | bytes 589828
  45.4 11.6 %copy-start.29 = (f32[96,256]{1,0:T(8,128)}, f32[96,256]{1,0:T(8,128)S(1)}, u32[]{:S(2)}) copy-start(f32[96,256]{1,0:T(8,128)S(1)} %get-tuple-element.41.kt_ref) | copy-start | bytes 294916
  45.4 11.6 %copy-start.31 = (f32[96,256]{1,0:T(8,128)}, f32[96,256]{1,0:T(8,128)S(1)}, u32[]{:S(2)}) copy-start(f32[96,256]{1,0:T(8,128)S(1)} %get-tuple-element.43.ct_ref) | copy-start | bytes 294916
  45.4 11.6 %copy-start.33 = (f32[128,128]{1,0:T(8,128)}, f32[128,128]{1,0:T(8,128)S(1)}, u32[]{:S(2)}) copy-start(f32[128,128]{1,0:T(8,128)S(1)} %get-tuple-element.38.ks_ref) | copy-start | bytes 196612
  45.4 11.6 %copy-start.35 = (f32[128,128]{1,0:T(8,128)}, f32[128,128]{1,0:T(8,128)S(1)}, u32[]{:S(2)}) copy-start(f32[128,128]{1,0:T(8,128)S(1)} %get-tuple-element.40.cs_ref) | copy-start | bytes 196612
  57.7 35.8 %all-to-all-start.2 = ((f32[32,1,512]{2,1,0:T(1,128)}), f32[32,1,512]{2,1,0:T(1,128)}, u32[]{:S(2)}, u32[]{:S(2)}) async-start(f32[32,1,512]{2,1,0:T(1,128)} %copy.20), calls=%async_computation.2 | async-start | bytes 131072 | tf_op jit(solution)/shard_map/all_to_all | solution.py:473
  70.4 24.0 %copy-start.1 = (f32[2,3,6,96,128]{4,3,2,1,0:T(8,128)S(1)}, f32[2,3,6,96,128]{4,3,2,1,0:T(8,128)}, u32[]{:S(2)}) copy-start(f32[2,3,6,96,128]{4,3,2,1,0:T(8,128)} %str_prev_ref.5) | copy-start | bytes 5308420
  103.1 24.1 %copy-start.9 = (s32[6,128,128]{2,1,0:T(8,128)S(1)}, s32[6,128,128]{2,1,0:T(8,128)}, u32[]{:S(2)}) copy-start(s32[6,128,128]{2,1,0:T(8,128)} %mat_ref.7) | copy-start | bytes 1179652
  103.1 24.1 %copy-start.12 = (f32[2,3,5,96,128]{4,3,2,1,0:T(8,128)S(1)}, f32[2,3,5,96,128]{4,3,2,1,0:T(8,128)}, u32[]{:S(2)}) copy-start(f32[2,3,5,96,128]{4,3,2,1,0:T(8,128)} %get-tuple-element.34.str_ref) | copy-start | bytes 4423684
  103.1 24.1 %copy-start.14 = (f32[3,5,128,128]{3,2,1,0:T(8,128)S(1)}, f32[3,5,128,128]{3,2,1,0:T(8,128)}, u32[]{:S(2)}) copy-start(f32[3,5,128,128]{3,2,1,0:T(8,128)} %copy-done.13) | copy-start | bytes 2949124
  103.1 24.1 %copy-start.17 = (f32[128,128]{1,0:T(8,128)S(1)}, f32[128,128]{1,0:T(8,128)}, u32[]{:S(2)}) copy-start(f32[128,128]{1,0:T(8,128)} %copy-done.15) | copy-start | bytes 196612
  103.1 24.1 %copy-start.20 = (f32[128,128]{1,0:T(8,128)S(1)}, f32[128,128]{1,0:T(8,128)}, u32[]{:S(2)}) copy-start(f32[128,128]{1,0:T(8,128)} %copy-done.18) | copy-start | bytes 196612
  103.1 24.1 %copy-start.23 = (f32[120,128]{1,0:T(8,128)S(1)}, f32[120,128]{1,0:T(8,128)}, u32[]{:S(2)}) copy-start(f32[120,128]{1,0:T(8,128)} %copy-done.21) | copy-start | bytes 184324
  103.1 24.1 %copy-start.48 = (f32[8]{0:T(128)S(1)}, f32[8]{0:T(128)}, u32[]{:S(2)}) copy-start(f32[8]{0:T(128)} %stiff_ref.7) | copy-start | bytes 100
  103.1 24.1 %copy-start.52 = (f32[8]{0:T(128)S(1)}, f32[8]{0:T(128)}, u32[]{:S(2)}) copy-start(f32[8]{0:T(128)} %coef_ref.7) | copy-start | bytes 100
  107.0 20.2 %collective-permute-start.6 = (f32[128,128]{1,0:T(8,128)S(1)}, f32[128,128]{1,0:T(8,128)S(1)}, u32[]{:S(2)}, u32[]{:S(2)}) collective-permute-start(f32[128,128]{1,0:T(8,128)S(1)} %get-tuple-element.50), channel_id=1, source_target_pairs={{0,1},{1,2},{2,3},{3,4},{4,5},{5,6},{6,7},{7,8},{8,9},{9,10},{10,1... | collective-permute-start | bytes 196616 | tf_op jit(solution)/shard_map/ppermute | solution.py:219
  109.1 18.1 %collective-permute-start.7 = (f32[128,128]{1,0:T(8,128)S(1)}, f32[128,128]{1,0:T(8,128)S(1)}, u32[]{:S(2)}, u32[]{:S(2)}) collective-permute-start(f32[128,128]{1,0:T(8,128)S(1)} %get-tuple-element.51), channel_id=1, source_target_pairs={{1,0},{2,1},{3,2},{4,3},{5,4},{6,5},{7,6},{8,7},{9,8},{10,9},{11,1... | collective-permute-start | bytes 196616 | tf_op jit(solution)/shard_map/ppermute | solution.py:220
  114.7 7.1 %collective-permute-start.4 = (f32[120,128]{1,0:T(8,128)S(1)}, f32[120,128]{1,0:T(8,128)S(1)}, u32[]{:S(2)}, u32[]{:S(2)}) collective-permute-start(f32[120,128]{1,0:T(8,128)S(1)} %get-tuple-element.48), channel_id=1, source_target_pairs={{0,32},{32,64},{64,96},{96,128},{128,160},{160,192},{192,224},{1,3... | collective-permute-start | bytes 184328 | tf_op jit(solution)/shard_map/ppermute | solution.py:217
  119.8 7.3 %collective-permute-start.5 = (f32[120,128]{1,0:T(8,128)S(1)}, f32[120,128]{1,0:T(8,128)S(1)}, u32[]{:S(2)}, u32[]{:S(2)}) collective-permute-start(f32[120,128]{1,0:T(8,128)S(1)} %get-tuple-element.49), channel_id=1, source_target_pairs={{32,0},{64,32},{96,64},{128,96},{160,128},{192,160},{224,192},{33,... | collective-permute-start | bytes 184328 | tf_op jit(solution)/shard_map/ppermute | solution.py:218
  (35 other events, 44.1 us)

commit v2 on v1

v2 whole, which is shorter than its diff:
```python
import jax
import jax.numpy as jnp
from jax import lax
from jax.experimental import pallas as pl
from jax.experimental.pallas import tpu as pltpu
from jax.sharding import PartitionSpec as P

F32 = jnp.float32
BF16 = jnp.bfloat16
NT = (((1,), (1,)), ((), ()))
TN = (((0,), (0,)), ((), ()))
FIELDS = 7


def iota(shape, dim):
    return lax.broadcasted_iota(jnp.int32, shape, dim)


def two_parts(values):
    high = values.astype(BF16)
    return high, (values - high.astype(F32)).astype(BF16)


def pick(mask, values):
    return jnp.where(mask, values, 0.0).astype(BF16)


def whole(shape):
    return pl.BlockSpec(tuple(shape), lambda i: (0,) * len(shape), pipeline_mode=pl.Buffered(1))


def call(body, outs, ins, name, smem=(), flops=0, nbytes=0, scratch=()):
    specs = [pl.BlockSpec(memory_space=pltpu.SMEM) if i in smem else whole(a.shape) for i, a in enumerate(ins)]
    return pl.pallas_call(
        body,
        grid=(1,),
        out_shape=[jax.ShapeDtypeStruct(s, F32) for s in outs],
        in_specs=specs,
        out_specs=[whole(s) for s in outs],
        scratch_shapes=[pltpu.VMEM(s, F32) for s in scratch],
        compiler_params=pltpu.CompilerParams(vmem_limit_bytes=56 * 1024 * 1024),
        cost_estimate=pl.CostEstimate(flops=flops, bytes_accessed=nbytes, transcendentals=0),
        name=name,
    )(*ins)


def tables(stiff_ref, coef_ref):
    half = [0.5 / jnp.full((1, 128), stiff_ref[m], F32) for m in range(8)]
    return half, [coef_ref[m] for m in range(8)]


def half_of(mat, tabs):
    out = jnp.broadcast_to(tabs[0][0], mat.shape)
    for m in range(1, 8):
        out = jnp.where(mat == m, tabs[0][m], out)
    return out


def half_coef(mat, tabs):
    half = jnp.broadcast_to(tabs[0][0], mat.shape)
    coef = jnp.full(mat.shape, tabs[1][0], F32)
    for m in range(1, 8):
        same = mat == m
        half = jnp.where(same, tabs[0][m], half)
        coef = jnp.where(same, tabs[1][m], coef)
    return half, coef


CHUNK = 32


def joined(before, after):
    lane = iota(before.shape, 1)
    return jnp.where((lane & 1) == 1, pltpu.roll(before, 1, 1), pltpu.roll(after, 127, 1))


def with_columns(columns, cells, field):
    lane = iota(cells.shape, 1)
    return jnp.where((lane >> 1) == field, pltpu.roll(cells, 2 * field + 1, 1), columns)


def row_neighbours(get, r0, total, ends):
    cells = get(r0, CHUNK)
    row = iota(cells.shape, 0)
    if r0 > 0:
        above = get(r0 - 1, CHUNK)
    else:
        above = pltpu.roll(cells, 1, 0)
        if ends is not None:
            above = jnp.where(row == 0, ends[0], above)
    if r0 + CHUNK < total:
        below = get(r0 + 1, CHUNK)
    else:
        below = pltpu.roll(cells, CHUNK - 1, 0)
        if ends is not None:
            below = jnp.where(row == CHUNK - 1, ends[1], below)
    return cells, above, below


def lane_neighbours(cells, edge, field):
    lane = iota(cells.shape, 1)
    turned = pltpu.roll(edge, (127 - 2 * field) % 128, 1)
    before = jnp.where(lane == 0, turned, pltpu.roll(cells, 1, 1))
    after = jnp.where(lane == 127, turned, pltpu.roll(cells, 127, 1))
    return before, after


def safe_bond(half, beside):
    return jnp.where(beside > 0.0, 1.0 / (half + beside), 0.0)


def layer_bonds(get, total, ends, edge, field, down, across, left):
    for r0 in range(0, total, CHUNK):
        half, _, below = row_neighbours(get, r0, total, ends)
        bond = safe_bond(half, below)
        if ends is None and r0 + CHUNK == total:
            bond = jnp.where(iota(half.shape, 0) == CHUNK - 1, 0.0, bond)
        down[8 + r0 : 8 + r0 + CHUNK, :] = bond
        if r0 == 0:
            down[7:8, :] = jnp.zeros((1, 128), F32) if ends is None else safe_bond(half[0:1], ends[0])
        before, after = lane_neighbours(half, edge[r0 : r0 + CHUNK, :], field)
        left[r0 : r0 + CHUNK, :] = safe_bond(half, before)
        across[r0 : r0 + CHUNK, :] = safe_bond(half, after)


def chunk_step(now, prev, total, r0, layer, comps, bonds, edge, fields, ends, extra, put):
    down, across, left, thick, coef = bonds
    sl = pl.ds(r0, CHUNK)
    up = down(layer)[pl.ds(7 + r0, CHUNK), :]
    dn = down(layer)[pl.ds(8 + r0, CHUNK), :]
    ac, al, co = across(layer)[sl, :], left(layer)[sl, :], coef(layer)[sl, :]
    for c in range(comps):
        cells, above, below = row_neighbours(now(c, layer), r0, total, None if ends is None else ends(c))
        before, after = lane_neighbours(cells, edge[sl, :], fields(c))
        pull = dn * (below - cells) + up * (above - cells)
        pull = pull + (ac * (after - cells) + al * (before - cells))
        if layer < 5:
            pull = pull + thick(layer)[sl, :] * (now(c, layer + 1)(r0, CHUNK) - cells)
        if layer > 0:
            pull = pull + thick(layer - 1)[sl, :] * (now(c, layer - 1)(r0, CHUNK) - cells)
        if extra is not None:
            pull = pull + extra(c)
        put(c, 2.0 * cells - prev(c, layer)(r0, CHUNK) + co * pull)


def rows_of(ref, *index):
    view = ref.at[index]
    return lambda lo, n: view[pl.ds(lo, n), :]


def ends_of(before, after, index):
    return before[index : index + 1, :], after[index : index + 1, :]


def prep_body(span_ref, chord_ref, stringer_ref, cell_ref, stiff_ref, owner_ref, out_ref, match_ref):
    def row_of(ref):
        return ref[...].reshape(1, -1)

    span, chord, stringer = row_of(span_ref), row_of(chord_ref), row_of(stringer_ref)
    cell, stiff = row_of(cell_ref), row_of(stiff_ref)
    count = span.shape[1]
    chunks = count // 128
    same = iota((48, count), 0) == stringer
    diagonal = iota((48, 48), 0) == iota((48, 48), 1)
    owner = jnp.sum(jnp.where(diagonal, owner_ref[...], 0).astype(F32), axis=1, keepdims=True).astype(jnp.int32)
    slot = jnp.sum(jnp.where(same, owner, 0).astype(F32), axis=0, keepdims=True).astype(jnp.int32)
    foot = (chord - (((2 * cell) * 171) >> 9)) >> 6
    foot_of = jnp.max(jnp.where(same, foot, 0).astype(F32), axis=1, keepdims=True).astype(jnp.int32)
    slots = iota((48, 64), 1)
    slot_hot = (slots == (owner & 1) * 32 + (owner >> 1)).astype(F32).astype(BF16)
    foot_hot = (slots == (foot_of & 1) * 32 + (foot_of >> 1)).astype(F32).astype(BF16)
    match_ref[0:64, 0:64] = lax.dot_general(foot_hot, slot_hot, TN, preferred_element_type=F32)
    match_ref[64:128, 0:64] = lax.dot_general(slot_hot, foot_hot, TN, preferred_element_type=F32)
    one = same.astype(F32)
    lower = (iota((128, 128), 0) < iota((128, 128), 1)).astype(F32).astype(BF16)
    both = jnp.concatenate([lower, jnp.ones((128, 128), BF16)], axis=1)
    offset = jnp.zeros((48, 128), F32)
    ranks = []
    for k in range(chunks):
        part = one[:, k * 128 : (k + 1) * 128]
        ahead = jnp.dot(part.astype(BF16), both, preferred_element_type=F32)
        ranks.append(jnp.sum(part * (ahead[:, :128] + offset), axis=0, keepdims=True))
        offset = offset + ahead[:, 128:]
    rank = jnp.concatenate(ranks, axis=1).astype(jnp.int32)
    place = iota((128, count), 0)
    place = place == jnp.where(
        place < 64, (slot & 1) * 32 + (slot >> 1), 64 + (foot & 1) * 32 + (foot >> 1)
    )
    place = place.astype(F32).astype(BF16)
    order = iota((16, count), 0) == rank
    high = stiff.astype(BF16).astype(F32)
    rest = stiff - high
    middle = rest.astype(BF16).astype(F32)
    fields = [cell.astype(F32), (span & 127).astype(F32), (chord & 127).astype(F32), high, middle, rest - middle]
    rows = jnp.concatenate([pick(order, f) for f in fields], axis=0)
    got = lax.dot_general(place, rows, NT, preferred_element_type=F32)
    for side in range(2):
        index, weight = [], []
        for p in range(2):
            part = got[side * 64 + p * 32 : side * 64 + p * 32 + 32]
            where_, across = part[:, 0:16], part[:, 16:32]
            if side == 1:
                where_, across = part[:, 16:32], part[:, 32:48]
            index.append(where_ * 128.0 + across)
            weight.append(part[:, 48:64] + part[:, 64:80] + part[:, 80:96])
        out_ref[:, side * 64 : side * 64 + 64] = jnp.concatenate(index + weight, axis=1)


def ends_exist():
    span, chord = lax.axis_index("span"), lax.axis_index("chord")
    yes = lambda cond: jnp.where(cond, 1.0, 0.0).astype(F32)
    return (
        yes(span > 0), yes(span < lax.axis_size("span") - 1),
        yes(chord > 0), yes(chord < lax.axis_size("chord") - 1),
    )


def pack_skin(columns, get, layers, r0, first_ref, last_ref):
    for l in layers:
        for c in range(3):
            f = c * 6 + l
            cells = get(c, l)
            columns = with_columns(columns, cells, f)
            if r0 == 0:
                first_ref[f : f + 1, :] = cells[0:1]
            if r0 == 128 - CHUNK:
                last_ref[f : f + 1, :] = cells[CHUNK - 1 : CHUNK]
    return columns


def pack_str(columns, get, layers):
    for p in range(2):
        for t in layers:
            for c in range(3):
                columns = with_columns(columns, get(p, c, t), (p * 3 + c) * 6 + t)
    return columns


def halo_body(stiff_ref, coef_ref, skin_ref, mat_ref, str_ref, smat_ref, after_ref, last_ref, first_ref, side_ref):
    tabs = tables(stiff_ref, coef_ref)
    at_prev, at_next, at_left, at_right = ends_exist()
    lane = iota((CHUNK, 128), 1)
    side_keep = jnp.where((lane & 1) == 0, at_right, at_left)
    span_keep = jnp.where((lane & 1) == 0, at_next, at_prev)
    for r0 in range(0, 128, CHUNK):
        columns = jnp.zeros((CHUNK, 128), F32)
        for l in range(6):
            half = half_of(mat_ref[l, pl.ds(r0, CHUNK), :], tabs)
            columns = with_columns(columns, half, 18 + l)
            if r0 == 0:
                first_ref[18 + l : 19 + l, :] = half[0:1] * at_prev
            if r0 == 128 - CHUNK:
                last_ref[18 + l : 19 + l, :] = half[CHUNK - 1 : CHUNK] * at_next
        columns = columns * side_keep
        side_ref[pl.ds(r0, CHUNK), :] = pack_skin(
            columns, lambda c, l: skin_ref[c, l, pl.ds(r0, CHUNK), :], range(6), r0, first_ref, last_ref
        )
    for r0 in range(0, 96, CHUNK):
        columns = jnp.zeros((CHUNK, 128), F32)
        for p in range(2):
            for t in range(6):
                half = half_of(smat_ref[p, t, pl.ds(r0, CHUNK), :], tabs)
                columns = with_columns(columns, half, 36 + p * 6 + t)
        columns = columns * span_keep
        columns = pack_str(columns, lambda p, c, t: str_ref[p, c, t, pl.ds(r0, CHUNK), :], range(6))
        last_ref[pl.ds(24 + r0, CHUNK), :] = columns
        first_ref[pl.ds(24 + r0, CHUNK), :] = columns


def exchange(last, first, side):
    def ring(axis):
        count = lax.axis_size(axis)
        return [(i, (i + 1) % count) for i in range(count)]

    back = lambda pairs: [(b, a) for a, b in pairs]
    before = lax.ppermute(last, "span", ring("span"))
    after = lax.ppermute(first, "span", back(ring("span")))
    lefts = lax.ppermute(side, "chord", ring("chord"))
    rights = lax.ppermute(side, "chord", back(ring("chord")))
    return before, after, lefts, rights


def row_lists(index):
    return jnp.concatenate([index[q * 8 : q * 8 + 8, :] for q in range(4)], axis=1)


def one_row(values):
    return jnp.concatenate([values[a : a + 1, :] for a in range(8)], axis=1)


def hots(rows_ref):
    text = one_row(row_lists(rows_ref[:, 0:32])).astype(jnp.int32)
    tk = one_row(row_lists(rows_ref[:, 32:64]))
    sext = one_row(row_lists(rows_ref[:, 64:96])).astype(jnp.int32)
    sk = one_row(row_lists(rows_ref[:, 96:128]))
    slot = ((iota((1, 1024), 1) >> 4) & 1) * 128
    t_row = iota((96, 1024), 0) == (text >> 7)
    t_lane = (iota((256, 1024), 0) == (text & 127) + slot).astype(F32).astype(BF16)
    s_row = iota((128, 1024), 0) == (sext >> 7)
    s_lane = (iota((128, 1024), 0) == (sext & 127)).astype(F32).astype(BF16)
    return (t_row, t_lane, tk), (s_row, s_lane, sk)


def spread(row_mask, lane_hot, values):
    high, low = two_parts(values)
    left = jnp.concatenate([pick(row_mask, high.astype(F32)), pick(row_mask, low.astype(F32))], axis=1)
    right = jnp.concatenate([lane_hot, lane_hot], axis=1)
    return lax.dot_general(left, right, NT, preferred_element_type=F32)


def fetch(row_mask, lane_hot2, cells):
    high, low = two_parts(cells)
    wide = jnp.dot(jnp.concatenate([high, low], axis=1), lane_hot2, preferred_element_type=F32)
    return jnp.sum(jnp.where(row_mask, wide, 0.0), axis=0, keepdims=True)


def as_lanes(row):
    return jnp.concatenate([row[:, a * 128 : (a + 1) * 128] for a in range(8)], axis=0)


def gather_body(
    stiff_ref, coef_ref, rows_ref, skin_ref, skin_prev_ref, mat_ref, str_ref, str_prev_ref, smat_ref,
    before_ref, after_ref, lefts_ref, rights_ref,
    out_ref, ks_ref, ps_ref, cs_ref, kt_ref, pt_ref, ct_ref,
    half_ref, down_ref, across_ref, left_ref, thick_ref, edge_ref, tedge_ref, co_ref,
):
    tabs = tables(stiff_ref, coef_ref)
    (t_row, t_lane, tk), (s_row, s_lane, sk) = hots(rows_ref)
    ks_ref[...] = spread(s_row, s_lane, sk)
    kt_ref[...] = spread(t_row, t_lane, tk)
    edge_ref[...] = joined(lefts_ref[...], rights_ref[...])
    tedge_ref[...] = joined(before_ref[24:120, :], after_ref[24:120, :])
    bonds = (lambda l: down_ref, lambda l: across_ref, lambda l: left_ref, lambda l: thick_ref, lambda l: co_ref)

    def prepare(total, own, other, ends, edge, field):
        for r0 in range(0, total, CHUNK):
            sl = pl.ds(r0, CHUNK)
            half, coef = half_coef(own[sl, :], tabs)
            half_ref[sl, :] = half
            co_ref[sl, :] = coef
            thick_ref[sl, :] = 1.0 / (half + half_of(other[sl, :], tabs))
        layer_bonds(lambda lo, n: half_ref[pl.ds(lo, n), :], total, ends, edge, field, down_ref, across_ref, left_ref)

    prepare(128, mat_ref.at[5], mat_ref.at[4], ends_of(before_ref, after_ref, 23), edge_ref, 23)
    cs_ref[...] = co_ref[...]
    for r0 in range(0, 128, CHUNK):
        sl = pl.ds(r0, CHUNK)

        def put(c, value):
            ps_ref[c, sl, :] = value - cs_ref[sl, :] * ks_ref[sl, :] * skin_ref[c, 5, sl, :]

        chunk_step(
            lambda c, l: rows_of(skin_ref, c, l), lambda c, l: rows_of(skin_prev_ref, c, l), 128, r0, 5, 3, bonds,
            edge_ref, lambda c: c * 6 + 5, lambda c: ends_of(before_ref, after_ref, c * 6 + 5), None, put,
        )
    for p in range(2):
        prepare(96, smat_ref.at[p, 0], smat_ref.at[p, 1], None, tedge_ref, 36 + p * 6)
        lanes = pl.ds(p * 128, 128)
        ct_ref[:, p * 128 : p * 128 + 128] = co_ref[0:96, :]
        for r0 in range(0, 96, CHUNK):
            sl = pl.ds(r0, CHUNK)

            def put(c, value):
                pt_ref[c, sl, lanes] = value - ct_ref[sl, lanes] * kt_ref[sl, lanes] * str_ref[p, c, 0, sl, :]

            chunk_step(
                lambda c, l: rows_of(str_ref, p, c, l), lambda c, l: rows_of(str_prev_ref, p, c, l), 96, r0, 0, 3, bonds,
                tedge_ref, lambda c: (p * 3 + c) * 6, None, None, put,
            )
    t_fields = [jnp.concatenate([str_ref[0, c, 0], str_ref[1, c, 0]], axis=1) for c in range(3)]
    t_fields += [pt_ref[c] for c in range(3)] + [ct_ref[...] * kt_ref[...]]
    s_fields = [skin_ref[c, 5] for c in range(3)] + [ps_ref[c] for c in range(3)] + [cs_ref[...]]
    t_two = jnp.concatenate([t_lane, t_lane], axis=0)
    s_two = jnp.concatenate([s_lane, s_lane], axis=0)
    got = [as_lanes(fetch(t_row, t_two, f)) for f in t_fields]
    got += [as_lanes(fetch(s_row, s_two, f)) for f in s_fields]
    pad = jnp.zeros((8, 128), F32)
    got += [pad, pad]
    for j in range(4):
        part = [
            jnp.concatenate([g[:, q * 32 : q * 32 + 32] for g in got[4 * j : 4 * j + 4]], axis=1) for q in range(4)
        ]
        out_ref[pl.ds(j, 32, stride=4), :] = jnp.concatenate(part, axis=0)


def bounce_body(match_ref, got_ref, after_ref, out_ref):
    got = jnp.concatenate([got_ref[pl.ds(j, 32, stride=4), :] for j in range(4)], axis=1)
    lane = iota(got.shape, 1)
    zero = (lane & 16) == 0

    def turned(base):
        def part(to, frm):
            m = match_ref[base + to * 32 : base + to * 32 + 32, frm * 32 : frm * 32 + 32]
            return jnp.dot(m, got, preferred_element_type=F32, precision=lax.Precision.HIGHEST)

        a = part(0, 0) + pltpu.roll(part(0, 1), 512 - 16, 1)
        b = part(1, 1) + pltpu.roll(part(1, 0), 16, 1)
        return jnp.where(zero, a, b)

    new = jnp.where(lane < FIELDS * 32, turned(0), turned(64))
    for j in range(4):
        out_ref[pl.ds(j, 32, stride=4), :] = new[:, j * 128 : j * 128 + 128]


def load_body(
    rows_ref, posted_ref, ks_ref, ps_ref, cs_ref, kt_ref, pt_ref, ct_ref, skin_ref, str_ref,
    last_in, first_in, side_in,
    skin1_ref, sload_ref, str1_ref, tload_ref, last_ref, first_ref, side_ref,
):
    (t_row, t_lane, tk), (s_row, s_lane, sk) = hots(rows_ref)
    posted = [posted_ref[pl.ds(j, 32, stride=4), :] for j in range(4)]

    def sums(side, row_mask, lane_hot, weight, f):
        g = side * FIELDS + f
        at = g % 4 * 32
        return spread(row_mask, lane_hot, weight * one_row(row_lists(posted[g // 4][:, at : at + 32])))

    last_ref[...] = last_in[...]
    first_ref[...] = first_in[...]
    side = side_in[...]
    ks, cs = ks_ref[...], cs_ref[...]
    qs = sums(0, s_row, s_lane, sk, 6)
    for c in range(3):
        now = skin_ref[c, 5]
        new = ps_ref[c] + cs * sums(0, s_row, s_lane, sk, c)
        skin1_ref[c] = new
        sload_ref[c] = sums(0, s_row, s_lane, sk, 3 + c) + qs * now - ks * new
        f = c * 6 + 5
        last_ref[f : f + 1, :] = new[127:128, :]
        first_ref[f : f + 1, :] = new[0:1, :]
        side = with_columns(side, new, f)
    side_ref[...] = side
    kt, ct = kt_ref[...], ct_ref[...]
    qt = sums(1, t_row, t_lane, tk, 6)
    third = iota((96, 256), 0) % 3
    columns = last_in[24:120, :]
    for c in range(3):
        now = jnp.concatenate([str_ref[0, c, 0], str_ref[1, c, 0]], axis=1)
        own = kt * now
        pair = jnp.where(third == 0, pltpu.roll(own, 95, 0), jnp.where(third == 1, pltpu.roll(own, 1, 0), 0.0))
        new = pt_ref[c] + ct * sums(1, t_row, t_lane, tk, c)
        load = sums(1, t_row, t_lane, tk, 3 + c) + qt * (own + pair) - kt * new
        for p in range(2):
            str1_ref[p, c] = new[:, p * 128 : p * 128 + 128]
            tload_ref[p, c] = load[:, p * 128 : p * 128 + 128]
            columns = with_columns(columns, new[:, p * 128 : p * 128 + 128], (p * 3 + c) * 6)
    last_ref[24:120, :] = columns
    first_ref[24:120, :] = columns


def bonds_body(
    stiff_ref, coef_ref, mat_ref, smat_ref, before_ref, after_ref, lefts_ref, rights_ref, later_ref,
    sd_ref, sa_ref, sl_ref, st_ref, sc_ref, td_ref, ta_ref, tl_ref, tt_ref, tc_ref,
    token_ref, sh_ref, th_ref, edge_ref, tedge_ref,
):
    token_ref[...] = jnp.zeros((8, 128), F32)
    tabs = tables(stiff_ref, coef_ref)
    edge_ref[...] = joined(lefts_ref[...], rights_ref[...])
    tedge_ref[...] = joined(before_ref[24:120, :], after_ref[24:120, :])
    for r0 in range(0, 128, CHUNK):
        sl = pl.ds(r0, CHUNK)
        for l in range(6):
            half, coef = half_coef(mat_ref[l, sl, :], tabs)
            if l > 0:
                st_ref[l - 1, sl, :] = 1.0 / (half + sh_ref[l - 1, sl, :])
            sh_ref[l, sl, :] = half
            sc_ref[l, sl, :] = coef
    for l in range(6):
        layer_bonds(
            rows_of(sh_ref, l), 128, ends_of(before_ref, after_ref, 18 + l), edge_ref, 18 + l,
            sd_ref.at[l], sa_ref.at[l], sl_ref.at[l],
        )
    for p in range(2):
        for r0 in range(0, 96, CHUNK):
            sl = pl.ds(r0, CHUNK)
            for t in range(6):
                half, coef = half_coef(smat_ref[p, t, sl, :], tabs)
                if t > 0:
                    tt_ref[p, t - 1, sl, :] = 1.0 / (half + th_ref[t - 1, sl, :])
                th_ref[t, sl, :] = half
                tc_ref[p, t, sl, :] = coef
        for t in range(6):
            layer_bonds(
                rows_of(th_ref, t), 96, None, tedge_ref, 36 + p * 6 + t, td_ref.at[p, t], ta_ref.at[p, t], tl_ref.at[p, t]
            )


def skin_chunks(now, prev, bonds, edge_ref, before_ref, after_ref, layers, extra, put):
    for r0 in range(0, 128, CHUNK):
        for l in layers:
            chunk_step(
                now, prev, 128, r0, l, 3, bonds, edge_ref, lambda c: c * 6 + l,
                lambda c: ends_of(before_ref, after_ref, c * 6 + l),
                (lambda c: extra(c, r0)) if l == 5 and extra is not None else None, lambda c, v: put(c, l, r0, v),
            )


def str_chunks(now, prev, bonds, edge_ref, layers, extra, put):
    for r0 in range(0, 96, CHUNK):
        for p in range(2):
            for t in layers:
                chunk_step(
                    lambda c, m: now(p, c, m), lambda c, m: prev(p, c, m), 96, r0, t, 3, bonds(p), edge_ref,
                    lambda c: (p * 3 + c) * 6 + t, None,
                    (lambda c: extra(p, c, r0)) if t == 0 and extra is not None else None,
                    lambda c, v: put(p, c, t, r0, v),
                )


def at_layers(*refs):
    return tuple((lambda l, ref=ref: ref.at[l]) for ref in refs)


def first_body(
    skin_ref, skin_prev_ref, str_ref, str_prev_ref, before_ref, after_ref, lefts_ref, rights_ref,
    sd_ref, sa_ref, sl_ref, st_ref, sc_ref, td_ref, ta_ref, tl_ref, tt_ref, tc_ref, later_ref,
    skin1_ref, str1_ref, last_ref, first_ref, side_ref,
    edge_ref, tedge_ref,
):
    edge_ref[...] = joined(lefts_ref[...], rights_ref[...])
    tedge_ref[...] = joined(before_ref[24:120, :], after_ref[24:120, :])
    last_ref[0:24, :] = jnp.zeros((24, 128), F32)
    first_ref[0:24, :] = jnp.zeros((24, 128), F32)

    def put_skin(c, l, r0, value):
        skin1_ref[c, l, pl.ds(r0, CHUNK), :] = value

    def put_str(p, c, t, r0, value):
        str1_ref[p, c, t - 1, pl.ds(r0, CHUNK), :] = value

    skin_chunks(
        lambda c, l: rows_of(skin_ref, c, l), lambda c, l: rows_of(skin_prev_ref, c, l),
        at_layers(sd_ref, sa_ref, sl_ref, st_ref, sc_ref), edge_ref, before_ref, after_ref, range(5), None, put_skin,
    )
    str_chunks(
        lambda p, c, t: rows_of(str_ref, p, c, t), lambda p, c, t: rows_of(str_prev_ref, p, c, t),
        lambda p: at_layers(*(r.at[p] for r in (td_ref, ta_ref, tl_ref, tt_ref, tc_ref))), tedge_ref, range(1, 6), None,
        put_str,
    )
    for r0 in range(0, 128, CHUNK):
        side_ref[pl.ds(r0, CHUNK), :] = pack_skin(
            jnp.zeros((CHUNK, 128), F32), lambda c, l: skin1_ref[c, l, pl.ds(r0, CHUNK), :], range(5), r0, first_ref, last_ref
        )
    for r0 in range(0, 96, CHUNK):
        columns = pack_str(
            jnp.zeros((CHUNK, 128), F32), lambda p, c, t: str1_ref[p, c, t - 1, pl.ds(r0, CHUNK), :], range(1, 6)
        )
        last_ref[pl.ds(24 + r0, CHUNK), :] = columns
        first_ref[pl.ds(24 + r0, CHUNK), :] = columns


def second_body(
    skin_ref, skin_prev_ref, str_ref, str_prev_ref, before_ref, after_ref, lefts_ref, rights_ref,
    sd_ref, sa_ref, sl_ref, st_ref, sc_ref, td_ref, ta_ref, tl_ref, tt_ref, tc_ref,
    skin_face_ref, str_face_ref, sload_ref, tload_ref, skin2_ref, str2_ref,
    edge_ref, tedge_ref,
):
    edge_ref[...] = joined(lefts_ref[...], rights_ref[...])
    tedge_ref[...] = joined(before_ref[24:120, :], after_ref[24:120, :])

    def put_skin(c, l, r0, value):
        skin2_ref[c, l, pl.ds(r0, CHUNK), :] = value

    def put_str(p, c, t, r0, value):
        str2_ref[p, c, t, pl.ds(r0, CHUNK), :] = value

    skin_chunks(
        lambda c, l: rows_of(skin_face_ref, c) if l == 5 else rows_of(skin_ref, c, l),
        lambda c, l: rows_of(skin_prev_ref, c, l),
        at_layers(sd_ref, sa_ref, sl_ref, st_ref, sc_ref), edge_ref, before_ref, after_ref, range(6),
        lambda c, r0: sload_ref[c, pl.ds(r0, CHUNK), :], put_skin,
    )
    str_chunks(
        lambda p, c, t: rows_of(str_face_ref, p, c) if t == 0 else rows_of(str_ref, p, c, t - 1),
        lambda p, c, t: rows_of(str_prev_ref, p, c, t),
        lambda p: at_layers(*(r.at[p] for r in (td_ref, ta_ref, tl_ref, tt_ref, tc_ref))), tedge_ref, range(6),
        lambda p, c, r0: tload_ref[p, c, pl.ds(r0, CHUNK), :], put_str,
    )


def swap(values):
    peers = lax.axis_size("chord")
    moved = lax.all_to_all(values.reshape(peers, -1, 128), "chord", split_axis=0, concat_axis=0, tiled=True)
    return moved.reshape(values.shape)


def shards(
    skin_now, skin_prev, skin_mat, stringer_now, stringer_prev, stringer_mat, owner_slot,
    rivet_span, rivet_chord, rivet_stringer, rivet_cell, rivet_stiff, mat_stiff, mat_coef,
):
    rivets = [rivet_span, rivet_chord, rivet_stringer, rivet_cell, rivet_stiff]
    sent, match = call(prep_body, [(32, 128), (128, 128)], rivets + [owner_slot.reshape(1, -1)], "prep")
    rows = swap(sent)
    mats = [mat_stiff, mat_coef]
    column = [(120, 128), (120, 128), (128, 128)]
    packs = call(
        halo_body, column, [*mats, skin_now, skin_mat, stringer_now, stringer_mat, match], "halo", smem=(0, 1),
        flops=4000000, nbytes=4000000,
    )
    halos = exchange(*packs)
    edges = [(128, 128), (96, 128)]
    found, *kept = call(
        gather_body, [(128, 128), (128, 128), (3, 128, 128), (128, 128), (96, 256), (3, 96, 256), (96, 256)],
        [*mats, rows, skin_now, skin_prev, skin_mat, stringer_now, stringer_prev, stringer_mat, *halos], "gather",
        smem=(0, 1), flops=1000000000, nbytes=2000000,
        scratch=[(128, 128), (136, 128), (128, 128), (128, 128), (128, 128), *edges, (128, 128)],
    )
    given = swap(found)
    bonds = call(
        bonds_body,
        [(6, 136, 128), *[(6, 128, 128)] * 4, (2, 6, 104, 128), *[(2, 6, 96, 128)] * 4, (8, 128)],
        [*mats, skin_mat, stringer_mat, *halos, found], "bonds", smem=(0, 1), flops=10000000, nbytes=8000000,
        scratch=[(6, 128, 128), (6, 96, 128), *edges],
    )
    (turned,) = call(bounce_body, [(128, 128)], [match, given, bonds[-1]], "bounce")
    posted = swap(turned)
    skin1, str1, *packs1 = call(
        first_body, [(3, 5, 128, 128), (2, 3, 5, 96, 128), *column],
        [skin_now, skin_prev, stringer_now, stringer_prev, *halos, *bonds[:-1], turned], "first",
        flops=20000000, nbytes=10000000, scratch=edges,
    )
    skin_face, sload, str_face, tload, *packs2 = call(
        load_body, [(3, 128, 128), (3, 128, 128), (2, 3, 96, 128), (2, 3, 96, 128), *column],
        [rows, posted, *kept, skin_now, stringer_now, *packs1], "load", flops=1000000000, nbytes=2000000,
    )
    halos1 = exchange(*packs2)
    return call(
        second_body, [(3, 6, 128, 128), (2, 3, 6, 96, 128)],
        [skin1, skin_now, str1, stringer_now, *halos1, *bonds[:-1], skin_face, str_face, sload, tload], "second",
        flops=20000000, nbytes=10000000, scratch=edges,
    )


def solution(mesh):
    placed = (
        P(None, None, "span", "chord"),
        P(None, None, "span", "chord"),
        P(None, "span", "chord"),
        P("chord", None, None, None, "span"),
        P("chord", None, None, None, "span"),
        P("chord", None, None, "span"),
        P(),
        P(("span", "chord")),
        P(("span", "chord")),
        P(("span", "chord")),
        P(("span", "chord")),
        P(("span", "chord")),
        P(),
        P(),
    )
    body = jax.shard_map(
        shards,
        mesh=mesh,
        in_specs=placed,
        out_specs=(P(None, None, "span", "chord"), P("chord", None, None, None, "span")),
        check_vma=False,
    )
    return lambda *args: tuple(body(*args))
```

time: 147 us -> 93.4 us (0.64)
  the two profiles are of different devices: /device:TPU:102 before, /device:TPU:96 now
where the time goes in v2:
time: 93.4 us; the launch traced here: 93 us
  Pallas kernels  43.5 us (47%)
  starting transfers between devices  24.2 us (26%)
  blocking collectives  13.6 us (15%)
  waiting for transfers between devices  8.43 us (9%)
  local copies, waits for them, and re-layouts  2.61 us (3%)
    pallas_call x8, Pallas kernels, call(): pl.pallas_call(body, grid=(1,), out_shape=[jax.ShapeDtypeStruct(s, F32) f...  43.5 us
    all_to_all x1, blocking collectives, swap(): lax.all_to_all(values.reshape(peers, -1, 128), 'chord', split_axis=0, con...  13.6 us
    ppermute x2, starting transfers between devices, exchange(): rights = lax.ppermute(side, 'chord', back(ring('chord')))  9.43 us
    all_to_all x2, starting transfers between devices, swap(): lax.all_to_all(values.reshape(peers, -1, 128), 'chord', split_axis=0, con...  8.66 us
    ppermute x2, starting transfers between devices, exchange(): before = lax.ppermute(last, 'span', ring('span'))  6.08 us
    ppermute x2, waiting for transfers between devices, exchange(): after = lax.ppermute(first, 'span', back(ring('span')))  3.46 us
    all_to_all x2, waiting for transfers between devices, swap(): lax.all_to_all(values.reshape(peers, -1, 128), 'chord', split_axis=0, con...  2.78 us
    unnamed x22, local copies, waits for them, and re-layouts  2.61 us
  transfers between devices with their start and end apart: 10, of which 3 were waited for; matrix products, arithmetic and copies ran while one was open for 0% of the time, Pallas kernels for 14%

profile of v2, /device:TPU:96, one launch (start us, length us, event | category | flops | bytes accessed | tf_op | source)
XLA Modules:
  0.0 93.0 jit_solution(381890403619250660)
XLA Ops:
  0.6 2.1 %prep.1 = (f32[32,128]{1,0:T(8,128)}, f32[128,128]{1,0:T(8,128)}) custom-call(s32[768]{0:T(1024)} %span_ref.1, s32[768]{0:T(1024)} %chord_ref.1, s32[768]{0:T(1024)} %stringer_ref.1, s32[768]{0:T(1024)} %cell_ref.1, f32[768]{0:T(1024)} %stiff_ref.4, s32[1,48]{1,0:T(1,128)} %bitcast.16), custom_call_target="tpu_custom_call" | custom-call | tf_op jit(solution)/shard_map/prep/pallas_call | solution.py:34
  2.8 4.2 %halo.1 = (f32[120,128]{1,0:T(8,128)}, f32[120,128]{1,0:T(8,128)}, f32[128,128]{1,0:T(8,128)}) custom-call(f32[8]{0:T(128)} %stiff_ref.7, f32[8]{0:T(128)} %coef_ref.5, f32[3,6,128,128]{3,2,1,0:T(8,128)} %skin_prev_ref.5, s32[6,128,128]{2,1,0:T(8,128)} %mat_ref.5, f32[2,3,6,96,128]{4,3,2,1,0:T(8,128)} %str_prev_ref.5, s32[2,6,96,128]{3,2,1,0:T(8,128)} %smat_ref.5, ...), custom_call_target="tpu_custom_call" | custom-call | flops 4000000 | bytes 4000000 | tf_op jit(solution)/shard_map/halo/pallas_call | solution.py:34
  6.9 4.6 %collective-permute-start.3 = (f32[128,128]{1,0:T(8,128)}, f32[128,128]{1,0:T(8,128)S(1)}, u32[]{:S(2)}, u32[]{:S(2)}) collective-permute-start(f32[128,128]{1,0:T(8,128)} %get-tuple-element.40), channel_id=1, source_target_pairs={{1,0},{2,1},{3,2},{4,3},{5,4},{6,5},{7,6},{8,7},{9,8},{10,9},{11,1... | collective-permute-start | bytes 196616 | tf_op jit(solution)/shard_map/ppermute | solution.py:279
  11.6 0.0 collective-permute-start.2
  11.6 3.1 %collective-permute-start = (f32[120,128]{1,0:T(8,128)}, f32[120,128]{1,0:T(8,128)S(1)}, u32[]{:S(2)}, u32[]{:S(2)}) collective-permute-start(f32[120,128]{1,0:T(8,128)} %get-tuple-element.38), channel_id=1, source_target_pairs={{0,32},{32,64},{64,96},{96,128},{128,160},{160,192},{192,224},{224... | collective-permute-start | bytes 184328 | tf_op jit(solution)/shard_map/ppermute | solution.py:276
  14.7 0.0 collective-permute-start.1
  14.7 13.6 %all_to_all.15 = f32[32,1,128]{2,1,0:T(1,128)} all-to-all(f32[32,1,128]{2,1,0:T(1,128)S(1)} %bitcast.15), channel_id=1, replica_groups=mesh['span'=8,'chord'=32] {'chord'}, dimensions={0} | all-to-all | bytes 32768 | tf_op jit(solution)/shard_map/all_to_all | solution.py:583
  28.3 0.0 collective-permute-done.before_ref
  28.3 0.0 collective-permute-done.1.after_ref
  28.3 0.0 collective-permute-done.2.lefts_ref
  28.3 0.6 copy-done.2
  28.9 0.0 copy-done.3
  29.0 0.0 copy-done
  29.0 0.0 copy-done.1
  29.0 6.8 %gather.1 = (f32[128,128]{1,0:T(8,128)}, f32[128,128]{1,0:T(8,128)}, f32[3,128,128]{2,1,0:T(8,128)}, f32[128,128]{1,0:T(8,128)}, f32[96,256]{1,0:T(8,128)}, /*index=5*/f32[3,96,256]{2,1,0:T(8,128)}, f32[96,256]{1,0:T(8,128)}) custom-call(f32[8]{0:T(128)} %stiff_ref.7, f32[8]{0:T(128)} %coef_ref.5, f32[32,128]{1,0:T(8,128)} %bitcast.13, ...), custom_call_target="tpu_custom_call" | custom-call | flops 1000000000 | bytes 2000000 | tf_op jit(solution)/shard_map/gather/pallas_call | solution.py:34
  35.8 3.9 %all-to-all-start.1 = ((f32[32,4,128]{2,1,0:T(4,128)}), f32[32,4,128]{2,1,0:T(4,128)S(1)}, u32[]{:S(2)}, u32[]{:S(2)}) async-start(f32[32,4,128]{2,1,0:T(4,128)} %bitcast.11), calls=%async_computation.1 | async-start | bytes 131072 | tf_op jit(solution)/shard_map/all_to_all | solution.py:583
  39.7 4.7 %bonds.1 = (f32[6,136,128]{2,1,0:T(8,128)}, f32[6,128,128]{2,1,0:T(8,128)}, f32[6,128,128]{2,1,0:T(8,128)}, f32[6,128,128]{2,1,0:T(8,128)}, f32[6,128,128]{2,1,0...) custom-call(f32[8]{0:T(128)} %stiff_ref.7, ...), custom_call_target="tpu_custom_call" | custom-call | flops 10000000 | bytes 8000000 | tf_op jit(solution)/shard_map/bonds/pallas_call | solution.py:34
  44.4 2.8 %all-to-all-done.1 = f32[32,4,128]{2,1,0:T(4,128)S(1)} async-done(((f32[32,4,128]{2,1,0:T(4,128)}), f32[32,4,128]{2,1,0:T(4,128)S(1)}, u32[]{:S(2)}, u32[]{:S(2)}) %all-to-all-start.1) | async-done | bytes 65568 | tf_op jit(solution)/shard_map/all_to_all | solution.py:583
  47.2 0.7 copy-done.5
  47.8 2.1 %bounce.1.later_ref = f32[128,128]{1,0:T(8,128)} custom-call(f32[128,128]{1,0:T(8,128)} %get-tuple-element.37.after_ref.match_ref, f32[128,128]{1,0:T(8,128)} %bitcast.12, f32[8,128]{1,0:T(8,128)} %get-tuple-element.53.after_ref), custom_call_target="tpu_custom_call" | custom-call | tf_op jit(solution)/shard_map/bounce/pallas_call | solution.py:34
  50.0 4.8 %all-to-all-start.2 = ((f32[32,4,128]{2,1,0:T(4,128)}), f32[32,4,128]{2,1,0:T(4,128)S(1)}, u32[]{:S(2)}, u32[]{:S(2)}) async-start(f32[32,4,128]{2,1,0:T(4,128)} %bitcast.9), calls=%async_computation.2 | async-start | bytes 131072 | tf_op jit(solution)/shard_map/all_to_all | solution.py:583
  54.8 8.6 %first.1 = (f32[3,5,128,128]{3,2,1,0:T(8,128)}, f32[2,3,5,96,128]{4,3,2,1,0:T(8,128)}, f32[120,128]{1,0:T(8,128)}, f32[120,128]{1,0:T(8,128)}, f32[128,128]{1,0:T(8,128)}) custom-call(f32[3,6,128,128]{3,2,1,0:T(8,128)} %skin_prev_ref.5, f32[3,6,128,128]{3,2,1,0:T(8,128)} %skin_prev_ref.4, f32[2,3,6,96,128]{4,3,2,1,0:T(8,128)} %str_prev_ref.5, ...), custom_call_target="tpu_custom_call" | custom-call | flops 20000000 | bytes 10000000 | tf_op jit(solution)/shard_map/first/pallas_call | solution.py:34
  63.4 0.6 copy-done.4
  64.0 6.7 %load.1 = (f32[3,128,128]{2,1,0:T(8,128)}, f32[3,128,128]{2,1,0:T(8,128)}, f32[2,3,96,128]{3,2,1,0:T(8,128)}, f32[2,3,96,128]{3,2,1,0:T(8,128)}, f32[120,128]{1,...) custom-call(f32[32,128]{1,0:T(8,128)} %bitcast.14, f32[128,128]{1,0:T(8,128)} %bitcast.10, ...), custom_call_target="tpu_custom_call" | custom-call | flops 1000000000 | bytes 2000000 | tf_op jit(solution)/shard_map/load/pallas_call | solution.py:34
  70.6 4.8 %collective-permute-start.7 = (f32[128,128]{1,0:T(8,128)}, f32[128,128]{1,0:T(8,128)S(1)}, u32[]{:S(2)}, u32[]{:S(2)}) collective-permute-start(f32[128,128]{1,0:T(8,128)} %get-tuple-element.67), channel_id=1, source_target_pairs={{1,0},{2,1},{3,2},{4,3},{5,4},{6,5},{7,6},{8,7},{9,8},{10,9},{11,1... | collective-permute-start | bytes 196616 | tf_op jit(solution)/shard_map/ppermute | solution.py:279
  75.4 2.9 %collective-permute-start.4 = (f32[120,128]{1,0:T(8,128)}, f32[120,128]{1,0:T(8,128)S(1)}, u32[]{:S(2)}, u32[]{:S(2)}) collective-permute-start(f32[120,128]{1,0:T(8,128)} %get-tuple-element.65), channel_id=1, source_target_pairs={{0,32},{32,64},{64,96},{96,128},{128,160},{160,192},{192,224},{224... | collective-permute-start | bytes 184328 | tf_op jit(solution)/shard_map/ppermute | solution.py:276
  78.4 2.2 %collective-permute-done.4.before_ref = f32[120,128]{1,0:T(8,128)S(1)} collective-permute-done((f32[120,128]{1,0:T(8,128)}, f32[120,128]{1,0:T(8,128)S(1)}, u32[]{:S(2)}, u32[]{:S(2)}) %collective-permute-start.4) | collective-permute-done | bytes 61472 | tf_op jit(solution)/shard_map/ppermute | solution.py:276
  80.6 3.5 %collective-permute-done.5.after_ref = f32[120,128]{1,0:T(8,128)S(1)} collective-permute-done((f32[120,128]{1,0:T(8,128)}, f32[120,128]{1,0:T(8,128)S(1)}, u32[]{:S(2)}, u32[]{:S(2)}) %collective-permute-start.5) | collective-permute-done | bytes 61472 | tf_op jit(solution)/shard_map/ppermute | solution.py:277
  84.0 0.6 copy-done.9
  84.6 0.0 copy-done.6
  84.7 0.0 copy-done.7
  84.7 8.3 %second.1 = (f32[3,6,128,128]{3,2,1,0:T(8,128)}, f32[2,3,6,96,128]{4,3,2,1,0:T(8,128)}) custom-call(f32[3,5,128,128]{3,2,1,0:T(8,128)} %get-tuple-element.54.skin_ref, f32[3,6,128,128]{3,2,1,0:T(8,128)} %skin_prev_ref.5, f32[2,3,5,96,128]{4,3,2,1,0:T(8,128)} %get-tuple-element.55.str_ref, f32[2,3,6,96,128]{4,3,2,1,0:T(8,128)} %str_prev_ref.5, ...), custom_call_target="tpu_custom_call" | custom-call | flops 20000000 | bytes 10000000 | tf_op jit(solution)/shard_map/second/pallas_call | solution.py:34
  (19 shorter events, 0.0 us)
Async XLA Ops:
  2.8 12.0 %copy-start.10 = (f32[32,128]{1,0:T(8,128)S(1)}, f32[32,128]{1,0:T(8,128)}, u32[]{:S(2)}) copy-start(f32[32,128]{1,0:T(8,128)} %get-tuple-element.41) | copy-start | bytes 49156
  6.9 21.4 %collective-permute-start.3 = (f32[128,128]{1,0:T(8,128)}, f32[128,128]{1,0:T(8,128)S(1)}, u32[]{:S(2)}, u32[]{:S(2)}) collective-permute-start(f32[128,128]{1,0:T(8,128)} %get-tuple-element.40), channel_id=1, source_target_pairs={{1,0},{2,1},{3,2},{4,3},{5,4},{6,5},{7,6},{8,7},{9,8},{10,9},{11,1... | collective-permute-start | bytes 196616 | tf_op jit(solution)/shard_map/ppermute | solution.py:279
  11.6 16.7 %collective-permute-start.2 = (f32[128,128]{1,0:T(8,128)}, f32[128,128]{1,0:T(8,128)S(1)}, u32[]{:S(2)}, u32[]{:S(2)}) collective-permute-start(f32[128,128]{1,0:T(8,128)} %get-tuple-element.40), channel_id=1, source_target_pairs={{0,1},{1,2},{2,3},{3,4},{4,5},{5,6},{6,7},{7,8},{8,9},{9,10},{10,1... | collective-permute-start | bytes 196616 | tf_op jit(solution)/shard_map/ppermute | solution.py:278
  11.6 16.7 %collective-permute-start = (f32[120,128]{1,0:T(8,128)}, f32[120,128]{1,0:T(8,128)S(1)}, u32[]{:S(2)}, u32[]{:S(2)}) collective-permute-start(f32[120,128]{1,0:T(8,128)} %get-tuple-element.38), channel_id=1, source_target_pairs={{0,32},{32,64},{64,96},{96,128},{128,160},{160,192},{192,224},{224... | collective-permute-start | bytes 184328 | tf_op jit(solution)/shard_map/ppermute | solution.py:276
  14.7 13.6 %collective-permute-start.1 = (f32[120,128]{1,0:T(8,128)}, f32[120,128]{1,0:T(8,128)S(1)}, u32[]{:S(2)}, u32[]{:S(2)}) collective-permute-start(f32[120,128]{1,0:T(8,128)} %get-tuple-element.39), channel_id=1, source_target_pairs={{32,0},{64,32},{96,64},{128,96},{160,128},{192,160},{224,192},{0,2... | collective-permute-start | bytes 184328 | tf_op jit(solution)/shard_map/ppermute | solution.py:277
  28.3 0.7 copy-start.2
  28.3 0.7 copy-start.3
  28.3 0.7 copy-start
  28.3 0.7 copy-start.1
  35.8 11.4 %all-to-all-start.1 = ((f32[32,4,128]{2,1,0:T(4,128)}), f32[32,4,128]{2,1,0:T(4,128)S(1)}, u32[]{:S(2)}, u32[]{:S(2)}) async-start(f32[32,4,128]{2,1,0:T(4,128)} %bitcast.11), calls=%async_computation.1 | async-start | bytes 131072 | tf_op jit(solution)/shard_map/all_to_all | solution.py:583
  47.2 0.7 copy-start.5
  50.0 13.4 %all-to-all-start.2 = ((f32[32,4,128]{2,1,0:T(4,128)}), f32[32,4,128]{2,1,0:T(4,128)S(1)}, u32[]{:S(2)}, u32[]{:S(2)}) async-start(f32[32,4,128]{2,1,0:T(4,128)} %bitcast.9), calls=%async_computation.2 | async-start | bytes 131072 | tf_op jit(solution)/shard_map/all_to_all | solution.py:583
  63.4 0.6 copy-start.4
  70.6 13.4 %collective-permute-start.7 = (f32[128,128]{1,0:T(8,128)}, f32[128,128]{1,0:T(8,128)S(1)}, u32[]{:S(2)}, u32[]{:S(2)}) collective-permute-start(f32[128,128]{1,0:T(8,128)} %get-tuple-element.67), channel_id=1, source_target_pairs={{1,0},{2,1},{3,2},{4,3},{5,4},{6,5},{7,6},{8,7},{9,8},{10,9},{11,1... | collective-permute-start | bytes 196616 | tf_op jit(solution)/shard_map/ppermute | solution.py:279
  75.4 8.6 %collective-permute-start.6 = (f32[128,128]{1,0:T(8,128)}, f32[128,128]{1,0:T(8,128)S(1)}, u32[]{:S(2)}, u32[]{:S(2)}) collective-permute-start(f32[128,128]{1,0:T(8,128)} %get-tuple-element.67), channel_id=1, source_target_pairs={{0,1},{1,2},{2,3},{3,4},{4,5},{5,6},{6,7},{7,8},{8,9},{9,10},{10,1... | collective-permute-start | bytes 196616 | tf_op jit(solution)/shard_map/ppermute | solution.py:278
  75.4 5.1 %collective-permute-start.4 = (f32[120,128]{1,0:T(8,128)}, f32[120,128]{1,0:T(8,128)S(1)}, u32[]{:S(2)}, u32[]{:S(2)}) collective-permute-start(f32[120,128]{1,0:T(8,128)} %get-tuple-element.65), channel_id=1, source_target_pairs={{0,32},{32,64},{64,96},{96,128},{128,160},{160,192},{192,224},{224... | collective-permute-start | bytes 184328 | tf_op jit(solution)/shard_map/ppermute | solution.py:276
  78.4 5.6 %collective-permute-start.5 = (f32[120,128]{1,0:T(8,128)}, f32[120,128]{1,0:T(8,128)S(1)}, u32[]{:S(2)}, u32[]{:S(2)}) collective-permute-start(f32[120,128]{1,0:T(8,128)} %get-tuple-element.66), channel_id=1, source_target_pairs={{32,0},{64,32},{96,64},{128,96},{160,128},{192,160},{224,192},{0,2... | collective-permute-start | bytes 184328 | tf_op jit(solution)/shard_map/ppermute | solution.py:277
  80.6 3.5 %copy-start.8 = (f32[120,128]{1,0:T(8,128)}, f32[120,128]{1,0:T(8,128)S(1)}, u32[]{:S(2)}) copy-start(f32[120,128]{1,0:T(8,128)S(1)} %collective-permute-done.4.before_ref) | copy-start | bytes 184324
  84.0 0.6 copy-start.9
  84.0 0.6 copy-start.6
  84.0 0.7 copy-start.7

commit v3 on v2

--- a/solution.py
+++ b/solution.py
@@ -29,19 +29,54 @@
     return pl.BlockSpec(tuple(shape), lambda i: (0,) * len(shape), pipeline_mode=pl.Buffered(1))
 
 
-def call(body, outs, ins, name, smem=(), flops=0, nbytes=0, scratch=()):
-    specs = [pl.BlockSpec(memory_space=pltpu.SMEM) if i in smem else whole(a.shape) for i, a in enumerate(ins)]
+def call(body, outs, ins, name, smem=(), far=(), fast=(), views=None, far_outs=(), flops=0, nbytes=0, scratch=(), sems=0, limit=56):
+    views = views or {}
+
+    def spec(i, a):
+        if i in smem:
+            return pl.BlockSpec(memory_space=pltpu.SMEM)
+        if i in far:
+            return pl.BlockSpec(memory_space=pl.ANY)
+        if i in fast:
+            return pl.BlockSpec(memory_space=pltpu.VMEM)
+        if i in views:
+            shape, at = views[i]
+            return pl.BlockSpec(shape, lambda g: at)
+        return whole(a.shape)
+
     return pl.pallas_call(
         body,
         grid=(1,),
         out_shape=[jax.ShapeDtypeStruct(s, F32) for s in outs],
-        in_specs=specs,
-        out_specs=[whole(s) for s in outs],
-        scratch_shapes=[pltpu.VMEM(s, F32) for s in scratch],
-        compiler_params=pltpu.CompilerParams(vmem_limit_bytes=56 * 1024 * 1024),
+        in_specs=[spec(i, a) for i, a in enumerate(ins)],
+        out_specs=[pl.BlockSpec(memory_space=pl.ANY) if i in far_outs else whole(s) for i, s in enumerate(outs)],
+        scratch_shapes=[pltpu.VMEM(s, t) for s, t in scratch] + ([pltpu.SemaphoreType.DMA((sems,))] if sems else []),
+        compiler_params=pltpu.CompilerParams(vmem_limit_bytes=limit * 1024 * 1024),
         cost_estimate=pl.CostEstimate(flops=flops, bytes_accessed=nbytes, transcendentals=0),
         name=name,
     )(*ins)
+
+
+def near(arrays):
+    return [(a.shape, a.dtype) for a in arrays]
+
+
+def floats(*shapes):
+    return [(s, F32) for s in shapes]
+
+
+def copies(sources, targets, sems, at=0):
+    return [pltpu.make_async_copy(s, t, sems.at[at + i]) for i, (s, t) in enumerate(zip(sources, targets))]
+
+
+def start(moves):
+    for move in moves:
+        move.start()
+
+
+def finish(moves):
+    for move in moves:
+        move.wait()
 
 
 def tables(stiff_ref, coef_ref):
@@ -152,7 +187,7 @@
     return before[index : index + 1, :], after[index : index + 1, :]
 
 
-def prep_body(span_ref, chord_ref, stringer_ref, cell_ref, stiff_ref, owner_ref, out_ref, match_ref):
+def prep_part(span_ref, chord_ref, stringer_ref, cell_ref, stiff_ref, owner_ref, out_ref, match_ref):
     def row_of(ref):
         return ref[...].reshape(1, -1)
 
@@ -236,7 +271,7 @@
     return columns
 
 
-def halo_body(stiff_ref, coef_ref, skin_ref, mat_ref, str_ref, smat_ref, after_ref, last_ref, first_ref, side_ref):
+def halo_part(stiff_ref, coef_ref, skin_ref, mat_ref, str_ref, smat_ref, last_ref, first_ref, side_ref):
     tabs = tables(stiff_ref, coef_ref)
     at_prev, at_next, at_left, at_right = ends_exist()
     lane = iota((CHUNK, 128), 1)
@@ -267,6 +302,19 @@
         first_ref[pl.ds(24 + r0, CHUNK), :] = columns
 
 
+def opening_body(
+    stiff_ref, coef_ref, span_ref, chord_ref, stringer_ref, cell_ref, weight_ref, owner_ref,
+    skin_far, mat_far, str_far, smat_far,
+    sent_ref, match_ref, last_ref, first_ref, side_ref,
+    skin_ref, mat_ref, str_ref, smat_ref, sems,
+):
+    moves = copies([skin_far, mat_far, str_far, smat_far], [skin_ref, mat_ref, str_ref, smat_ref], sems)
+    start(moves)
+    prep_part(span_ref, chord_ref, stringer_ref, cell_ref, weight_ref, owner_ref, sent_ref, match_ref)
+    finish(moves)
+    halo_part(stiff_ref, coef_ref, skin_ref, mat_ref, str_ref, smat_ref, last_ref, first_ref, side_ref)
+
+
 def exchange(last, first, side):
     def ring(axis):
         count = lax.axis_size(axis)
@@ -320,7 +368,7 @@
 
 def gather_body(
     stiff_ref, coef_ref, rows_ref, skin_ref, skin_prev_ref, mat_ref, str_ref, str_prev_ref, smat_ref,
-    before_ref, after_ref, lefts_ref, rights_ref,
+    before_ref, after_ref, lefts_ref, rights_ref, later_ref,
     out_ref, ks_ref, ps_ref, cs_ref, kt_ref, pt_ref, ct_ref,
     half_ref, down_ref, across_ref, left_ref, thick_ref, edge_ref, tedge_ref, co_ref,
 ):
@@ -341,16 +389,16 @@
             thick_ref[sl, :] = 1.0 / (half + half_of(other[sl, :], tabs))
         layer_bonds(lambda lo, n: half_ref[pl.ds(lo, n), :], total, ends, edge, field, down_ref, across_ref, left_ref)
 
-    prepare(128, mat_ref.at[5], mat_ref.at[4], ends_of(before_ref, after_ref, 23), edge_ref, 23)
+    prepare(128, mat_ref.at[1], mat_ref.at[0], ends_of(before_ref, after_ref, 23), edge_ref, 23)
     cs_ref[...] = co_ref[...]
     for r0 in range(0, 128, CHUNK):
         sl = pl.ds(r0, CHUNK)
 
         def put(c, value):
-            ps_ref[c, sl, :] = value - cs_ref[sl, :] * ks_ref[sl, :] * skin_ref[c, 5, sl, :]
+            ps_ref[c, sl, :] = value - cs_ref[sl, :] * ks_ref[sl, :] * skin_ref[c, 1, sl, :]
 
         chunk_step(
-            lambda c, l: rows_of(skin_ref, c, l), lambda c, l: rows_of(skin_prev_ref, c, l), 128, r0, 5, 3, bonds,
+            lambda c, l: rows_of(skin_ref, c, l - 4), lambda c, l: rows_of(skin_prev_ref, c, 0), 128, r0, 5, 3, bonds,
             edge_ref, lambda c: c * 6 + 5, lambda c: ends_of(before_ref, after_ref, c * 6 + 5), None, put,
         )
     for p in range(2):
@@ -369,7 +417,7 @@
             )
     t_fields = [jnp.concatenate([str_ref[0, c, 0], str_ref[1, c, 0]], axis=1) for c in range(3)]
     t_fields += [pt_ref[c] for c in range(3)] + [ct_ref[...] * kt_ref[...]]
-    s_fields = [skin_ref[c, 5] for c in range(3)] + [ps_ref[c] for c in range(3)] + [cs_ref[...]]
+    s_fields = [skin_ref[c, 1] for c in range(3)] + [ps_ref[c] for c in range(3)] + [cs_ref[...]]
     t_two = jnp.concatenate([t_lane, t_lane], axis=0)
     s_two = jnp.concatenate([s_lane, s_lane], axis=0)
     got = [as_lanes(fetch(t_row, t_two, f)) for f in t_fields]
@@ -383,7 +431,7 @@
         out_ref[pl.ds(j, 32, stride=4), :] = jnp.concatenate(part, axis=0)
 
 
-def bounce_body(match_ref, got_ref, after_ref, out_ref):
+def bounce_body(match_ref, got_ref, later_ref, out_ref):
     got = jnp.concatenate([got_ref[pl.ds(j, 32, stride=4), :] for j in range(4)], axis=1)
     lane = iota(got.shape, 1)
     zero = (lane & 16) == 0
@@ -402,44 +450,59 @@
         out_ref[pl.ds(j, 32, stride=4), :] = new[:, j * 128 : j * 128 + 128]
 
 
+def spread_all(row_mask, lane_hot_t, values):
+    rows = []
+    for value in values:
+        high, low = two_parts(value)
+        rows.append(jnp.concatenate([pick(row_mask, high.astype(F32)), pick(row_mask, low.astype(F32))], axis=1))
+    count = row_mask.shape[0]
+    got = jnp.dot(
+        jnp.concatenate(rows, axis=0), jnp.concatenate([lane_hot_t, lane_hot_t], axis=0), preferred_element_type=F32
+    )
+    return [got[f * count : f * count + count] for f in range(len(values))]
+
+
 def load_body(
     rows_ref, posted_ref, ks_ref, ps_ref, cs_ref, kt_ref, pt_ref, ct_ref, skin_ref, str_ref,
-    last_in, first_in, side_in,
+    last_in, first_in, side_in, columns_in,
     skin1_ref, sload_ref, str1_ref, tload_ref, last_ref, first_ref, side_ref,
 ):
     (t_row, t_lane, tk), (s_row, s_lane, sk) = hots(rows_ref)
     posted = [posted_ref[pl.ds(j, 32, stride=4), :] for j in range(4)]
 
-    def sums(side, row_mask, lane_hot, weight, f):
-        g = side * FIELDS + f
-        at = g % 4 * 32
-        return spread(row_mask, lane_hot, weight * one_row(row_lists(posted[g // 4][:, at : at + 32])))
-
-    last_ref[...] = last_in[...]
-    first_ref[...] = first_in[...]
+    def sums(side, row_mask, lane_hot, weight):
+        values = []
+        for f in range(FIELDS):
+            g = side * FIELDS + f
+            at = g % 4 * 32
+            values.append(weight * one_row(row_lists(posted[g // 4][:, at : at + 32])))
+        return spread_all(row_mask, lane_hot.astype(F32).T.astype(BF16), values)
+
+    last_ref[0:24, :] = last_in[...]
+    first_ref[0:24, :] = first_in[...]
     side = side_in[...]
     ks, cs = ks_ref[...], cs_ref[...]
-    qs = sums(0, s_row, s_lane, sk, 6)
+    got = sums(0, s_row, s_lane, sk)
     for c in range(3):
-        now = skin_ref[c, 5]
-        new = ps_ref[c] + cs * sums(0, s_row, s_lane, sk, c)
+        now = skin_ref[c, 0]
+        new = ps_ref[c] + cs * got[c]
         skin1_ref[c] = new
-        sload_ref[c] = sums(0, s_row, s_lane, sk, 3 + c) + qs * now - ks * new
+        sload_ref[c] = got[3 + c] + got[6] * now - ks * new
         f = c * 6 + 5
         last_ref[f : f + 1, :] = new[127:128, :]
         first_ref[f : f + 1, :] = new[0:1, :]
         side = with_columns(side, new, f)
     side_ref[...] = side
     kt, ct = kt_ref[...], ct_ref[...]
-    qt = sums(1, t_row, t_lane, tk, 6)
+    got = sums(1, t_row, t_lane, tk)
     third = iota((96, 256), 0) % 3
-    columns = last_in[24:120, :]
+    columns = columns_in[...]
     for c in range(3):
         now = jnp.concatenate([str_ref[0, c, 0], str_ref[1, c, 0]], axis=1)
         own = kt * now
         pair = jnp.where(third == 0, pltpu.roll(own, 95, 0), jnp.where(third == 1, pltpu.roll(own, 1, 0), 0.0))
-        new = pt_ref[c] + ct * sums(1, t_row, t_lane, tk, c)
-        load = sums(1, t_row, t_lane, tk, 3 + c) + qt * (own + pair) - kt * new
+        new = pt_ref[c] + ct * got[c]
+        load = got[3 + c] + got[6] * (own + pair) - kt * new
         for p in range(2):
             str1_ref[p, c] = new[:, p * 128 : p * 128 + 128]
             tload_ref[p, c] = load[:, p * 128 : p * 128 + 128]
@@ -449,11 +512,10 @@
 
 
 def bonds_body(
-    stiff_ref, coef_ref, mat_ref, smat_ref, before_ref, after_ref, lefts_ref, rights_ref, later_ref,
+    stiff_ref, coef_ref, mat_ref, smat_ref, before_ref, after_ref, lefts_ref, rights_ref,
     sd_ref, sa_ref, sl_ref, st_ref, sc_ref, td_ref, ta_ref, tl_ref, tt_ref, tc_ref,
-    token_ref, sh_ref, th_ref, edge_ref, tedge_ref,
+    sh_ref, th_ref, edge_ref, tedge_ref,
 ):
-    token_ref[...] = jnp.zeros((8, 128), F32)
     tabs = tables(stiff_ref, coef_ref)
     edge_ref[...] = joined(lefts_ref[...], rights_ref[...])
     tedge_ref[...] = joined(before_ref[24:120, :], after_ref[24:120, :])
@@ -495,9 +557,9 @@
             )
 
 
-def str_chunks(now, prev, bonds, edge_ref, layers, extra, put):
-    for r0 in range(0, 96, CHUNK):
-        for p in range(2):
+def str_chunks(now, prev, bonds, edge_ref, layers, extra, put, done=None):
+    for p in range(2):
+        for r0 in range(0, 96, CHUNK):
             for t in layers:
                 chunk_step(
                     lambda c, m: now(p, c, m), lambda c, m: prev(p, c, m), 96, r0, t, 3, bonds(p), edge_ref,
@@ -505,56 +567,88 @@
                     (lambda c: extra(p, c, r0)) if t == 0 and extra is not None else None,
                     lambda c, v: put(p, c, t, r0, v),
                 )
+        if done is not None:
+            done(p)
 
 
 def at_layers(*refs):
     return tuple((lambda l, ref=ref: ref.at[l]) for ref in refs)
 
 
-def first_body(
-    skin_ref, skin_prev_ref, str_ref, str_prev_ref, before_ref, after_ref, lefts_ref, rights_ref,
-    sd_ref, sa_ref, sl_ref, st_ref, sc_ref, td_ref, ta_ref, tl_ref, tt_ref, tc_ref, later_ref,
-    skin1_ref, str1_ref, last_ref, first_ref, side_ref,
-    edge_ref, tedge_ref,
-):
+def first_skin_body(*refs):
+    far, (skin1_far, last_ref, first_ref, side_ref), near_refs = refs[:11], refs[12:16], refs[16:27]
+    skin1_ref, edge_ref, sems = refs[27:]
+    skin_ref, skin_prev_ref, before_ref, after_ref, lefts_ref, rights_ref, sd_ref, sa_ref, sl_ref, st_ref, sc_ref = near_refs
+    moves = copies(far, near_refs, sems)
+    start(moves)
+    finish(moves)
     edge_ref[...] = joined(lefts_ref[...], rights_ref[...])
-    tedge_ref[...] = joined(before_ref[24:120, :], after_ref[24:120, :])
-    last_ref[0:24, :] = jnp.zeros((24, 128), F32)
-    first_ref[0:24, :] = jnp.zeros((24, 128), F32)
+    last_ref[...] = jnp.zeros((24, 128), F32)
+    first_ref[...] = jnp.zeros((24, 128), F32)
 
     def put_skin(c, l, r0, value):
         skin1_ref[c, l, pl.ds(r0, CHUNK), :] = value
-
-    def put_str(p, c, t, r0, value):
-        str1_ref[p, c, t - 1, pl.ds(r0, CHUNK), :] = value
 
     skin_chunks(
         lambda c, l: rows_of(skin_ref, c, l), lambda c, l: rows_of(skin_prev_ref, c, l),
         at_layers(sd_ref, sa_ref, sl_ref, st_ref, sc_ref), edge_ref, before_ref, after_ref, range(5), None, put_skin,
     )
-    str_chunks(
-        lambda p, c, t: rows_of(str_ref, p, c, t), lambda p, c, t: rows_of(str_prev_ref, p, c, t),
-        lambda p: at_layers(*(r.at[p] for r in (td_ref, ta_ref, tl_ref, tt_ref, tc_ref))), tedge_ref, range(1, 6), None,
-        put_str,
-    )
+    out = copies([skin1_ref], [skin1_far], sems, 11)
+    start(out)
     for r0 in range(0, 128, CHUNK):
         side_ref[pl.ds(r0, CHUNK), :] = pack_skin(
             jnp.zeros((CHUNK, 128), F32), lambda c, l: skin1_ref[c, l, pl.ds(r0, CHUNK), :], range(5), r0, first_ref, last_ref
         )
+    finish(out)
+
+
+def first_str_body(*refs):
+    far, (str1_far, columns_ref), near_refs = refs[:9], refs[10:12], refs[12:21]
+    str1_ref, tedge_ref, sems = refs[21:]
+    str_ref, str_prev_ref, before_ref, after_ref, td_ref, ta_ref, tl_ref, tt_ref, tc_ref = near_refs
+    moves = [
+        copies([f.at[p] for f in far[:2] + far[4:]], [n.at[p] for n in near_refs[:2] + near_refs[4:]], sems, 7 * p)
+        for p in range(2)
+    ]
+    ends = copies(far[2:4], near_refs[2:4], sems, 14)
+    start(ends + moves[0] + moves[1])
+    finish(ends + moves[0])
+    tedge_ref[...] = joined(before_ref[24:120, :], after_ref[24:120, :])
+    out = copies([str1_ref.at[0], str1_ref.at[1]], [str1_far.at[0], str1_far.at[1]], sems, 16)
+
+    def put_str(p, c, t, r0, value):
+        str1_ref[p, c, t - 1, pl.ds(r0, CHUNK), :] = value
+
+    def done(p):
+        out[p].start()
+        if p == 0:
+            finish(moves[1])
+
+    str_chunks(
+        lambda p, c, t: rows_of(str_ref, p, c, t), lambda p, c, t: rows_of(str_prev_ref, p, c, t),
+        lambda p: at_layers(*(r.at[p] for r in (td_ref, ta_ref, tl_ref, tt_ref, tc_ref))), tedge_ref, range(1, 6), None,
+        put_str, done,
+    )
     for r0 in range(0, 96, CHUNK):
-        columns = pack_str(
+        columns_ref[pl.ds(r0, CHUNK), :] = pack_str(
             jnp.zeros((CHUNK, 128), F32), lambda p, c, t: str1_ref[p, c, t - 1, pl.ds(r0, CHUNK), :], range(1, 6)
         )
-        last_ref[pl.ds(24 + r0, CHUNK), :] = columns
-        first_ref[pl.ds(24 + r0, CHUNK), :] = columns
-
-
-def second_body(
-    skin_ref, skin_prev_ref, str_ref, str_prev_ref, before_ref, after_ref, lefts_ref, rights_ref,
-    sd_ref, sa_ref, sl_ref, st_ref, sc_ref, td_ref, ta_ref, tl_ref, tt_ref, tc_ref,
-    skin_face_ref, str_face_ref, sload_ref, tload_ref, skin2_ref, str2_ref,
-    edge_ref, tedge_ref,
-):
+    finish(out)
+
+
+def second_body(*refs):
+    far, (skin2_far, str2_far), near_refs = refs[:22], refs[22:24], refs[24:46]
+    skin2_ref, str2_ref, edge_ref, tedge_ref, sems = refs[46:]
+    moves = copies(far, near_refs, sems)
+    (
+        skin_ref, skin_prev_ref, str_ref, str_prev_ref, before_ref, after_ref, lefts_ref, rights_ref,
+        sd_ref, sa_ref, sl_ref, st_ref, sc_ref, td_ref, ta_ref, tl_ref, tt_ref, tc_ref,
+        skin_face_ref, str_face_ref, sload_ref, tload_ref,
+    ) = near_refs
+    skin_moves = [moves[i] for i in (4, 5, 6, 7, 8, 9, 10, 11, 12, 0, 1, 18, 20)]
+    str_moves = [moves[i] for i in (13, 14, 15, 16, 17, 2, 3, 19, 21)]
+    start(skin_moves + str_moves)
+    finish(skin_moves)
     edge_ref[...] = joined(lefts_ref[...], rights_ref[...])
     tedge_ref[...] = joined(before_ref[24:120, :], after_ref[24:120, :])
 
@@ -570,12 +664,16 @@
         at_layers(sd_ref, sa_ref, sl_ref, st_ref, sc_ref), edge_ref, before_ref, after_ref, range(6),
         lambda c, r0: sload_ref[c, pl.ds(r0, CHUNK), :], put_skin,
     )
+    out_moves = copies([skin2_ref, str2_ref.at[0], str2_ref.at[1]], [skin2_far, str2_far.at[0], str2_far.at[1]], sems, 22)
+    out_moves[0].start()
+    finish(str_moves)
     str_chunks(
         lambda p, c, t: rows_of(str_face_ref, p, c) if t == 0 else rows_of(str_ref, p, c, t - 1),
         lambda p, c, t: rows_of(str_prev_ref, p, c, t),
         lambda p: at_layers(*(r.at[p] for r in (td_ref, ta_ref, tl_ref, tt_ref, tc_ref))), tedge_ref, range(6),
-        lambda p, c, r0: tload_ref[p, c, pl.ds(r0, CHUNK), :], put_str,
-    )
+        lambda p, c, r0: tload_ref[p, c, pl.ds(r0, CHUNK), :], put_str, lambda p: out_moves[1 + p].start(),
+    )
+    finish(out_moves)
 
 
 def swap(values):
@@ -588,46 +686,62 @@
     skin_now, skin_prev, skin_mat, stringer_now, stringer_prev, stringer_mat, owner_slot,
     rivet_span, rivet_chord, rivet_stringer, rivet_cell, rivet_stiff, mat_stiff, mat_coef,
 ):
-    rivets = [rivet_span, rivet_chord, rivet_stringer, rivet_cell, rivet_stiff]
-    sent, match = call(prep_body, [(32, 128), (128, 128)], rivets + [owner_slot.reshape(1, -1)], "prep")
+    mats = [mat_stiff, mat_coef]
+    own = [skin_now, skin_mat, stringer_now, stringer_mat]
+    column = [(120, 128), (120, 128), (128, 128)]
+    sent, match, *packs = call(
+        opening_body, [(32, 128), (128, 128), *column],
+        [*mats, rivet_span, rivet_chord, rivet_stringer, rivet_cell, rivet_stiff, owner_slot.reshape(1, -1), *own],
+        "opening", smem=(0, 1), far=range(8, 12), flops=4000000, nbytes=4000000, scratch=near(own), sems=4,
+    )
     rows = swap(sent)
-    mats = [mat_stiff, mat_coef]
-    column = [(120, 128), (120, 128), (128, 128)]
-    packs = call(
-        halo_body, column, [*mats, skin_now, skin_mat, stringer_now, stringer_mat, match], "halo", smem=(0, 1),
-        flops=4000000, nbytes=4000000,
-    )
     halos = exchange(*packs)
     edges = [(128, 128), (96, 128)]
+    bonds = call(
+        bonds_body, [(6, 136, 128), *[(6, 128, 128)] * 4, (2, 6, 104, 128), *[(2, 6, 96, 128)] * 4],
+        [*mats, skin_mat, stringer_mat, *halos], "bonds", smem=(0, 1), flops=10000000, nbytes=8000000,
+        scratch=floats((6, 128, 128), (6, 96, 128), *edges),
+    )
     found, *kept = call(
         gather_body, [(128, 128), (128, 128), (3, 128, 128), (128, 128), (96, 256), (3, 96, 256), (96, 256)],
-        [*mats, rows, skin_now, skin_prev, skin_mat, stringer_now, stringer_prev, stringer_mat, *halos], "gather",
-        smem=(0, 1), flops=1000000000, nbytes=2000000,
-        scratch=[(128, 128), (136, 128), (128, 128), (128, 128), (128, 128), *edges, (128, 128)],
+        [*mats, rows, skin_now, skin_prev, skin_mat, stringer_now, stringer_prev, stringer_mat, *halos, bonds[0]], "gather",
+        smem=(0, 1), far=(13,), flops=1000000000, nbytes=2000000,
+        views={
+            3: ((3, 2, 128, 128), (0, 2, 0, 0)),
+            4: ((3, 1, 128, 128), (0, 5, 0, 0)),
+            5: ((2, 128, 128), (2, 0, 0)),
+            6: ((2, 3, 2, 96, 128), (0, 0, 0, 0, 0)),
+            7: ((2, 3, 1, 96, 128), (0, 0, 0, 0, 0)),
+            8: ((2, 2, 96, 128), (0, 0, 0, 0)),
+        },
+        scratch=floats((128, 128), (136, 128), (128, 128), (128, 128), (128, 128), *edges, (128, 128)),
     )
     given = swap(found)
-    bonds = call(
-        bonds_body,
-        [(6, 136, 128), *[(6, 128, 128)] * 4, (2, 6, 104, 128), *[(2, 6, 96, 128)] * 4, (8, 128)],
-        [*mats, skin_mat, stringer_mat, *halos, found], "bonds", smem=(0, 1), flops=10000000, nbytes=8000000,
-        scratch=[(6, 128, 128), (6, 96, 128), *edges],
-    )
-    (turned,) = call(bounce_body, [(128, 128)], [match, given, bonds[-1]], "bounce")
+    parts = [skin_now, skin_prev, *halos, *bonds[:5]]
+    skin1, last, first, side = call(
+        first_skin_body, [(3, 5, 128, 128), (24, 128), (24, 128), (128, 128)], [*parts, found], "first_skin",
+        far=range(12), far_outs=(0,), flops=10000000, nbytes=5000000,
+        scratch=near(parts) + floats((3, 5, 128, 128), (128, 128)), sems=12,
+    )
+    (turned,) = call(bounce_body, [(128, 128)], [match, given, last], "bounce", fast=(1,), far=(2,), limit=8)
     posted = swap(turned)
-    skin1, str1, *packs1 = call(
-        first_body, [(3, 5, 128, 128), (2, 3, 5, 96, 128), *column],
-        [skin_now, skin_prev, stringer_now, stringer_prev, *halos, *bonds[:-1], turned], "first",
-        flops=20000000, nbytes=10000000, scratch=edges,
+    parts = [stringer_now, stringer_prev, *halos[:2], *bonds[5:]]
+    str1, columns = call(
+        first_str_body, [(2, 3, 5, 96, 128), (96, 128)], [*parts, turned], "first_str",
+        far=range(10), far_outs=(0,), flops=10000000, nbytes=5000000,
+        scratch=near(parts) + floats((2, 3, 5, 96, 128), (96, 128)), sems=18,
     )
     skin_face, sload, str_face, tload, *packs2 = call(
         load_body, [(3, 128, 128), (3, 128, 128), (2, 3, 96, 128), (2, 3, 96, 128), *column],
-        [rows, posted, *kept, skin_now, stringer_now, *packs1], "load", flops=1000000000, nbytes=2000000,
+        [rows, posted, *kept, skin_now, stringer_now, last, first, side, columns], "load", flops=1000000000, nbytes=2000000,
+        views={8: ((3, 1, 128, 128), (0, 5, 0, 0)), 9: ((2, 3, 1, 96, 128), (0, 0, 0, 0, 0))},
     )
     halos1 = exchange(*packs2)
+    parts = [skin1, skin_now, str1, stringer_now, *halos1, *bonds, skin_face, str_face, sload, tload]
+    results = [(3, 6, 128, 128), (2, 3, 6, 96, 128)]
     return call(
-        second_body, [(3, 6, 128, 128), (2, 3, 6, 96, 128)],
-        [skin1, skin_now, str1, stringer_now, *halos1, *bonds[:-1], skin_face, str_face, sload, tload], "second",
-        flops=20000000, nbytes=10000000, scratch=edges,
+        second_body, results, parts, "second", far=range(22), far_outs=(0, 1), flops=20000000, nbytes=10000000,
+        scratch=near(parts) + floats(*results, *edges), sems=25, limit=56,
     )
 
 

time: 93.4 us -> 86.5 us (0.926)
  blocking collectives: 13.6 us -> 0 us
  starting transfers between devices: 24.2 us -> 31.7 us
  Pallas kernels: 43.5 us -> 38.6 us
  waiting for transfers between devices: 8.43 us -> 11 us
  local copies, waits for them, and re-layouts: 2.61 us -> 3.84 us
    all_to_all x1 -> x0, blocking collectives: 13.6 us -> none  [swap(): lax.all_to_all(values.reshape(peers, -1, 128), 'chord', split_axis=0, con...]
    all_to_all x2 -> x3, starting transfers between devices: 8.66 us -> 17.9 us  [swap(): lax.all_to_all(values.reshape(peers, -1, 128), 'chord', split_axis=0, con...]
    pallas_call x8, Pallas kernels: 43.5 us -> 38.6 us  [call(): pl.pallas_call(body, grid=(1,), out_shape=[jax.ShapeDtypeStruct(s, F32) f...]
    all_to_all x2 -> x3, waiting for transfers between devices: 2.78 us -> 5.36 us  [swap(): lax.all_to_all(values.reshape(peers, -1, 128), 'chord', split_axis=0, con...]
    ppermute x2, starting transfers between devices: 9.43 us -> 7.72 us  [exchange(): rights = lax.ppermute(side, 'chord', back(ring('chord')))]
    unnamed x22 -> x24, local copies, waits for them, and re-layouts: 2.61 us -> 3.84 us
  transfers between devices with their start and end apart: 10 -> 11, of which waited for: 3 -> 5; matrix products, arithmetic and copies ran while one was open for 0% -> 0% of each run, Pallas kernels for 14% -> 18%
where the time goes in v3:
time: 86.5 us; the launch traced here: 86 us
  Pallas kernels  38.6 us (45%)
  starting transfers between devices  31.7 us (37%)
  waiting for transfers between devices  11 us (13%)
  local copies, waits for them, and re-layouts  3.84 us (4%)
  between operations  0.94 us (1%)
    pallas_call x8, Pallas kernels, call(): pl.pallas_call(body, grid=(1,), out_shape=[jax.ShapeDtypeStruct(s, F32) f...  38.6 us
    all_to_all x3, starting transfers between devices, swap(): lax.all_to_all(values.reshape(peers, -1, 128), 'chord', split_axis=0, con...  17.9 us
    ppermute x2, starting transfers between devices, exchange(): rights = lax.ppermute(side, 'chord', back(ring('chord')))  7.72 us
    ppermute x2, starting transfers between devices, exchange(): before = lax.ppermute(last, 'span', ring('span'))  6.08 us
    all_to_all x3, waiting for transfers between devices, swap(): lax.all_to_all(values.reshape(peers, -1, 128), 'chord', split_axis=0, con...  5.36 us
    unnamed x24, local copies, waits for them, and re-layouts  3.84 us
    ppermute x2, waiting for transfers between devices, exchange(): after = lax.ppermute(first, 'span', back(ring('span')))  3.46 us
    ppermute x2, waiting for transfers between devices, exchange(): before = lax.ppermute(last, 'span', ring('span'))  2.18 us
  transfers between devices with their start and end apart: 11, of which 5 were waited for; matrix products, arithmetic and copies ran while one was open for 0% of the time, Pallas kernels for 18%

profile of v3, /device:TPU:96, one launch (start us, length us, event | category | flops | bytes accessed | tf_op | source)
XLA Modules:
  0.0 86.0 jit_solution(13516333791730691982)
XLA Ops:
  0.6 5.0 %opening.1 = (f32[32,128]{1,0:T(8,128)}, f32[128,128]{1,0:T(8,128)}, f32[120,128]{1,0:T(8,128)}, f32[120,128]{1,0:T(8,128)}, f32[128,128]{1,0:T(8,128)}) custom-call(f32[8]{0:T(128)} %stiff_ref.5, f32[8]{0:T(128)} %coef_ref.5, s32[768]{0:T(1024)} %span_ref.1, s32[768]{0:T(1024)} %chord_ref.1, s32[768]{0:T(1024)} %stringer_ref.1, s32[768]{0:T(1024)} %cell_ref.1, ...), custom_call_target="tpu_custom_call" | custom-call | flops 4000000 | bytes 4000000 | tf_op jit(solution)/shard_map/opening/pallas_call | solution.py:47
  5.6 4.7 %collective-permute-start.3 = (f32[128,128]{1,0:T(8,128)}, f32[128,128]{1,0:T(8,128)S(1)}, u32[]{:S(2)}, u32[]{:S(2)}) collective-permute-start(f32[128,128]{1,0:T(8,128)} %get-tuple-element.39), channel_id=1, source_target_pairs={{1,0},{2,1},{3,2},{4,3},{5,4},{6,5},{7,6},{8,7},{9,8},{10,9},{11,1... | collective-permute-start | bytes 196616 | tf_op jit(solution)/shard_map/ppermute | solution.py:327
  10.3 3.1 %collective-permute-start = (f32[120,128]{1,0:T(8,128)}, f32[120,128]{1,0:T(8,128)S(1)}, u32[]{:S(2)}, u32[]{:S(2)}) collective-permute-start(f32[120,128]{1,0:T(8,128)} %get-tuple-element.37), channel_id=1, source_target_pairs={{0,32},{32,64},{64,96},{96,128},{128,160},{160,192},{192,224},{224... | collective-permute-start | bytes 184328 | tf_op jit(solution)/shard_map/ppermute | solution.py:324
  13.5 0.0 collective-permute-start.1
  13.5 6.5 %all-to-all-start = ((f32[32,1,128]{2,1,0:T(1,128)}), f32[32,1,128]{2,1,0:T(1,128)S(1)}, u32[]{:S(2)}, u32[]{:S(2)}) async-start(f32[32,1,128]{2,1,0:T(1,128)} %bitcast.14), calls=%async_computation | async-start | bytes 32768 | tf_op jit(solution)/shard_map/all_to_all | solution.py:681
  19.9 0.0 collective-permute-done.before_ref.refs_2_
  20.0 0.6 copy-done.2
  20.6 0.0 copy-done.3
  20.6 0.0 copy-done.4
  20.6 0.6 copy-done.5
  21.2 4.9 %bonds.1 = (f32[6,136,128]{2,1,0:T(8,128)}, f32[6,128,128]{2,1,0:T(8,128)}, f32[6,128,128]{2,1,0:T(8,128)}, f32[6,128,128]{2,1,0:T(8,128)}, f32[6,128,128]{2,1,0...) custom-call(f32[8]{0:T(128)} %stiff_ref.5, ...), custom_call_target="tpu_custom_call" | custom-call | flops 10000000 | bytes 8000000 | tf_op jit(solution)/shard_map/bonds/pallas_call | solution.py:47
  26.1 1.2 %all-to-all-done = f32[32,1,128]{2,1,0:T(1,128)S(1)} async-done(((f32[32,1,128]{2,1,0:T(1,128)}), f32[32,1,128]{2,1,0:T(1,128)S(1)}, u32[]{:S(2)}, u32[]{:S(2)}) %all-to-all-start) | async-done | bytes 16416 | tf_op jit(solution)/shard_map/all_to_all | solution.py:681
  27.3 0.6 copy-done.7
  27.9 5.2 %gather.1 = (f32[128,128]{1,0:T(8,128)}, f32[128,128]{1,0:T(8,128)}, f32[3,128,128]{2,1,0:T(8,128)}, f32[128,128]{1,0:T(8,128)}, f32[96,256]{1,0:T(8,128)}, /*index=5*/f32[3,96,256]{2,1,0:T(8,128)}, f32[96,256]{1,0:T(8,128)}) custom-call(f32[8]{0:T(128)} %stiff_ref.5, f32[8]{0:T(128)} %coef_ref.5, f32[32,128]{1,0:T(8,128)} %bitcast.12, ...), custom_call_target="tpu_custom_call" | custom-call | flops 1000000000 | bytes 2000000 | tf_op jit(solution)/shard_map/gather/pallas_call | solution.py:47
  33.1 6.4 %all-to-all-start.1 = ((f32[32,4,128]{2,1,0:T(4,128)}), f32[32,4,128]{2,1,0:T(4,128)S(1)}, u32[]{:S(2)}, u32[]{:S(2)}) async-start(f32[32,4,128]{2,1,0:T(4,128)} %bitcast.11), calls=%async_computation.1 | async-start | bytes 131072 | tf_op jit(solution)/shard_map/all_to_all | solution.py:681
  39.5 5.1 %first_skin.1 = (f32[3,5,128,128]{3,2,1,0:T(8,128)}, f32[24,128]{1,0:T(8,128)}, f32[24,128]{1,0:T(8,128)}, f32[128,128]{1,0:T(8,128)}) custom-call(f32[3,6,128,128]{3,2,1,0:T(8,128)} %refs_1_.5, f32[3,6,128,128]{3,2,1,0:T(8,128)} %refs_1_.3, f32[120,128]{1,0:T(8,128)} %copy-done.2, f32[120,128]{1,0:T(8,128)} %copy-done.3, f32[128,128]{1,0:T(8,128)} %copy-done.5, ...), custom_call_target="tpu_custom_call" | custom-call | flops 10000000 | bytes 5000000 | tf_op jit(solution)/shard_map/first_skin/pallas_call | solution.py:47
  44.6 2.2 %all-to-all-done.1 = f32[32,4,128]{2,1,0:T(4,128)S(1)} async-done(((f32[32,4,128]{2,1,0:T(4,128)}), f32[32,4,128]{2,1,0:T(4,128)S(1)}, u32[]{:S(2)}, u32[]{:S(2)}) %all-to-all-start.1) | async-done | bytes 65568 | tf_op jit(solution)/shard_map/all_to_all | solution.py:681
  46.9 0.7 copy-done.1
  47.6 1.3 %bounce.1.refs_9_ = f32[128,128]{1,0:T(8,128)} custom-call(f32[128,128]{1,0:T(8,128)S(1)} %copy-done, f32[128,128]{1,0:T(8,128)S(1)} %bitcast.9, f32[24,128]{1,0:T(8,128)S(1)} %copy-done.1), custom_call_target="tpu_custom_call" | custom-call | tf_op jit(solution)/shard_map/bounce/pallas_call | solution.py:47
  48.9 5.0 %all-to-all-start.2 = ((f32[32,4,128]{2,1,0:T(4,128)}), f32[32,4,128]{2,1,0:T(4,128)S(1)}, u32[]{:S(2)}, u32[]{:S(2)}) async-start(f32[32,4,128]{2,1,0:T(4,128)} %bitcast.6), calls=%async_computation.2 | async-start | bytes 131072 | tf_op jit(solution)/shard_map/all_to_all | solution.py:681
  53.9 5.5 %first_str.1 = (f32[2,3,5,96,128]{4,3,2,1,0:T(8,128)}, f32[96,128]{1,0:T(8,128)}) custom-call(f32[2,3,6,96,128]{4,3,2,1,0:T(8,128)} %refs_3_.1, f32[2,3,6,96,128]{4,3,2,1,0:T(8,128)} %refs_1_.4, f32[120,128]{1,0:T(8,128)} %copy-done.2, f32[120,128]{1,0:T(8,128)} %copy-done.3, f32[2,6,104,128]{3,2,1,0:T(8,128)} %get-tuple-element.48.refs_4_.refs_13_, ...), custom_call_target="tpu_custom_call" | custom-call | flops 10000000 | bytes 5000000 | tf_op jit(solution)/shard_map/first_str/pallas_call | solution.py:47
  59.4 2.0 %all-to-all-done.2 = f32[32,4,128]{2,1,0:T(4,128)S(1)} async-done(((f32[32,4,128]{2,1,0:T(4,128)}), f32[32,4,128]{2,1,0:T(4,128)S(1)}, u32[]{:S(2)}, u32[]{:S(2)}) %all-to-all-start.2) | async-done | bytes 65568 | tf_op jit(solution)/shard_map/all_to_all | solution.py:681
  61.4 0.6 copy-done.6
  62.0 4.6 %load.1 = (f32[3,128,128]{2,1,0:T(8,128)}, f32[3,128,128]{2,1,0:T(8,128)}, f32[2,3,96,128]{3,2,1,0:T(8,128)}, f32[2,3,96,128]{3,2,1,0:T(8,128)}, f32[120,128]{1,...) custom-call(f32[32,128]{1,0:T(8,128)} %bitcast.13, f32[128,128]{1,0:T(8,128)} %bitcast.10, ...), custom_call_target="tpu_custom_call" | custom-call | flops 1000000000 | bytes 2000000 | tf_op jit(solution)/shard_map/load/pallas_call | solution.py:47
  66.6 3.0 %collective-permute-start.7 = (f32[128,128]{1,0:T(8,128)}, f32[128,128]{1,0:T(8,128)S(1)}, u32[]{:S(2)}, u32[]{:S(2)}) collective-permute-start(f32[128,128]{1,0:T(8,128)} %get-tuple-element.67), channel_id=1, source_target_pairs={{1,0},{2,1},{3,2},{4,3},{5,4},{6,5},{7,6},{8,7},{9,8},{10,9},{11,1... | collective-permute-start | bytes 196616 | tf_op jit(solution)/shard_map/ppermute | solution.py:327
  69.6 2.9 %collective-permute-start.4 = (f32[120,128]{1,0:T(8,128)}, f32[120,128]{1,0:T(8,128)S(1)}, u32[]{:S(2)}, u32[]{:S(2)}) collective-permute-start(f32[120,128]{1,0:T(8,128)} %get-tuple-element.65), channel_id=1, source_target_pairs={{0,32},{32,64},{64,96},{96,128},{128,160},{160,192},{192,224},{224... | collective-permute-start | bytes 184328 | tf_op jit(solution)/shard_map/ppermute | solution.py:324
  72.5 2.2 %collective-permute-done.4.refs_4_ = f32[120,128]{1,0:T(8,128)S(1)} collective-permute-done((f32[120,128]{1,0:T(8,128)}, f32[120,128]{1,0:T(8,128)S(1)}, u32[]{:S(2)}, u32[]{:S(2)}) %collective-permute-start.4) | collective-permute-done | bytes 61472 | tf_op jit(solution)/shard_map/ppermute | solution.py:324
  74.7 3.5 %collective-permute-done.5.refs_5_ = f32[120,128]{1,0:T(8,128)S(1)} collective-permute-done((f32[120,128]{1,0:T(8,128)}, f32[120,128]{1,0:T(8,128)S(1)}, u32[]{:S(2)}, u32[]{:S(2)}) %collective-permute-start.5) | collective-permute-done | bytes 61472 | tf_op jit(solution)/shard_map/ppermute | solution.py:325
  78.2 0.6 copy-done.11
  78.8 0.0 copy-done.8
  78.8 0.0 copy-done.9
  78.8 7.0 %second.1 = (f32[3,6,128,128]{3,2,1,0:T(8,128)}, f32[2,3,6,96,128]{4,3,2,1,0:T(8,128)}) custom-call(f32[3,5,128,128]{3,2,1,0:T(8,128)} %get-tuple-element.47.refs_0_, f32[3,6,128,128]{3,2,1,0:T(8,128)} %refs_1_.5, f32[2,3,5,96,128]{4,3,2,1,0:T(8,128)} %get-tuple-element.55.refs_2_, f32[2,3,6,96,128]{4,3,2,1,0:T(8,128)} %refs_3_.1, f32[120,128]{1,0:T(8,128)} %copy-done.10, ...), custom_call_target="tpu_custom_call" | custom-call | flops 20000000 | bytes 10000000 | tf_op jit(solution)/shard_map/second/pallas_call | solution.py:47
  (22 shorter events, 0.0 us)
Async XLA Ops:
  5.6 14.4 %collective-permute-start.3 = (f32[128,128]{1,0:T(8,128)}, f32[128,128]{1,0:T(8,128)S(1)}, u32[]{:S(2)}, u32[]{:S(2)}) collective-permute-start(f32[128,128]{1,0:T(8,128)} %get-tuple-element.39), channel_id=1, source_target_pairs={{1,0},{2,1},{3,2},{4,3},{5,4},{6,5},{7,6},{8,7},{9,8},{10,9},{11,1... | collective-permute-start | bytes 196616 | tf_op jit(solution)/shard_map/ppermute | solution.py:327
  10.3 9.7 %collective-permute-start.2 = (f32[128,128]{1,0:T(8,128)}, f32[128,128]{1,0:T(8,128)S(1)}, u32[]{:S(2)}, u32[]{:S(2)}) collective-permute-start(f32[128,128]{1,0:T(8,128)} %get-tuple-element.39), channel_id=1, source_target_pairs={{0,1},{1,2},{2,3},{3,4},{4,5},{5,6},{6,7},{7,8},{8,9},{9,10},{10,1... | collective-permute-start | bytes 196616 | tf_op jit(solution)/shard_map/ppermute | solution.py:326
  10.3 9.6 %collective-permute-start = (f32[120,128]{1,0:T(8,128)}, f32[120,128]{1,0:T(8,128)S(1)}, u32[]{:S(2)}, u32[]{:S(2)}) collective-permute-start(f32[120,128]{1,0:T(8,128)} %get-tuple-element.37), channel_id=1, source_target_pairs={{0,32},{32,64},{64,96},{96,128},{128,160},{160,192},{192,224},{224... | collective-permute-start | bytes 184328 | tf_op jit(solution)/shard_map/ppermute | solution.py:324
  13.5 6.5 %collective-permute-start.1 = (f32[120,128]{1,0:T(8,128)}, f32[120,128]{1,0:T(8,128)S(1)}, u32[]{:S(2)}, u32[]{:S(2)}) collective-permute-start(f32[120,128]{1,0:T(8,128)} %get-tuple-element.38), channel_id=1, source_target_pairs={{32,0},{64,32},{96,64},{128,96},{160,128},{192,160},{224,192},{0,2... | collective-permute-start | bytes 184328 | tf_op jit(solution)/shard_map/ppermute | solution.py:325
  13.5 13.8 %all-to-all-start = ((f32[32,1,128]{2,1,0:T(1,128)}), f32[32,1,128]{2,1,0:T(1,128)S(1)}, u32[]{:S(2)}, u32[]{:S(2)}) async-start(f32[32,1,128]{2,1,0:T(1,128)} %bitcast.14), calls=%async_computation | async-start | bytes 32768 | tf_op jit(solution)/shard_map/all_to_all | solution.py:681
  19.9 0.6 copy-start.2
  19.9 0.6 copy-start.3
  20.0 0.7 copy-start.4
  20.6 0.6 copy-start.5
  27.3 0.6 copy-start.7
  33.1 13.8 %all-to-all-start.1 = ((f32[32,4,128]{2,1,0:T(4,128)}), f32[32,4,128]{2,1,0:T(4,128)S(1)}, u32[]{:S(2)}, u32[]{:S(2)}) async-start(f32[32,4,128]{2,1,0:T(4,128)} %bitcast.11), calls=%async_computation.1 | async-start | bytes 131072 | tf_op jit(solution)/shard_map/all_to_all | solution.py:681
  39.5 7.3 %copy-start = (f32[128,128]{1,0:T(8,128)S(1)}, f32[128,128]{1,0:T(8,128)}, u32[]{:S(2)}) copy-start(f32[128,128]{1,0:T(8,128)} %get-tuple-element.53.match_ref) | copy-start | bytes 196612
  46.9 0.7 copy-start.1
  48.9 12.5 %all-to-all-start.2 = ((f32[32,4,128]{2,1,0:T(4,128)}), f32[32,4,128]{2,1,0:T(4,128)S(1)}, u32[]{:S(2)}, u32[]{:S(2)}) async-start(f32[32,4,128]{2,1,0:T(4,128)} %bitcast.6), calls=%async_computation.2 | async-start | bytes 131072 | tf_op jit(solution)/shard_map/all_to_all | solution.py:681
  61.4 0.6 copy-start.6
  66.6 11.6 %collective-permute-start.7 = (f32[128,128]{1,0:T(8,128)}, f32[128,128]{1,0:T(8,128)S(1)}, u32[]{:S(2)}, u32[]{:S(2)}) collective-permute-start(f32[128,128]{1,0:T(8,128)} %get-tuple-element.67), channel_id=1, source_target_pairs={{1,0},{2,1},{3,2},{4,3},{5,4},{6,5},{7,6},{8,7},{9,8},{10,9},{11,1... | collective-permute-start | bytes 196616 | tf_op jit(solution)/shard_map/ppermute | solution.py:327
  69.6 8.6 %collective-permute-start.6 = (f32[128,128]{1,0:T(8,128)}, f32[128,128]{1,0:T(8,128)S(1)}, u32[]{:S(2)}, u32[]{:S(2)}) collective-permute-start(f32[128,128]{1,0:T(8,128)} %get-tuple-element.67), channel_id=1, source_target_pairs={{0,1},{1,2},{2,3},{3,4},{4,5},{5,6},{6,7},{7,8},{8,9},{9,10},{10,1... | collective-permute-start | bytes 196616 | tf_op jit(solution)/shard_map/ppermute | solution.py:326
  69.6 5.1 %collective-permute-start.4 = (f32[120,128]{1,0:T(8,128)}, f32[120,128]{1,0:T(8,128)S(1)}, u32[]{:S(2)}, u32[]{:S(2)}) collective-permute-start(f32[120,128]{1,0:T(8,128)} %get-tuple-element.65), channel_id=1, source_target_pairs={{0,32},{32,64},{64,96},{96,128},{128,160},{160,192},{192,224},{224... | collective-permute-start | bytes 184328 | tf_op jit(solution)/shard_map/ppermute | solution.py:324
  72.5 5.6 %collective-permute-start.5 = (f32[120,128]{1,0:T(8,128)}, f32[120,128]{1,0:T(8,128)S(1)}, u32[]{:S(2)}, u32[]{:S(2)}) collective-permute-start(f32[120,128]{1,0:T(8,128)} %get-tuple-element.66), channel_id=1, source_target_pairs={{32,0},{64,32},{96,64},{128,96},{160,128},{192,160},{224,192},{0,2... | collective-permute-start | bytes 184328 | tf_op jit(solution)/shard_map/ppermute | solution.py:325
  74.7 3.5 %copy-start.10 = (f32[120,128]{1,0:T(8,128)}, f32[120,128]{1,0:T(8,128)S(1)}, u32[]{:S(2)}) copy-start(f32[120,128]{1,0:T(8,128)S(1)} %collective-permute-done.4.refs_4_) | copy-start | bytes 184324
  78.2 0.6 copy-start.11
  78.2 0.7 copy-start.8
  78.2 0.7 copy-start.9

commit v4 on v3

--- a/solution.py
+++ b/solution.py
@@ -55,6 +55,18 @@
         cost_estimate=pl.CostEstimate(flops=flops, bytes_accessed=nbytes, transcendentals=0),
         name=name,
     )(*ins)
+
+
+def gate(moves):
+    waited = set()
+
+    def need(*keys):
+        for key in keys:
+            if key in moves and key not in waited:
+                waited.add(key)
+                moves[key].wait()
+
+    return need
 
 
 def near(arrays):
@@ -356,10 +368,16 @@
     return lax.dot_general(left, right, NT, preferred_element_type=F32)
 
 
-def fetch(row_mask, lane_hot2, cells):
-    high, low = two_parts(cells)
-    wide = jnp.dot(jnp.concatenate([high, low], axis=1), lane_hot2, preferred_element_type=F32)
-    return jnp.sum(jnp.where(row_mask, wide, 0.0), axis=0, keepdims=True)
+def fetch_all(row_mask, lane_hot, fields):
+    parts = [jnp.concatenate(two_parts(cells), axis=1) for cells in fields]
+    wide = jnp.dot(
+        jnp.concatenate(parts, axis=0), jnp.concatenate([lane_hot, lane_hot], axis=0), preferred_element_type=F32
+    )
+    count = row_mask.shape[0]
+    return [
+        jnp.sum(jnp.where(row_mask, wide[f * count : f * count + count], 0.0), axis=0, keepdims=True)
+        for f in range(len(fields))
+    ]
 
 
 def as_lanes(row):
@@ -418,10 +436,7 @@
     t_fields = [jnp.concatenate([str_ref[0, c, 0], str_ref[1, c, 0]], axis=1) for c in range(3)]
     t_fields += [pt_ref[c] for c in range(3)] + [ct_ref[...] * kt_ref[...]]
     s_fields = [skin_ref[c, 1] for c in range(3)] + [ps_ref[c] for c in range(3)] + [cs_ref[...]]
-    t_two = jnp.concatenate([t_lane, t_lane], axis=0)
-    s_two = jnp.concatenate([s_lane, s_lane], axis=0)
-    got = [as_lanes(fetch(t_row, t_two, f)) for f in t_fields]
-    got += [as_lanes(fetch(s_row, s_two, f)) for f in s_fields]
+    got = [as_lanes(row) for row in fetch_all(t_row, t_lane, t_fields) + fetch_all(s_row, s_lane, s_fields)]
     pad = jnp.zeros((8, 128), F32)
     got += [pad, pad]
     for j in range(4):
@@ -513,88 +528,114 @@
 
 def bonds_body(
     stiff_ref, coef_ref, mat_ref, smat_ref, before_ref, after_ref, lefts_ref, rights_ref,
-    sd_ref, sa_ref, sl_ref, st_ref, sc_ref, td_ref, ta_ref, tl_ref, tt_ref, tc_ref,
-    sh_ref, th_ref, edge_ref, tedge_ref,
+    sb_far, tb_far, sb_ref, tb_ref, sh_ref, th_ref, edge_ref, tedge_ref, sems,
 ):
     tabs = tables(stiff_ref, coef_ref)
     edge_ref[...] = joined(lefts_ref[...], rights_ref[...])
     tedge_ref[...] = joined(before_ref[24:120, :], after_ref[24:120, :])
-    for r0 in range(0, 128, CHUNK):
-        sl = pl.ds(r0, CHUNK)
-        for l in range(6):
+    out = []
+
+    def send(source, target):
+        move = pltpu.make_async_copy(source, target, sems.at[len(out)])
+        move.start()
+        out.append(move)
+
+    for l in range(6):
+        for r0 in range(0, 128, CHUNK):
+            sl = pl.ds(r0, CHUNK)
             half, coef = half_coef(mat_ref[l, sl, :], tabs)
             if l > 0:
-                st_ref[l - 1, sl, :] = 1.0 / (half + sh_ref[l - 1, sl, :])
+                sb_ref[l - 1, 3, sl, :] = 1.0 / (half + sh_ref[l - 1, sl, :])
             sh_ref[l, sl, :] = half
-            sc_ref[l, sl, :] = coef
-    for l in range(6):
+            sb_ref[l, 4, sl, :] = coef
         layer_bonds(
             rows_of(sh_ref, l), 128, ends_of(before_ref, after_ref, 18 + l), edge_ref, 18 + l,
-            sd_ref.at[l], sa_ref.at[l], sl_ref.at[l],
+            sb_ref.at[l, 0], sb_ref.at[l, 1], sb_ref.at[l, 2],
         )
+        if l > 0:
+            send(sb_ref.at[l - 1], sb_far.at[l - 1])
+    send(sb_ref.at[5], sb_far.at[5])
     for p in range(2):
-        for r0 in range(0, 96, CHUNK):
-            sl = pl.ds(r0, CHUNK)
-            for t in range(6):
+        for t in range(6):
+            for r0 in range(0, 96, CHUNK):
+                sl = pl.ds(r0, CHUNK)
                 half, coef = half_coef(smat_ref[p, t, sl, :], tabs)
                 if t > 0:
-                    tt_ref[p, t - 1, sl, :] = 1.0 / (half + th_ref[t - 1, sl, :])
+                    tb_ref[p, t - 1, 3, sl, :] = 1.0 / (half + th_ref[t - 1, sl, :])
                 th_ref[t, sl, :] = half
-                tc_ref[p, t, sl, :] = coef
-        for t in range(6):
+                tb_ref[p, t, 4, sl, :] = coef
             layer_bonds(
-                rows_of(th_ref, t), 96, None, tedge_ref, 36 + p * 6 + t, td_ref.at[p, t], ta_ref.at[p, t], tl_ref.at[p, t]
+                rows_of(th_ref, t), 96, None, tedge_ref, 36 + p * 6 + t,
+                tb_ref.at[p, t, 0], tb_ref.at[p, t, 1], tb_ref.at[p, t, 2],
             )
-
-
-def skin_chunks(now, prev, bonds, edge_ref, before_ref, after_ref, layers, extra, put):
+            if t > 0:
+                send(tb_ref.at[p, t - 1], tb_far.at[p, t - 1])
+        send(tb_ref.at[p, 5], tb_far.at[p, 5])
+    finish(out)
+
+
+def kinds(ref):
+    return tuple((lambda l, k=k: ref.at[l, k]) for k in range(5))
+
+
+def skin_layer(layer, now, prev, bonds, edge_ref, before_ref, after_ref, extra, put):
     for r0 in range(0, 128, CHUNK):
-        for l in layers:
-            chunk_step(
-                now, prev, 128, r0, l, 3, bonds, edge_ref, lambda c: c * 6 + l,
-                lambda c: ends_of(before_ref, after_ref, c * 6 + l),
-                (lambda c: extra(c, r0)) if l == 5 and extra is not None else None, lambda c, v: put(c, l, r0, v),
-            )
-
-
-def str_chunks(now, prev, bonds, edge_ref, layers, extra, put, done=None):
-    for p in range(2):
-        for r0 in range(0, 96, CHUNK):
-            for t in layers:
-                chunk_step(
-                    lambda c, m: now(p, c, m), lambda c, m: prev(p, c, m), 96, r0, t, 3, bonds(p), edge_ref,
-                    lambda c: (p * 3 + c) * 6 + t, None,
-                    (lambda c: extra(p, c, r0)) if t == 0 and extra is not None else None,
-                    lambda c, v: put(p, c, t, r0, v),
-                )
-        if done is not None:
-            done(p)
-
-
-def at_layers(*refs):
-    return tuple((lambda l, ref=ref: ref.at[l]) for ref in refs)
-
-
-def first_skin_body(*refs):
-    far, (skin1_far, last_ref, first_ref, side_ref), near_refs = refs[:11], refs[12:16], refs[16:27]
-    skin1_ref, edge_ref, sems = refs[27:]
-    skin_ref, skin_prev_ref, before_ref, after_ref, lefts_ref, rights_ref, sd_ref, sa_ref, sl_ref, st_ref, sc_ref = near_refs
-    moves = copies(far, near_refs, sems)
-    start(moves)
-    finish(moves)
-    edge_ref[...] = joined(lefts_ref[...], rights_ref[...])
+        chunk_step(
+            now, prev, 128, r0, layer, 3, bonds, edge_ref, lambda c: c * 6 + layer,
+            lambda c: ends_of(before_ref, after_ref, c * 6 + layer),
+            None if extra is None else (lambda c: extra[c, pl.ds(r0, CHUNK), :]),
+            lambda c, v: put(c, pl.ds(r0, CHUNK), v),
+        )
+
+
+def str_layer(p, layer, now, prev, bonds, edge_ref, extra, put):
+    for r0 in range(0, 96, CHUNK):
+        chunk_step(
+            now, prev, 96, r0, layer, 3, bonds, edge_ref, lambda c: (p * 3 + c) * 6 + layer, None,
+            None if extra is None else (lambda c: extra[p, c, pl.ds(r0, CHUNK), :]),
+            lambda c, v: put(c, pl.ds(r0, CHUNK), v),
+        )
+
+
+def moving(pairs, sems):
+    moves = {}
+    for key, source, target in pairs:
+        moves[key] = pltpu.make_async_copy(source, target, sems.at[len(moves)])
+        moves[key].start()
+    return moves
+
+
+def first_skin_body(
+    skin_far, prev_far, before_far, after_far, lefts_far, rights_far, sb_far, later_ref,
+    skin1_far, last_ref, first_ref, side_ref,
+    skin_ref, prev_ref, before_ref, after_ref, lefts_ref, rights_ref, sb_ref, skin1_ref, edge_ref, sems,
+):
+    pairs = [
+        ("l", lefts_far, lefts_ref), ("r", rights_far, rights_ref), ("b", before_far, before_ref), ("a", after_far, after_ref),
+    ]
+    for l in range(6):
+        pairs.append((("u", l), skin_far.at[:, l], skin_ref.at[:, l]))
+        if l < 5:
+            pairs += [(("k", l), sb_far.at[l], sb_ref.at[l]), (("v", l), prev_far.at[:, l], prev_ref.at[:, l])]
+    moves = moving(pairs, sems)
+    need = gate(moves)
     last_ref[...] = jnp.zeros((24, 128), F32)
     first_ref[...] = jnp.zeros((24, 128), F32)
-
-    def put_skin(c, l, r0, value):
-        skin1_ref[c, l, pl.ds(r0, CHUNK), :] = value
-
-    skin_chunks(
-        lambda c, l: rows_of(skin_ref, c, l), lambda c, l: rows_of(skin_prev_ref, c, l),
-        at_layers(sd_ref, sa_ref, sl_ref, st_ref, sc_ref), edge_ref, before_ref, after_ref, range(5), None, put_skin,
-    )
-    out = copies([skin1_ref], [skin1_far], sems, 11)
-    start(out)
+    need("l", "r", "b", "a")
+    edge_ref[...] = joined(lefts_ref[...], rights_ref[...])
+    out = []
+    for l in range(5):
+        need(("u", l), ("u", l + 1), ("k", l), ("v", l))
+
+        def put(c, sl, value):
+            skin1_ref[c, l, sl, :] = value
+
+        skin_layer(
+            l, lambda c, m: rows_of(skin_ref, c, m), lambda c, m: rows_of(prev_ref, c, m), kinds(sb_ref), edge_ref,
+            before_ref, after_ref, None, put,
+        )
+        out.append(pltpu.make_async_copy(skin1_ref.at[:, l], skin1_far.at[:, l], sems.at[len(pairs) + l]))
+        out[l].start()
     for r0 in range(0, 128, CHUNK):
         side_ref[pl.ds(r0, CHUNK), :] = pack_skin(
             jnp.zeros((CHUNK, 128), F32), lambda c, l: skin1_ref[c, l, pl.ds(r0, CHUNK), :], range(5), r0, first_ref, last_ref
@@ -602,33 +643,40 @@
     finish(out)
 
 
-def first_str_body(*refs):
-    far, (str1_far, columns_ref), near_refs = refs[:9], refs[10:12], refs[12:21]
-    str1_ref, tedge_ref, sems = refs[21:]
-    str_ref, str_prev_ref, before_ref, after_ref, td_ref, ta_ref, tl_ref, tt_ref, tc_ref = near_refs
-    moves = [
-        copies([f.at[p] for f in far[:2] + far[4:]], [n.at[p] for n in near_refs[:2] + near_refs[4:]], sems, 7 * p)
-        for p in range(2)
-    ]
-    ends = copies(far[2:4], near_refs[2:4], sems, 14)
-    start(ends + moves[0] + moves[1])
-    finish(ends + moves[0])
+def first_str_body(
+    str_far, prev_far, before_far, after_far, tb_far, later_ref,
+    str1_far, columns_ref,
+    str_ref, prev_ref, before_ref, after_ref, tb_ref, str1_ref, tedge_ref, sems,
+):
+    pairs = [("b", before_far, before_ref), ("a", after_far, after_ref)]
+    for p in range(2):
+        for t in range(6):
+            pairs += [
+                (("u", p, t), str_far.at[p, :, t], str_ref.at[p, :, t]), (("k", p, t), tb_far.at[p, t], tb_ref.at[p, t]),
+            ]
+            if t > 0:
+                pairs.append((("v", p, t), prev_far.at[p, :, t], prev_ref.at[p, :, t]))
+    moves = moving(pairs, sems)
+    need = gate(moves)
+    need("b", "a")
     tedge_ref[...] = joined(before_ref[24:120, :], after_ref[24:120, :])
-    out = copies([str1_ref.at[0], str1_ref.at[1]], [str1_far.at[0], str1_far.at[1]], sems, 16)
-
-    def put_str(p, c, t, r0, value):
-        str1_ref[p, c, t - 1, pl.ds(r0, CHUNK), :] = value
-
-    def done(p):
-        out[p].start()
-        if p == 0:
-            finish(moves[1])
-
-    str_chunks(
-        lambda p, c, t: rows_of(str_ref, p, c, t), lambda p, c, t: rows_of(str_prev_ref, p, c, t),
-        lambda p: at_layers(*(r.at[p] for r in (td_ref, ta_ref, tl_ref, tt_ref, tc_ref))), tedge_ref, range(1, 6), None,
-        put_str, done,
-    )
+    out = []
+    for p in range(2):
+        for t in range(1, 6):
+            need(("u", p, t - 1), ("k", p, t - 1), ("u", p, t), ("u", p, t + 1), ("k", p, t), ("v", p, t))
+
+            def put(c, sl, value):
+                str1_ref[p, c, t - 1, sl, :] = value
+
+            str_layer(
+                p, t, lambda c, m: rows_of(str_ref, p, c, m), lambda c, m: rows_of(prev_ref, p, c, m),
+                kinds(tb_ref.at[p]), tedge_ref, None, put,
+            )
+            move = pltpu.make_async_copy(
+                str1_ref.at[p, :, t - 1], str1_far.at[p, :, t - 1], sems.at[len(pairs) + len(out)]
+            )
+            move.start()
+            out.append(move)
     for r0 in range(0, 96, CHUNK):
         columns_ref[pl.ds(r0, CHUNK), :] = pack_str(
             jnp.zeros((CHUNK, 128), F32), lambda p, c, t: str1_ref[p, c, t - 1, pl.ds(r0, CHUNK), :], range(1, 6)
@@ -636,44 +684,73 @@
     finish(out)
 
 
-def second_body(*refs):
-    far, (skin2_far, str2_far), near_refs = refs[:22], refs[22:24], refs[24:46]
-    skin2_ref, str2_ref, edge_ref, tedge_ref, sems = refs[46:]
-    moves = copies(far, near_refs, sems)
-    (
-        skin_ref, skin_prev_ref, str_ref, str_prev_ref, before_ref, after_ref, lefts_ref, rights_ref,
-        sd_ref, sa_ref, sl_ref, st_ref, sc_ref, td_ref, ta_ref, tl_ref, tt_ref, tc_ref,
-        skin_face_ref, str_face_ref, sload_ref, tload_ref,
-    ) = near_refs
-    skin_moves = [moves[i] for i in (4, 5, 6, 7, 8, 9, 10, 11, 12, 0, 1, 18, 20)]
-    str_moves = [moves[i] for i in (13, 14, 15, 16, 17, 2, 3, 19, 21)]
-    start(skin_moves + str_moves)
-    finish(skin_moves)
+def second_body(
+    skin_far, prev_far, str_far, str_prev_far, before_far, after_far, lefts_far, rights_far, sb_far, tb_far,
+    skin_face_far, str_face_far, sload_far, tload_far,
+    skin2_far, str2_far,
+    skin_ref, prev_ref, str_ref, str_prev_ref, before_ref, after_ref, lefts_ref, rights_ref, sb_ref, tb_ref,
+    skin_face_ref, str_face_ref, sload_ref, tload_ref,
+    skin2_ref, str2_ref, edge_ref, tedge_ref, sems,
+):
+    pairs = [
+        ("l", lefts_far, lefts_ref), ("r", rights_far, rights_ref), ("b", before_far, before_ref), ("a", after_far, after_ref),
+    ]
+    for l in range(6):
+        if l < 5:
+            pairs.append((("u", l), skin_far.at[:, l], skin_ref.at[:, l]))
+        else:
+            pairs += [(("u", l), skin_face_far, skin_face_ref), ("s", sload_far, sload_ref)]
+        pairs += [(("k", l), sb_far.at[l], sb_ref.at[l]), (("v", l), prev_far.at[:, l], prev_ref.at[:, l])]
+    pairs += [("f", str_face_far, str_face_ref), ("t", tload_far, tload_ref)]
+    for p in range(2):
+        for t in range(6):
+            if t > 0:
+                pairs.append((("u", p, t), str_far.at[p, :, t - 1], str_ref.at[p, :, t - 1]))
+            pairs += [
+                (("k", p, t), tb_far.at[p, t], tb_ref.at[p, t]),
+                (("v", p, t), str_prev_far.at[p, :, t], str_prev_ref.at[p, :, t]),
+            ]
+    moves = moving(pairs, sems)
+    need = gate(moves)
+    need("l", "r", "b", "a")
     edge_ref[...] = joined(lefts_ref[...], rights_ref[...])
     tedge_ref[...] = joined(before_ref[24:120, :], after_ref[24:120, :])
-
-    def put_skin(c, l, r0, value):
-        skin2_ref[c, l, pl.ds(r0, CHUNK), :] = value
-
-    def put_str(p, c, t, r0, value):
-        str2_ref[p, c, t, pl.ds(r0, CHUNK), :] = value
-
-    skin_chunks(
-        lambda c, l: rows_of(skin_face_ref, c) if l == 5 else rows_of(skin_ref, c, l),
-        lambda c, l: rows_of(skin_prev_ref, c, l),
-        at_layers(sd_ref, sa_ref, sl_ref, st_ref, sc_ref), edge_ref, before_ref, after_ref, range(6),
-        lambda c, r0: sload_ref[c, pl.ds(r0, CHUNK), :], put_skin,
-    )
-    out_moves = copies([skin2_ref, str2_ref.at[0], str2_ref.at[1]], [skin2_far, str2_far.at[0], str2_far.at[1]], sems, 22)
-    out_moves[0].start()
-    finish(str_moves)
-    str_chunks(
-        lambda p, c, t: rows_of(str_face_ref, p, c) if t == 0 else rows_of(str_ref, p, c, t - 1),
-        lambda p, c, t: rows_of(str_prev_ref, p, c, t),
-        lambda p: at_layers(*(r.at[p] for r in (td_ref, ta_ref, tl_ref, tt_ref, tc_ref))), tedge_ref, range(6),
-        lambda p, c, r0: tload_ref[p, c, pl.ds(r0, CHUNK), :], put_str, lambda p: out_moves[1 + p].start(),
-    )
-    finish(out_moves)
+    out = []
+
+    def send(source, target):
+        move = pltpu.make_async_copy(source, target, sems.at[len(pairs) + len(out)])
+        move.start()
+        out.append(move)
+
+    for l in range(6):
+        need(("u", l), ("u", l + 1), ("k", l), ("v", l))
+        if l == 5:
+            need("s")
+
+        def put(c, sl, value):
+            skin2_ref[c, l, sl, :] = value
+
+        skin_layer(
+            l, lambda c, m: rows_of(skin_face_ref, c) if m == 5 else rows_of(skin_ref, c, m),
+            lambda c, m: rows_of(prev_ref, c, m), kinds(sb_ref), edge_ref, before_ref, after_ref,
+            sload_ref if l == 5 else None, put,
+        )
+        send(skin2_ref.at[:, l], skin2_far.at[:, l])
+    need("f", "t")
+    for p in range(2):
+        for t in range(6):
+            need(("u", p, t), ("u", p, t + 1), ("k", p, t), ("v", p, t))
+
+            def put(c, sl, value):
+                str2_ref[p, c, t, sl, :] = value
+
+            str_layer(
+                p, t, lambda c, m: rows_of(str_face_ref, p, c) if m == 0 else rows_of(str_ref, p, c, m - 1),
+                lambda c, m: rows_of(str_prev_ref, p, c, m), kinds(tb_ref.at[p]), tedge_ref,
+                tload_ref if t == 0 else None, put,
+            )
+            send(str2_ref.at[p, :, t], str2_far.at[p, :, t])
+    finish(out)
 
 
 def swap(values):
@@ -697,10 +774,10 @@
     rows = swap(sent)
     halos = exchange(*packs)
     edges = [(128, 128), (96, 128)]
+    bonds = [(6, 5, 136, 128), (2, 6, 5, 104, 128)]
     bonds = call(
-        bonds_body, [(6, 136, 128), *[(6, 128, 128)] * 4, (2, 6, 104, 128), *[(2, 6, 96, 128)] * 4],
-        [*mats, skin_mat, stringer_mat, *halos], "bonds", smem=(0, 1), flops=10000000, nbytes=8000000,
-        scratch=floats((6, 128, 128), (6, 96, 128), *edges),
+        bonds_body, bonds, [*mats, skin_mat, stringer_mat, *halos], "bonds", smem=(0, 1), far_outs=(0, 1),
+        flops=10000000, nbytes=8000000, scratch=floats(*bonds, (6, 128, 128), (6, 96, 128), *edges), sems=18,
     )
     found, *kept = call(
         gather_body, [(128, 128), (128, 128), (3, 128, 128), (128, 128), (96, 256), (3, 96, 256), (96, 256)],
@@ -717,19 +794,19 @@
         scratch=floats((128, 128), (136, 128), (128, 128), (128, 128), (128, 128), *edges, (128, 128)),
     )
     given = swap(found)
-    parts = [skin_now, skin_prev, *halos, *bonds[:5]]
+    parts = [skin_now, skin_prev, *halos, bonds[0]]
     skin1, last, first, side = call(
         first_skin_body, [(3, 5, 128, 128), (24, 128), (24, 128), (128, 128)], [*parts, found], "first_skin",
-        far=range(12), far_outs=(0,), flops=10000000, nbytes=5000000,
-        scratch=near(parts) + floats((3, 5, 128, 128), (128, 128)), sems=12,
+        far=range(8), far_outs=(0,), flops=10000000, nbytes=5000000,
+        scratch=near(parts) + floats((3, 5, 128, 128), (128, 128)), sems=25,
     )
     (turned,) = call(bounce_body, [(128, 128)], [match, given, last], "bounce", fast=(1,), far=(2,), limit=8)
     posted = swap(turned)
-    parts = [stringer_now, stringer_prev, *halos[:2], *bonds[5:]]
+    parts = [stringer_now, stringer_prev, *halos[:2], bonds[1]]
     str1, columns = call(
         first_str_body, [(2, 3, 5, 96, 128), (96, 128)], [*parts, turned], "first_str",
-        far=range(10), far_outs=(0,), flops=10000000, nbytes=5000000,
-        scratch=near(parts) + floats((2, 3, 5, 96, 128), (96, 128)), sems=18,
+        far=range(6), far_outs=(0,), flops=10000000, nbytes=5000000,
+        scratch=near(parts) + floats((2, 3, 5, 96, 128), (96, 128)), sems=46,
     )
     skin_face, sload, str_face, tload, *packs2 = call(
         load_body, [(3, 128, 128), (3, 128, 128), (2, 3, 96, 128), (2, 3, 96, 128), *column],
@@ -740,8 +817,8 @@
     parts = [skin1, skin_now, str1, stringer_now, *halos1, *bonds, skin_face, str_face, sload, tload]
     results = [(3, 6, 128, 128), (2, 3, 6, 96, 128)]
     return call(
-        second_body, results, parts, "second", far=range(22), far_outs=(0, 1), flops=20000000, nbytes=10000000,
-        scratch=near(parts) + floats(*results, *edges), sems=25, limit=56,
+        second_body, results, parts, "second", far=range(14), far_outs=(0, 1), flops=20000000, nbytes=10000000,
+        scratch=near(parts) + floats(*results, *edges), sems=80, limit=56,
     )
 
 

time: 86.5 us -> 84 us (0.971)
  Pallas kernels: 38.6 us -> 36.1 us
  starting transfers between devices: 31.7 us -> 29.7 us
  waiting for transfers between devices: 11 us -> 13 us
    pallas_call x8, Pallas kernels: 38.6 us -> 36.1 us  [call(): pl.pallas_call(body, grid=(1,), out_shape=[jax.ShapeDtypeStruct(s, F32) f...]
    all_to_all x3, waiting for transfers between devices: 5.36 us -> 7.32 us  [swap(): lax.all_to_all(values.reshape(peers, -1, 128), 'chord', split_axis=0, con...]
    all_to_all x3, starting transfers between devices: 17.9 us -> 16.2 us  [swap(): lax.all_to_all(values.reshape(peers, -1, 128), 'chord', split_axis=0, con...]
  transfers between devices with their start and end apart: 11 -> 11, of which waited for: 5 -> 5; matrix products, arithmetic and copies ran while one was open for 0% -> 0% of each run, Pallas kernels for 18% -> 16%
where the time goes in v4:
time: 84 us; the launch traced here: 83.6 us
  Pallas kernels  36.1 us (43%)
  starting transfers between devices  29.7 us (35%)
  waiting for transfers between devices  13 us (15%)
  local copies, waits for them, and re-layouts  3.87 us (5%)
  between operations  0.97 us (1%)
    pallas_call x8, Pallas kernels, call(): pl.pallas_call(body, grid=(1,), out_shape=[jax.ShapeDtypeStruct(s, F32) f...  36.1 us
    all_to_all x3, starting transfers between devices, swap(): lax.all_to_all(values.reshape(peers, -1, 128), 'chord', split_axis=0, con...  16.2 us
    ppermute x2, starting transfers between devices, exchange(): rights = lax.ppermute(side, 'chord', back(ring('chord')))  7.47 us
    all_to_all x3, waiting for transfers between devices, swap(): lax.all_to_all(values.reshape(peers, -1, 128), 'chord', split_axis=0, con...  7.32 us
    ppermute x2, starting transfers between devices, exchange(): before = lax.ppermute(last, 'span', ring('span'))  6.07 us
    unnamed x24, local copies, waits for them, and re-layouts  3.87 us
    ppermute x2, waiting for transfers between devices, exchange(): after = lax.ppermute(first, 'span', back(ring('span')))  3.46 us
    ppermute x2, waiting for transfers between devices, exchange(): before = lax.ppermute(last, 'span', ring('span'))  2.18 us
  transfers between devices with their start and end apart: 11, of which 5 were waited for; matrix products, arithmetic and copies ran while one was open for 0% of the time, Pallas kernels for 16%

profile of v4, /device:TPU:96, one launch (start us, length us, event | category | flops | bytes accessed | tf_op | source)
XLA Modules:
  0.0 83.6 jit_solution(9046835772239024893)
XLA Ops:
  0.6 5.0 %opening.1 = (f32[32,128]{1,0:T(8,128)}, f32[128,128]{1,0:T(8,128)}, f32[120,128]{1,0:T(8,128)}, f32[120,128]{1,0:T(8,128)}, f32[128,128]{1,0:T(8,128)}) custom-call(f32[8]{0:T(128)} %stiff_ref.5, f32[8]{0:T(128)} %coef_ref.5, s32[768]{0:T(1024)} %span_ref.1, s32[768]{0:T(1024)} %chord_ref.1, s32[768]{0:T(1024)} %stringer_ref.1, s32[768]{0:T(1024)} %cell_ref.1, ...), custom_call_target="tpu_custom_call" | custom-call | flops 4000000 | bytes 4000000 | tf_op jit(solution)/shard_map/opening/pallas_call | solution.py:47
  5.6 4.7 %collective-permute-start.3 = (f32[128,128]{1,0:T(8,128)}, f32[128,128]{1,0:T(8,128)S(1)}, u32[]{:S(2)}, u32[]{:S(2)}) collective-permute-start(f32[128,128]{1,0:T(8,128)} %get-tuple-element.31), channel_id=1, source_target_pairs={{1,0},{2,1},{3,2},{4,3},{5,4},{6,5},{7,6},{8,7},{9,8},{10,9},{11,1... | collective-permute-start | bytes 196616 | tf_op jit(solution)/shard_map/ppermute | solution.py:339
  10.3 3.1 %collective-permute-start = (f32[120,128]{1,0:T(8,128)}, f32[120,128]{1,0:T(8,128)S(1)}, u32[]{:S(2)}, u32[]{:S(2)}) collective-permute-start(f32[120,128]{1,0:T(8,128)} %get-tuple-element.29), channel_id=1, source_target_pairs={{0,32},{32,64},{64,96},{96,128},{128,160},{160,192},{192,224},{224... | collective-permute-start | bytes 184328 | tf_op jit(solution)/shard_map/ppermute | solution.py:336
  13.5 0.0 collective-permute-start.1
  13.5 6.5 %all-to-all-start = ((f32[32,1,128]{2,1,0:T(1,128)}), f32[32,1,128]{2,1,0:T(1,128)S(1)}, u32[]{:S(2)}, u32[]{:S(2)}) async-start(f32[32,1,128]{2,1,0:T(1,128)} %bitcast.14), calls=%async_computation | async-start | bytes 32768 | tf_op jit(solution)/shard_map/all_to_all | solution.py:758
  20.0 0.6 copy-done.2
  20.6 0.0 copy-done.3
  20.6 0.0 copy-done.4
  20.6 0.6 copy-done.5
  21.3 4.2 %bonds.1 = (f32[6,5,136,128]{3,2,1,0:T(8,128)}, f32[2,6,5,104,128]{4,3,2,1,0:T(8,128)}) custom-call(f32[8]{0:T(128)} %stiff_ref.5, f32[8]{0:T(128)} %coef_ref.5, s32[6,128,128]{2,1,0:T(8,128)} %mat_ref.3, s32[2,6,96,128]{3,2,1,0:T(8,128)} %smat_ref.3, f32[120,128]{1,0:T(8,128)} %copy-done.2, f32[120,128]{1,0:T(8,128)} %copy-done.3, f32[128,128]{1,0:T(8,128)} %copy-done.5, ...), custom_call_target="tpu_custom_call" | custom-call | flops 10000000 | bytes 8000000 | tf_op jit(solution)/shard_map/bonds/pallas_call | solution.py:47
  25.4 1.8 %all-to-all-done = f32[32,1,128]{2,1,0:T(1,128)S(1)} async-done(((f32[32,1,128]{2,1,0:T(1,128)}), f32[32,1,128]{2,1,0:T(1,128)S(1)}, u32[]{:S(2)}, u32[]{:S(2)}) %all-to-all-start) | async-done | bytes 16416 | tf_op jit(solution)/shard_map/all_to_all | solution.py:758
  27.3 0.6 copy-done.7
  27.9 4.9 %gather.1 = (f32[128,128]{1,0:T(8,128)}, f32[128,128]{1,0:T(8,128)}, f32[3,128,128]{2,1,0:T(8,128)}, f32[128,128]{1,0:T(8,128)}, f32[96,256]{1,0:T(8,128)}, /*index=5*/f32[3,96,256]{2,1,0:T(8,128)}, f32[96,256]{1,0:T(8,128)}) custom-call(f32[8]{0:T(128)} %stiff_ref.5, f32[8]{0:T(128)} %coef_ref.5, f32[32,128]{1,0:T(8,128)} %bitcast.12, ...), custom_call_target="tpu_custom_call" | custom-call | flops 1000000000 | bytes 2000000 | tf_op jit(solution)/shard_map/gather/pallas_call | solution.py:47
  32.8 5.7 %all-to-all-start.1 = ((f32[32,4,128]{2,1,0:T(4,128)}), f32[32,4,128]{2,1,0:T(4,128)S(1)}, u32[]{:S(2)}, u32[]{:S(2)}) async-start(f32[32,4,128]{2,1,0:T(4,128)} %bitcast.11), calls=%async_computation.1 | async-start | bytes 131072 | tf_op jit(solution)/shard_map/all_to_all | solution.py:758
  38.5 4.1 %first_skin.1 = (f32[3,5,128,128]{3,2,1,0:T(8,128)}, f32[24,128]{1,0:T(8,128)}, f32[24,128]{1,0:T(8,128)}, f32[128,128]{1,0:T(8,128)}) custom-call(f32[3,6,128,128]{3,2,1,0:T(8,128)} %prev_far.5, f32[3,6,128,128]{3,2,1,0:T(8,128)} %prev_far.3, f32[120,128]{1,0:T(8,128)} %copy-done.2, f32[120,128]{1,0:T(8,128)} %copy-done.3, f32[128,128]{1,0:T(8,128)} %copy-done.5, ...), custom_call_target="tpu_custom_call" | custom-call | flops 10000000 | bytes 5000000 | tf_op jit(solution)/shard_map/first_skin/pallas_call | solution.py:47
  42.6 3.3 %all-to-all-done.1 = f32[32,4,128]{2,1,0:T(4,128)S(1)} async-done(((f32[32,4,128]{2,1,0:T(4,128)}), f32[32,4,128]{2,1,0:T(4,128)S(1)}, u32[]{:S(2)}, u32[]{:S(2)}) %all-to-all-start.1) | async-done | bytes 65568 | tf_op jit(solution)/shard_map/all_to_all | solution.py:758
  45.9 0.7 copy-done.1
  46.6 1.3 %bounce.1.later_ref = f32[128,128]{1,0:T(8,128)} custom-call(f32[128,128]{1,0:T(8,128)S(1)} %copy-done, f32[128,128]{1,0:T(8,128)S(1)} %bitcast.9, f32[24,128]{1,0:T(8,128)S(1)} %copy-done.1), custom_call_target="tpu_custom_call" | custom-call | tf_op jit(solution)/shard_map/bounce/pallas_call | solution.py:47
  47.9 4.0 %all-to-all-start.2 = ((f32[32,4,128]{2,1,0:T(4,128)}), f32[32,4,128]{2,1,0:T(4,128)S(1)}, u32[]{:S(2)}, u32[]{:S(2)}) async-start(f32[32,4,128]{2,1,0:T(4,128)} %bitcast.6), calls=%async_computation.2 | async-start | bytes 131072 | tf_op jit(solution)/shard_map/all_to_all | solution.py:758
  51.9 5.3 %first_str.1 = (f32[2,3,5,96,128]{4,3,2,1,0:T(8,128)}, f32[96,128]{1,0:T(8,128)}) custom-call(f32[2,3,6,96,128]{4,3,2,1,0:T(8,128)} %str_prev_far.1, f32[2,3,6,96,128]{4,3,2,1,0:T(8,128)} %prev_far.4, f32[120,128]{1,0:T(8,128)} %copy-done.2, f32[120,128]{1,0:T(8,128)} %copy-done.3, f32[2,6,5,104,128]{4,3,2,1,0:T(8,128)} %get-tuple-element.36.tb_far, ...), custom_call_target="tpu_custom_call" | custom-call | flops 10000000 | bytes 5000000 | tf_op jit(solution)/shard_map/first_str/pallas_call | solution.py:47
  57.2 2.2 %all-to-all-done.2 = f32[32,4,128]{2,1,0:T(4,128)S(1)} async-done(((f32[32,4,128]{2,1,0:T(4,128)}), f32[32,4,128]{2,1,0:T(4,128)S(1)}, u32[]{:S(2)}, u32[]{:S(2)}) %all-to-all-start.2) | async-done | bytes 65568 | tf_op jit(solution)/shard_map/all_to_all | solution.py:758
  59.4 0.6 copy-done.6
  60.0 4.6 %load.1 = (f32[3,128,128]{2,1,0:T(8,128)}, f32[3,128,128]{2,1,0:T(8,128)}, f32[2,3,96,128]{3,2,1,0:T(8,128)}, f32[2,3,96,128]{3,2,1,0:T(8,128)}, f32[120,128]{1,...) custom-call(f32[32,128]{1,0:T(8,128)} %bitcast.13, f32[128,128]{1,0:T(8,128)} %bitcast.10, ...), custom_call_target="tpu_custom_call" | custom-call | flops 1000000000 | bytes 2000000 | tf_op jit(solution)/shard_map/load/pallas_call | solution.py:47
  64.6 2.7 %collective-permute-start.7 = (f32[128,128]{1,0:T(8,128)}, f32[128,128]{1,0:T(8,128)S(1)}, u32[]{:S(2)}, u32[]{:S(2)}) collective-permute-start(f32[128,128]{1,0:T(8,128)} %get-tuple-element.51), channel_id=1, source_target_pairs={{1,0},{2,1},{3,2},{4,3},{5,4},{6,5},{7,6},{8,7},{9,8},{10,9},{11,1... | collective-permute-start | bytes 196616 | tf_op jit(solution)/shard_map/ppermute | solution.py:339
  67.4 2.9 %collective-permute-start.4 = (f32[120,128]{1,0:T(8,128)}, f32[120,128]{1,0:T(8,128)S(1)}, u32[]{:S(2)}, u32[]{:S(2)}) collective-permute-start(f32[120,128]{1,0:T(8,128)} %get-tuple-element.49), channel_id=1, source_target_pairs={{0,32},{32,64},{64,96},{96,128},{128,160},{160,192},{192,224},{224... | collective-permute-start | bytes 184328 | tf_op jit(solution)/shard_map/ppermute | solution.py:336
  70.3 0.0 collective-permute-start.5
  70.3 2.2 %collective-permute-done.4.before_far = f32[120,128]{1,0:T(8,128)S(1)} collective-permute-done((f32[120,128]{1,0:T(8,128)}, f32[120,128]{1,0:T(8,128)S(1)}, u32[]{:S(2)}, u32[]{:S(2)}) %collective-permute-start.4) | collective-permute-done | bytes 61472 | tf_op jit(solution)/shard_map/ppermute | solution.py:336
  72.5 3.5 %collective-permute-done.5.after_far = f32[120,128]{1,0:T(8,128)S(1)} collective-permute-done((f32[120,128]{1,0:T(8,128)}, f32[120,128]{1,0:T(8,128)S(1)}, u32[]{:S(2)}, u32[]{:S(2)}) %collective-permute-start.5) | collective-permute-done | bytes 61472 | tf_op jit(solution)/shard_map/ppermute | solution.py:337
  76.0 0.6 copy-done.11
  76.6 0.0 copy-done.8
  76.6 0.0 copy-done.9
  76.6 6.8 %second.1 = (f32[3,6,128,128]{3,2,1,0:T(8,128)}, f32[2,3,6,96,128]{4,3,2,1,0:T(8,128)}) custom-call(f32[3,5,128,128]{3,2,1,0:T(8,128)} %get-tuple-element.35.skin_far, f32[3,6,128,128]{3,2,1,0:T(8,128)} %prev_far.5, f32[2,3,5,96,128]{4,3,2,1,0:T(8,128)} %get-tuple-element.39.str_far, f32[2,3,6,96,128]{4,3,2,1,0:T(8,128)} %str_prev_far.1, ...), custom_call_target="tpu_custom_call" | custom-call | flops 20000000 | bytes 10000000 | tf_op jit(solution)/shard_map/second/pallas_call | solution.py:47
  (22 shorter events, 0.0 us)
Async XLA Ops:
  5.6 14.4 %collective-permute-start.3 = (f32[128,128]{1,0:T(8,128)}, f32[128,128]{1,0:T(8,128)S(1)}, u32[]{:S(2)}, u32[]{:S(2)}) collective-permute-start(f32[128,128]{1,0:T(8,128)} %get-tuple-element.31), channel_id=1, source_target_pairs={{1,0},{2,1},{3,2},{4,3},{5,4},{6,5},{7,6},{8,7},{9,8},{10,9},{11,1... | collective-permute-start | bytes 196616 | tf_op jit(solution)/shard_map/ppermute | solution.py:339
  10.3 9.7 %collective-permute-start.2 = (f32[128,128]{1,0:T(8,128)}, f32[128,128]{1,0:T(8,128)S(1)}, u32[]{:S(2)}, u32[]{:S(2)}) collective-permute-start(f32[128,128]{1,0:T(8,128)} %get-tuple-element.31), channel_id=1, source_target_pairs={{0,1},{1,2},{2,3},{3,4},{4,5},{5,6},{6,7},{7,8},{8,9},{9,10},{10,1... | collective-permute-start | bytes 196616 | tf_op jit(solution)/shard_map/ppermute | solution.py:338
  10.3 9.6 %collective-permute-start = (f32[120,128]{1,0:T(8,128)}, f32[120,128]{1,0:T(8,128)S(1)}, u32[]{:S(2)}, u32[]{:S(2)}) collective-permute-start(f32[120,128]{1,0:T(8,128)} %get-tuple-element.29), channel_id=1, source_target_pairs={{0,32},{32,64},{64,96},{96,128},{128,160},{160,192},{192,224},{224... | collective-permute-start | bytes 184328 | tf_op jit(solution)/shard_map/ppermute | solution.py:336
  13.5 6.5 %collective-permute-start.1 = (f32[120,128]{1,0:T(8,128)}, f32[120,128]{1,0:T(8,128)S(1)}, u32[]{:S(2)}, u32[]{:S(2)}) collective-permute-start(f32[120,128]{1,0:T(8,128)} %get-tuple-element.30), channel_id=1, source_target_pairs={{32,0},{64,32},{96,64},{128,96},{160,128},{192,160},{224,192},{0,2... | collective-permute-start | bytes 184328 | tf_op jit(solution)/shard_map/ppermute | solution.py:337
  13.5 13.8 %all-to-all-start = ((f32[32,1,128]{2,1,0:T(1,128)}), f32[32,1,128]{2,1,0:T(1,128)S(1)}, u32[]{:S(2)}, u32[]{:S(2)}) async-start(f32[32,1,128]{2,1,0:T(1,128)} %bitcast.14), calls=%async_computation | async-start | bytes 32768 | tf_op jit(solution)/shard_map/all_to_all | solution.py:758
  19.9 0.6 copy-start.2
  19.9 0.6 copy-start.3
  20.0 0.7 copy-start.4
  20.6 0.6 copy-start.5
  27.3 0.6 copy-start.7
  32.8 13.1 %all-to-all-start.1 = ((f32[32,4,128]{2,1,0:T(4,128)}), f32[32,4,128]{2,1,0:T(4,128)S(1)}, u32[]{:S(2)}, u32[]{:S(2)}) async-start(f32[32,4,128]{2,1,0:T(4,128)} %bitcast.11), calls=%async_computation.1 | async-start | bytes 131072 | tf_op jit(solution)/shard_map/all_to_all | solution.py:758
  38.5 7.3 %copy-start = (f32[128,128]{1,0:T(8,128)S(1)}, f32[128,128]{1,0:T(8,128)}, u32[]{:S(2)}) copy-start(f32[128,128]{1,0:T(8,128)} %get-tuple-element.37.match_ref) | copy-start | bytes 196612
  45.9 0.7 copy-start.1
  47.9 11.5 %all-to-all-start.2 = ((f32[32,4,128]{2,1,0:T(4,128)}), f32[32,4,128]{2,1,0:T(4,128)S(1)}, u32[]{:S(2)}, u32[]{:S(2)}) async-start(f32[32,4,128]{2,1,0:T(4,128)} %bitcast.6), calls=%async_computation.2 | async-start | bytes 131072 | tf_op jit(solution)/shard_map/all_to_all | solution.py:758
  59.4 0.6 copy-start.6
  64.6 11.3 %collective-permute-start.7 = (f32[128,128]{1,0:T(8,128)}, f32[128,128]{1,0:T(8,128)S(1)}, u32[]{:S(2)}, u32[]{:S(2)}) collective-permute-start(f32[128,128]{1,0:T(8,128)} %get-tuple-element.51), channel_id=1, source_target_pairs={{1,0},{2,1},{3,2},{4,3},{5,4},{6,5},{7,6},{8,7},{9,8},{10,9},{11,1... | collective-permute-start | bytes 196616 | tf_op jit(solution)/shard_map/ppermute | solution.py:339
  67.4 8.6 %collective-permute-start.6 = (f32[128,128]{1,0:T(8,128)}, f32[128,128]{1,0:T(8,128)S(1)}, u32[]{:S(2)}, u32[]{:S(2)}) collective-permute-start(f32[128,128]{1,0:T(8,128)} %get-tuple-element.51), channel_id=1, source_target_pairs={{0,1},{1,2},{2,3},{3,4},{4,5},{5,6},{6,7},{7,8},{8,9},{9,10},{10,1... | collective-permute-start | bytes 196616 | tf_op jit(solution)/shard_map/ppermute | solution.py:338
  67.4 5.1 %collective-permute-start.4 = (f32[120,128]{1,0:T(8,128)}, f32[120,128]{1,0:T(8,128)S(1)}, u32[]{:S(2)}, u32[]{:S(2)}) collective-permute-start(f32[120,128]{1,0:T(8,128)} %get-tuple-element.49), channel_id=1, source_target_pairs={{0,32},{32,64},{64,96},{96,128},{128,160},{160,192},{192,224},{224... | collective-permute-start | bytes 184328 | tf_op jit(solution)/shard_map/ppermute | solution.py:336
  70.3 5.6 %collective-permute-start.5 = (f32[120,128]{1,0:T(8,128)}, f32[120,128]{1,0:T(8,128)S(1)}, u32[]{:S(2)}, u32[]{:S(2)}) collective-permute-start(f32[120,128]{1,0:T(8,128)} %get-tuple-element.50), channel_id=1, source_target_pairs={{32,0},{64,32},{96,64},{128,96},{160,128},{192,160},{224,192},{0,2... | collective-permute-start | bytes 184328 | tf_op jit(solution)/shard_map/ppermute | solution.py:337
  72.5 3.5 %copy-start.10 = (f32[120,128]{1,0:T(8,128)}, f32[120,128]{1,0:T(8,128)S(1)}, u32[]{:S(2)}) copy-start(f32[120,128]{1,0:T(8,128)S(1)} %collective-permute-done.4.before_far) | copy-start | bytes 184324
  75.9 0.6 copy-start.11
  76.0 0.6 copy-start.8
  76.0 0.7 copy-start.9

commit v5 on v4

--- a/solution.py
+++ b/solution.py
@@ -289,26 +289,23 @@
     lane = iota((CHUNK, 128), 1)
     side_keep = jnp.where((lane & 1) == 0, at_right, at_left)
     span_keep = jnp.where((lane & 1) == 0, at_next, at_prev)
+    for l in range(6):
+        first_ref[18 + l : 19 + l, :] = half_of(mat_ref[l, 0:1, :], tabs) * at_prev
+        last_ref[18 + l : 19 + l, :] = half_of(mat_ref[l, 127:128, :], tabs) * at_next
     for r0 in range(0, 128, CHUNK):
-        columns = jnp.zeros((CHUNK, 128), F32)
+        mats = jnp.zeros((CHUNK, 128), jnp.int32)
         for l in range(6):
-            half = half_of(mat_ref[l, pl.ds(r0, CHUNK), :], tabs)
-            columns = with_columns(columns, half, 18 + l)
-            if r0 == 0:
-                first_ref[18 + l : 19 + l, :] = half[0:1] * at_prev
-            if r0 == 128 - CHUNK:
-                last_ref[18 + l : 19 + l, :] = half[CHUNK - 1 : CHUNK] * at_next
-        columns = columns * side_keep
+            mats = with_columns(mats, mat_ref[l, pl.ds(r0, CHUNK), :], 18 + l)
+        columns = jnp.where(((lane >> 1) >= 18) & ((lane >> 1) < 24), half_of(mats, tabs) * side_keep, 0.0)
         side_ref[pl.ds(r0, CHUNK), :] = pack_skin(
             columns, lambda c, l: skin_ref[c, l, pl.ds(r0, CHUNK), :], range(6), r0, first_ref, last_ref
         )
     for r0 in range(0, 96, CHUNK):
-        columns = jnp.zeros((CHUNK, 128), F32)
+        mats = jnp.zeros((CHUNK, 128), jnp.int32)
         for p in range(2):
             for t in range(6):
-                half = half_of(smat_ref[p, t, pl.ds(r0, CHUNK), :], tabs)
-                columns = with_columns(columns, half, 36 + p * 6 + t)
-        columns = columns * span_keep
+                mats = with_columns(mats, smat_ref[p, t, pl.ds(r0, CHUNK), :], 36 + p * 6 + t)
+        columns = jnp.where(((lane >> 1) >= 36) & ((lane >> 1) < 48), half_of(mats, tabs) * span_keep, 0.0)
         columns = pack_str(columns, lambda p, c, t: str_ref[p, c, t, pl.ds(r0, CHUNK), :], range(6))
         last_ref[pl.ds(24 + r0, CHUNK), :] = columns
         first_ref[pl.ds(24 + r0, CHUNK), :] = columns
@@ -333,10 +330,10 @@
         return [(i, (i + 1) % count) for i in range(count)]
 
     back = lambda pairs: [(b, a) for a, b in pairs]
+    lefts = lax.ppermute(side, "chord", ring("chord"))
+    rights = lax.ppermute(side, "chord", back(ring("chord")))
     before = lax.ppermute(last, "span", ring("span"))
     after = lax.ppermute(first, "span", back(ring("span")))
-    lefts = lax.ppermute(side, "chord", ring("chord"))
-    rights = lax.ppermute(side, "chord", back(ring("chord")))
     return before, after, lefts, rights
 
 
@@ -446,7 +443,7 @@
         out_ref[pl.ds(j, 32, stride=4), :] = jnp.concatenate(part, axis=0)
 
 
-def bounce_body(match_ref, got_ref, later_ref, out_ref):
+def bounce_body(match_ref, got_ref, out_ref):
     got = jnp.concatenate([got_ref[pl.ds(j, 32, stride=4), :] for j in range(4)], axis=1)
     lane = iota(got.shape, 1)
     zero = (lane & 16) == 0
@@ -527,7 +524,7 @@
 
 
 def bonds_body(
-    stiff_ref, coef_ref, mat_ref, smat_ref, before_ref, after_ref, lefts_ref, rights_ref,
+    stiff_ref, coef_ref, mat_ref, smat_ref, lefts_ref, rights_ref, before_ref, after_ref,
     sb_far, tb_far, sb_ref, tb_ref, sh_ref, th_ref, edge_ref, tedge_ref, sems,
 ):
     tabs = tables(stiff_ref, coef_ref)
@@ -685,10 +682,10 @@
 
 
 def second_body(
-    skin_far, prev_far, str_far, str_prev_far, before_far, after_far, lefts_far, rights_far, sb_far, tb_far,
+    skin_far, prev_far, str_far, str_prev_far, lefts_far, rights_far, before_far, after_far, sb_far, tb_far,
     skin_face_far, str_face_far, sload_far, tload_far,
     skin2_far, str2_far,
-    skin_ref, prev_ref, str_ref, str_prev_ref, before_ref, after_ref, lefts_ref, rights_ref, sb_ref, tb_ref,
+    skin_ref, prev_ref, str_ref, str_prev_ref, lefts_ref, rights_ref, before_ref, after_ref, sb_ref, tb_ref,
     skin_face_ref, str_face_ref, sload_ref, tload_ref,
     skin2_ref, str2_ref, edge_ref, tedge_ref, sems,
 ):
@@ -776,7 +773,7 @@
     edges = [(128, 128), (96, 128)]
     bonds = [(6, 5, 136, 128), (2, 6, 5, 104, 128)]
     bonds = call(
-        bonds_body, bonds, [*mats, skin_mat, stringer_mat, *halos], "bonds", smem=(0, 1), far_outs=(0, 1),
+        bonds_body, bonds, [*mats, skin_mat, stringer_mat, *halos[2:], *halos[:2]], "bonds", smem=(0, 1), far_outs=(0, 1),
         flops=10000000, nbytes=8000000, scratch=floats(*bonds, (6, 128, 128), (6, 96, 128), *edges), sems=18,
     )
     found, *kept = call(
@@ -800,7 +797,8 @@
         far=range(8), far_outs=(0,), flops=10000000, nbytes=5000000,
         scratch=near(parts) + floats((3, 5, 128, 128), (128, 128)), sems=25,
     )
-    (turned,) = call(bounce_body, [(128, 128)], [match, given, last], "bounce", fast=(1,), far=(2,), limit=8)
+    given, last, side = lax.optimization_barrier((given, last, side))
+    (turned,) = call(bounce_body, [(128, 128)], [match, given], "bounce", fast=(1,), limit=8)
     posted = swap(turned)
     parts = [stringer_now, stringer_prev, *halos[:2], bonds[1]]
     str1, columns = call(
@@ -814,7 +812,7 @@
         views={8: ((3, 1, 128, 128), (0, 5, 0, 0)), 9: ((2, 3, 1, 96, 128), (0, 0, 0, 0, 0))},
     )
     halos1 = exchange(*packs2)
-    parts = [skin1, skin_now, str1, stringer_now, *halos1, *bonds, skin_face, str_face, sload, tload]
+    parts = [skin1, skin_now, str1, stringer_now, *halos1[2:], *halos1[:2], *bonds, skin_face, str_face, sload, tload]
     results = [(3, 6, 128, 128), (2, 3, 6, 96, 128)]
     return call(
         second_body, results, parts, "second", far=range(14), far_outs=(0, 1), flops=20000000, nbytes=10000000,

time: 84 us -> 83 us (0.988)
    unnamed x24 -> x22, local copies, waits for them, and re-layouts: 3.87 us -> 3.17 us
where the time goes in v5:
time: 83 us; the launch traced here: 82.6 us
  Pallas kernels  35.8 us (43%)
  starting transfers between devices  29.6 us (36%)
  waiting for transfers between devices  13.2 us (16%)
  local copies, waits for them, and re-layouts  3.17 us (4%)
  between operations  0.95 us (1%)
    pallas_call x8, Pallas kernels, call(): pl.pallas_call(body, grid=(1,), out_shape=[jax.ShapeDtypeStruct(s, F32) f...  35.8 us
    all_to_all x3, starting transfers between devices, swap(): lax.all_to_all(values.reshape(peers, -1, 128), 'chord', split_axis=0, con...  16 us
    all_to_all x3, waiting for transfers between devices, swap(): lax.all_to_all(values.reshape(peers, -1, 128), 'chord', split_axis=0, con...  7.5 us
    ppermute x2, starting transfers between devices, exchange(): rights = lax.ppermute(side, 'chord', back(ring('chord')))  7.46 us
    ppermute x2, starting transfers between devices, exchange(): before = lax.ppermute(last, 'span', ring('span'))  6.08 us
    ppermute x2, waiting for transfers between devices, exchange(): after = lax.ppermute(first, 'span', back(ring('span')))  3.46 us
    unnamed x22, local copies, waits for them, and re-layouts  3.17 us
    ppermute x2, waiting for transfers between devices, exchange(): before = lax.ppermute(last, 'span', ring('span'))  2.18 us
  transfers between devices with their start and end apart: 11, of which 5 were waited for; matrix products, arithmetic and copies ran while one was open for 0% of the time, Pallas kernels for 16%

profile of v5, /device:TPU:96, one launch (start us, length us, event | category | flops | bytes accessed | tf_op | source)
XLA Modules:
  0.0 82.6 jit_solution(14018579128730800892)
XLA Ops:
  0.6 4.7 %opening.1 = (f32[32,128]{1,0:T(8,128)}, f32[128,128]{1,0:T(8,128)}, f32[120,128]{1,0:T(8,128)}, f32[120,128]{1,0:T(8,128)}, f32[128,128]{1,0:T(8,128)}) custom-call(f32[8]{0:T(128)} %stiff_ref.5, f32[8]{0:T(128)} %coef_ref.5, s32[768]{0:T(1024)} %span_ref.1, s32[768]{0:T(1024)} %chord_ref.1, s32[768]{0:T(1024)} %stringer_ref.1, s32[768]{0:T(1024)} %cell_ref.1, ...), custom_call_target="tpu_custom_call" | custom-call | flops 4000000 | bytes 4000000 | tf_op jit(solution)/shard_map/opening/pallas_call | solution.py:47
  5.4 4.7 %collective-permute-start.3 = (f32[128,128]{1,0:T(8,128)}, f32[128,128]{1,0:T(8,128)S(1)}, u32[]{:S(2)}, u32[]{:S(2)}) collective-permute-start(f32[128,128]{1,0:T(8,128)} %get-tuple-element.34), channel_id=1, source_target_pairs={{1,0},{2,1},{3,2},{4,3},{5,4},{6,5},{7,6},{8,7},{9,8},{10,9},{11,1... | collective-permute-start | bytes 196616 | tf_op jit(solution)/shard_map/ppermute | solution.py:334
  10.1 3.1 %collective-permute-start = (f32[120,128]{1,0:T(8,128)}, f32[120,128]{1,0:T(8,128)S(1)}, u32[]{:S(2)}, u32[]{:S(2)}) collective-permute-start(f32[120,128]{1,0:T(8,128)} %get-tuple-element.32), channel_id=1, source_target_pairs={{0,32},{32,64},{64,96},{96,128},{128,160},{160,192},{192,224},{224... | collective-permute-start | bytes 184328 | tf_op jit(solution)/shard_map/ppermute | solution.py:335
  13.2 0.0 collective-permute-start.1
  13.2 6.5 %all-to-all-start = ((f32[32,1,128]{2,1,0:T(1,128)}), f32[32,1,128]{2,1,0:T(1,128)S(1)}, u32[]{:S(2)}, u32[]{:S(2)}) async-start(f32[32,1,128]{2,1,0:T(1,128)} %bitcast.14), calls=%async_computation | async-start | bytes 32768 | tf_op jit(solution)/shard_map/all_to_all | solution.py:755
  19.7 0.0 collective-permute-done.1.after_ref.after_far
  19.8 0.6 copy-done.1
  20.3 0.0 copy-done.2
  20.3 0.1 copy-done.3
  20.4 0.6 copy-done.4
  21.0 4.2 %bonds.1 = (f32[6,5,136,128]{3,2,1,0:T(8,128)}, f32[2,6,5,104,128]{4,3,2,1,0:T(8,128)}) custom-call(f32[8]{0:T(128)} %stiff_ref.5, f32[8]{0:T(128)} %coef_ref.5, s32[6,128,128]{2,1,0:T(8,128)} %mat_ref.3, s32[2,6,96,128]{3,2,1,0:T(8,128)} %smat_ref.3, f32[128,128]{1,0:T(8,128)} %copy-done.4, f32[128,128]{1,0:T(8,128)} %copy-done.3, f32[120,128]{1,0:T(8,128)} %copy-done.1, ...), custom_call_target="tpu_custom_call" | custom-call | flops 10000000 | bytes 8000000 | tf_op jit(solution)/shard_map/bonds/pallas_call | solution.py:47
  25.2 1.8 %all-to-all-done = f32[32,1,128]{2,1,0:T(1,128)S(1)} async-done(((f32[32,1,128]{2,1,0:T(1,128)}), f32[32,1,128]{2,1,0:T(1,128)S(1)}, u32[]{:S(2)}, u32[]{:S(2)}) %all-to-all-start) | async-done | bytes 16416 | tf_op jit(solution)/shard_map/all_to_all | solution.py:755
  27.0 0.6 copy-done.6
  27.6 4.9 %gather.1 = (f32[128,128]{1,0:T(8,128)}, f32[128,128]{1,0:T(8,128)}, f32[3,128,128]{2,1,0:T(8,128)}, f32[128,128]{1,0:T(8,128)}, f32[96,256]{1,0:T(8,128)}, /*index=5*/f32[3,96,256]{2,1,0:T(8,128)}, f32[96,256]{1,0:T(8,128)}) custom-call(f32[8]{0:T(128)} %stiff_ref.5, f32[8]{0:T(128)} %coef_ref.5, f32[32,128]{1,0:T(8,128)} %bitcast.12, ...), custom_call_target="tpu_custom_call" | custom-call | flops 1000000000 | bytes 2000000 | tf_op jit(solution)/shard_map/gather/pallas_call | solution.py:47
  32.5 5.6 %all-to-all-start.1 = ((f32[32,4,128]{2,1,0:T(4,128)}), f32[32,4,128]{2,1,0:T(4,128)S(1)}, u32[]{:S(2)}, u32[]{:S(2)}) async-start(f32[32,4,128]{2,1,0:T(4,128)} %bitcast.11), calls=%async_computation.1 | async-start | bytes 131072 | tf_op jit(solution)/shard_map/all_to_all | solution.py:755
  38.1 4.1 %first_skin.1 = (f32[3,5,128,128]{3,2,1,0:T(8,128)}, f32[24,128]{1,0:T(8,128)}, f32[24,128]{1,0:T(8,128)}, f32[128,128]{1,0:T(8,128)}) custom-call(f32[3,6,128,128]{3,2,1,0:T(8,128)} %prev_far.5, f32[3,6,128,128]{3,2,1,0:T(8,128)} %prev_far.3, f32[120,128]{1,0:T(8,128)} %copy-done.1, f32[120,128]{1,0:T(8,128)} %copy-done.2, f32[128,128]{1,0:T(8,128)} %copy-done.4, ...), custom_call_target="tpu_custom_call" | custom-call | flops 10000000 | bytes 5000000 | tf_op jit(solution)/shard_map/first_skin/pallas_call | solution.py:47
  42.2 3.5 %all-to-all-done.1 = f32[32,4,128]{2,1,0:T(4,128)S(1)} async-done(((f32[32,4,128]{2,1,0:T(4,128)}), f32[32,4,128]{2,1,0:T(4,128)S(1)}, u32[]{:S(2)}, u32[]{:S(2)}) %all-to-all-start.1) | async-done | bytes 65568 | tf_op jit(solution)/shard_map/all_to_all | solution.py:755
  45.6 1.3 %bounce.1.later_ref = f32[128,128]{1,0:T(8,128)} custom-call(f32[128,128]{1,0:T(8,128)S(1)} %copy-done, f32[128,128]{1,0:T(8,128)S(1)} %bitcast.9), custom_call_target="tpu_custom_call" | custom-call | tf_op jit(solution)/shard_map/bounce/pallas_call | solution.py:47
  46.9 4.0 %all-to-all-start.2 = ((f32[32,4,128]{2,1,0:T(4,128)}), f32[32,4,128]{2,1,0:T(4,128)S(1)}, u32[]{:S(2)}, u32[]{:S(2)}) async-start(f32[32,4,128]{2,1,0:T(4,128)} %bitcast.6), calls=%async_computation.2 | async-start | bytes 131072 | tf_op jit(solution)/shard_map/all_to_all | solution.py:755
  50.9 5.3 %first_str.1 = (f32[2,3,5,96,128]{4,3,2,1,0:T(8,128)}, f32[96,128]{1,0:T(8,128)}) custom-call(f32[2,3,6,96,128]{4,3,2,1,0:T(8,128)} %str_prev_far.1, f32[2,3,6,96,128]{4,3,2,1,0:T(8,128)} %prev_far.4, f32[120,128]{1,0:T(8,128)} %copy-done.1, f32[120,128]{1,0:T(8,128)} %copy-done.2, f32[2,6,5,104,128]{4,3,2,1,0:T(8,128)} %get-tuple-element.39.tb_far, ...), custom_call_target="tpu_custom_call" | custom-call | flops 10000000 | bytes 5000000 | tf_op jit(solution)/shard_map/first_str/pallas_call | solution.py:47
  56.2 2.2 %all-to-all-done.2 = f32[32,4,128]{2,1,0:T(4,128)S(1)} async-done(((f32[32,4,128]{2,1,0:T(4,128)}), f32[32,4,128]{2,1,0:T(4,128)S(1)}, u32[]{:S(2)}, u32[]{:S(2)}) %all-to-all-start.2) | async-done | bytes 65568 | tf_op jit(solution)/shard_map/all_to_all | solution.py:755
  58.5 0.6 copy-done.5
  59.1 4.6 %load.1 = (f32[3,128,128]{2,1,0:T(8,128)}, f32[3,128,128]{2,1,0:T(8,128)}, f32[2,3,96,128]{3,2,1,0:T(8,128)}, f32[2,3,96,128]{3,2,1,0:T(8,128)}, f32[120,128]{1,...) custom-call(f32[32,128]{1,0:T(8,128)} %bitcast.13, f32[128,128]{1,0:T(8,128)} %bitcast.10, ...), custom_call_target="tpu_custom_call" | custom-call | flops 1000000000 | bytes 2000000 | tf_op jit(solution)/shard_map/load/pallas_call | solution.py:47
  63.7 2.7 %collective-permute-start.5 = (f32[128,128]{1,0:T(8,128)}, f32[128,128]{1,0:T(8,128)S(1)}, u32[]{:S(2)}, u32[]{:S(2)}) collective-permute-start(f32[128,128]{1,0:T(8,128)} %get-tuple-element.55), channel_id=1, source_target_pairs={{1,0},{2,1},{3,2},{4,3},{5,4},{6,5},{7,6},{8,7},{9,8},{10,9},{11,1... | collective-permute-start | bytes 196616 | tf_op jit(solution)/shard_map/ppermute | solution.py:334
  66.4 2.9 %collective-permute-start.6 = (f32[120,128]{1,0:T(8,128)}, f32[120,128]{1,0:T(8,128)S(1)}, u32[]{:S(2)}, u32[]{:S(2)}) collective-permute-start(f32[120,128]{1,0:T(8,128)} %get-tuple-element.56), channel_id=1, source_target_pairs={{0,32},{32,64},{64,96},{96,128},{128,160},{160,192},{192,224},{224... | collective-permute-start | bytes 184328 | tf_op jit(solution)/shard_map/ppermute | solution.py:335
  69.3 0.0 collective-permute-start.7
  69.3 2.2 %collective-permute-done.6.before_far = f32[120,128]{1,0:T(8,128)S(1)} collective-permute-done((f32[120,128]{1,0:T(8,128)}, f32[120,128]{1,0:T(8,128)S(1)}, u32[]{:S(2)}, u32[]{:S(2)}) %collective-permute-start.6) | collective-permute-done | bytes 61472 | tf_op jit(solution)/shard_map/ppermute | solution.py:335
  71.5 3.5 %collective-permute-done.7.after_far = f32[120,128]{1,0:T(8,128)S(1)} collective-permute-done((f32[120,128]{1,0:T(8,128)}, f32[120,128]{1,0:T(8,128)S(1)}, u32[]{:S(2)}, u32[]{:S(2)}) %collective-permute-start.7) | collective-permute-done | bytes 61472 | tf_op jit(solution)/shard_map/ppermute | solution.py:336
  75.0 0.6 copy-done.10
  75.6 0.0 copy-done.7
  75.6 0.0 copy-done.8
  75.7 6.8 %second.1 = (f32[3,6,128,128]{3,2,1,0:T(8,128)}, f32[2,3,6,96,128]{4,3,2,1,0:T(8,128)}) custom-call(f32[3,5,128,128]{3,2,1,0:T(8,128)} %get-tuple-element.38.skin_far, f32[3,6,128,128]{3,2,1,0:T(8,128)} %prev_far.5, f32[2,3,5,96,128]{4,3,2,1,0:T(8,128)} %get-tuple-element.44.str_far, f32[2,3,6,96,128]{4,3,2,1,0:T(8,128)} %str_prev_far.1, ...), custom_call_target="tpu_custom_call" | custom-call | flops 20000000 | bytes 10000000 | tf_op jit(solution)/shard_map/second/pallas_call | solution.py:47
  (20 shorter events, 0.0 us)
Async XLA Ops:
  5.4 14.4 %collective-permute-start.3 = (f32[128,128]{1,0:T(8,128)}, f32[128,128]{1,0:T(8,128)S(1)}, u32[]{:S(2)}, u32[]{:S(2)}) collective-permute-start(f32[128,128]{1,0:T(8,128)} %get-tuple-element.34), channel_id=1, source_target_pairs={{1,0},{2,1},{3,2},{4,3},{5,4},{6,5},{7,6},{8,7},{9,8},{10,9},{11,1... | collective-permute-start | bytes 196616 | tf_op jit(solution)/shard_map/ppermute | solution.py:334
  10.1 9.7 %collective-permute-start.2 = (f32[128,128]{1,0:T(8,128)}, f32[128,128]{1,0:T(8,128)S(1)}, u32[]{:S(2)}, u32[]{:S(2)}) collective-permute-start(f32[128,128]{1,0:T(8,128)} %get-tuple-element.34), channel_id=1, source_target_pairs={{0,1},{1,2},{2,3},{3,4},{4,5},{5,6},{6,7},{7,8},{8,9},{9,10},{10,1... | collective-permute-start | bytes 196616 | tf_op jit(solution)/shard_map/ppermute | solution.py:333
  10.1 9.6 %collective-permute-start = (f32[120,128]{1,0:T(8,128)}, f32[120,128]{1,0:T(8,128)S(1)}, u32[]{:S(2)}, u32[]{:S(2)}) collective-permute-start(f32[120,128]{1,0:T(8,128)} %get-tuple-element.32), channel_id=1, source_target_pairs={{0,32},{32,64},{64,96},{96,128},{128,160},{160,192},{192,224},{224... | collective-permute-start | bytes 184328 | tf_op jit(solution)/shard_map/ppermute | solution.py:335
  13.2 6.5 %collective-permute-start.1 = (f32[120,128]{1,0:T(8,128)}, f32[120,128]{1,0:T(8,128)S(1)}, u32[]{:S(2)}, u32[]{:S(2)}) collective-permute-start(f32[120,128]{1,0:T(8,128)} %get-tuple-element.33), channel_id=1, source_target_pairs={{32,0},{64,32},{96,64},{128,96},{160,128},{192,160},{224,192},{0,2... | collective-permute-start | bytes 184328 | tf_op jit(solution)/shard_map/ppermute | solution.py:336
  13.2 13.8 %all-to-all-start = ((f32[32,1,128]{2,1,0:T(1,128)}), f32[32,1,128]{2,1,0:T(1,128)S(1)}, u32[]{:S(2)}, u32[]{:S(2)}) async-start(f32[32,1,128]{2,1,0:T(1,128)} %bitcast.14), calls=%async_computation | async-start | bytes 32768 | tf_op jit(solution)/shard_map/all_to_all | solution.py:755
  19.7 0.6 copy-start.1
  19.7 0.6 copy-start.2
  19.7 0.7 copy-start.3
  20.4 0.6 copy-start.4
  27.0 0.6 copy-start.6
  32.5 13.1 %all-to-all-start.1 = ((f32[32,4,128]{2,1,0:T(4,128)}), f32[32,4,128]{2,1,0:T(4,128)S(1)}, u32[]{:S(2)}, u32[]{:S(2)}) async-start(f32[32,4,128]{2,1,0:T(4,128)} %bitcast.11), calls=%async_computation.1 | async-start | bytes 131072 | tf_op jit(solution)/shard_map/all_to_all | solution.py:755
  38.1 7.5 %copy-start = (f32[128,128]{1,0:T(8,128)S(1)}, f32[128,128]{1,0:T(8,128)}, u32[]{:S(2)}) copy-start(f32[128,128]{1,0:T(8,128)} %get-tuple-element.40.match_ref) | copy-start | bytes 196612
  46.9 11.6 %all-to-all-start.2 = ((f32[32,4,128]{2,1,0:T(4,128)}), f32[32,4,128]{2,1,0:T(4,128)S(1)}, u32[]{:S(2)}, u32[]{:S(2)}) async-start(f32[32,4,128]{2,1,0:T(4,128)} %bitcast.6), calls=%async_computation.2 | async-start | bytes 131072 | tf_op jit(solution)/shard_map/all_to_all | solution.py:755
  58.5 0.6 copy-start.5
  63.7 11.3 %collective-permute-start.5 = (f32[128,128]{1,0:T(8,128)}, f32[128,128]{1,0:T(8,128)S(1)}, u32[]{:S(2)}, u32[]{:S(2)}) collective-permute-start(f32[128,128]{1,0:T(8,128)} %get-tuple-element.55), channel_id=1, source_target_pairs={{1,0},{2,1},{3,2},{4,3},{5,4},{6,5},{7,6},{8,7},{9,8},{10,9},{11,1... | collective-permute-start | bytes 196616 | tf_op jit(solution)/shard_map/ppermute | solution.py:334
  66.4 8.6 %collective-permute-start.4 = (f32[128,128]{1,0:T(8,128)}, f32[128,128]{1,0:T(8,128)S(1)}, u32[]{:S(2)}, u32[]{:S(2)}) collective-permute-start(f32[128,128]{1,0:T(8,128)} %get-tuple-element.55), channel_id=1, source_target_pairs={{0,1},{1,2},{2,3},{3,4},{4,5},{5,6},{6,7},{7,8},{8,9},{9,10},{10,1... | collective-permute-start | bytes 196616 | tf_op jit(solution)/shard_map/ppermute | solution.py:333
  66.4 5.1 %collective-permute-start.6 = (f32[120,128]{1,0:T(8,128)}, f32[120,128]{1,0:T(8,128)S(1)}, u32[]{:S(2)}, u32[]{:S(2)}) collective-permute-start(f32[120,128]{1,0:T(8,128)} %get-tuple-element.56), channel_id=1, source_target_pairs={{0,32},{32,64},{64,96},{96,128},{128,160},{160,192},{192,224},{224... | collective-permute-start | bytes 184328 | tf_op jit(solution)/shard_map/ppermute | solution.py:335
  69.3 5.6 %collective-permute-start.7 = (f32[120,128]{1,0:T(8,128)}, f32[120,128]{1,0:T(8,128)S(1)}, u32[]{:S(2)}, u32[]{:S(2)}) collective-permute-start(f32[120,128]{1,0:T(8,128)} %get-tuple-element.57), channel_id=1, source_target_pairs={{32,0},{64,32},{96,64},{128,96},{160,128},{192,160},{224,192},{0,2... | collective-permute-start | bytes 184328 | tf_op jit(solution)/shard_map/ppermute | solution.py:336
  71.5 3.5 %copy-start.9 = (f32[120,128]{1,0:T(8,128)}, f32[120,128]{1,0:T(8,128)S(1)}, u32[]{:S(2)}) copy-start(f32[120,128]{1,0:T(8,128)S(1)} %collective-permute-done.6.before_far) | copy-start | bytes 184324
  75.0 0.6 copy-start.10
  75.0 0.6 copy-start.7
  75.0 0.7 copy-start.8
